TPU v7x, 32 devices: a whole 2x2x4 slice. The times are simulated.
32 devices in a mesh: shard: 4 (over z), ctx: 4 (over x, core), tp: 2 (over y).
Axes of the slice: x: 2, y: 2, z: 4, core: 2. Of those that a mesh axis runs over, the one named last changes fastest.
Arguments:
- inputs: bfloat16 [8192, 2048], P(('shard', 'ctx')), may hold values from -6 to 6
- segments: int32 [8192], P(('shard', 'ctx')), may hold values from 0 to 11, as said below
- routes: int32 [8192, 6], P(('shard', 'ctx')), may hold values from 0 to 15, all different within a row; in each aligned block of 512 rows (0 to 511, 512 to 1023, ...) at most 288 rows name the same one
- gate_share: float32 [8192, 6], P(('shard', 'ctx')), may hold values from 0.16 to 0.64
- cotangent: bfloat16 [8192, 2048], P(('shard', 'ctx')), may hold values from -6 to 6
- attn_gain: bfloat16 [2048], P(('shard', 'ctx')), may hold values from 0.5 to 1.5
- kv_gain: bfloat16 [512], P(('shard', 'ctx')), may hold values from 0.5 to 1.5
- ffn_gain: bfloat16 [2048], P(('shard', 'ctx')), may hold values from 0.5 to 1.5
- w_query: bfloat16 [2048, 3072], P(('shard', 'ctx'), 'tp'), may hold values from -0.125 to 0.125
- w_latent: bfloat16 [2048, 576], P(('shard', 'ctx')), may hold values from -0.125 to 0.125
- w_expand: bfloat16 [512, 4096], P(('shard', 'ctx'), 'tp'), may hold values from -0.25 to 0.25
- w_output: bfloat16 [2048, 2048], P('tp', ('shard', 'ctx')), may hold values from -1.5 to 1.5
- w_shared_gate: bfloat16 [2048, 2816], P(('shard', 'ctx'), 'tp'), may hold values from -0.125 to 0.125
- w_shared_up: bfloat16 [2048, 2816], P(('shard', 'ctx'), 'tp'), may hold values from -0.125 to 0.125
- w_shared_down: bfloat16 [2816, 2048], P('tp', ('shard', 'ctx')), may hold values from -0.109375 to 0.109375
- expert_gate: bfloat16 [16, 2048, 1408], P(('shard', 'ctx'), None, 'tp'), may hold values from -0.125 to 0.125
- expert_up: bfloat16 [16, 2048, 1408], P(('shard', 'ctx'), None, 'tp'), may hold values from -0.125 to 0.125
- expert_down: bfloat16 [16, 1408, 2048], P(('shard', 'ctx'), 'tp'), may hold values from -0.625 to 0.625
Outputs:
- result: bfloat16 [8192, 2048], P(('shard', 'ctx'))
- grad_inputs: float32 [8192, 2048], P(('shard', 'ctx'))
- grad_attn_gain: float32 [2048], P(('shard', 'ctx'))
- grad_kv_gain: float32 [512], P(('shard', 'ctx'))
- grad_ffn_gain: float32 [2048], P(('shard', 'ctx'))
- grad_w_query: float32 [2048, 3072], P(('shard', 'ctx'), 'tp')
- grad_w_latent: float32 [2048, 576], P(('shard', 'ctx'))
- grad_w_expand: float32 [512, 4096], P(('shard', 'ctx'), 'tp')
- grad_w_output: float32 [2048, 2048], P('tp', ('shard', 'ctx'))
- grad_w_shared_gate: float32 [2048, 2816], P(('shard', 'ctx'), 'tp')
- grad_w_shared_up: float32 [2048, 2816], P(('shard', 'ctx'), 'tp')
- grad_w_shared_down: float32 [2816, 2048], P('tp', ('shard', 'ctx'))
- grad_expert_gate: float32 [16, 2048, 1408], P(('shard', 'ctx'), None, 'tp')
- grad_expert_up: float32 [16, 2048, 1408], P(('shard', 'ctx'), None, 'tp')
- grad_expert_down: float32 [16, 1408, 2048], P(('shard', 'ctx'), 'tp')
Inputs may be any that keep to these rules, and one draw needn't show every extreme that they name: `segments`: never falling along the tokens; tokens of different sequences (runs of 2048) have different numbers. `routes`: in each aligned block of 512 rows (the tokens of one index of shard and ctx) no expert is named by more than 288 rows, a bound that some block reaches; the 6 experts of a row differ.
All inputs are finite; a program needn't handle non-finite values.
Results may differ from a plain program's by a relative error of at most 0.019.
Values may be sent and summed in bfloat16 or wider, within the bound.
A program may use at most 448 MiB of HBM per device.

v0:
```python
import jax
import jax.numpy as jnp
from jax import lax
from jax.sharding import PartitionSpec as P

NOPE = 128
ROPE = 64
V = 128
R = 512


EPS = 1e-06


def norm_forward(values, gain):
    inverse = lax.rsqrt(jnp.mean(values * values, -1, keepdims=True) + EPS)
    return (values * inverse * gain, inverse)


def norm_backward(values, inverse, gain, upstream):
    scaled = upstream * gain
    gain_grad = jnp.sum(upstream * values * inverse, 0)
    value_grad = inverse * scaled - values * inverse**3 * jnp.mean(
        scaled * values, -1, keepdims=True
    )
    return (value_grad, gain_grad)


def rotate(values, sines, cosines):
    half_width = values.shape[-1] // 2
    first = values[..., :half_width]
    second = values[..., half_width:]
    return jnp.concatenate([first * cosines - second * sines, second * cosines + first * sines], -1)


def angles(positions):
    half_width = ROPE // 2
    freq_table = 10000.0 ** (-jnp.arange(half_width, dtype=jnp.float32) / half_width)
    turned = positions.astype(jnp.float32)[:, None] * freq_table[None, :]
    return (jnp.sin(turned), jnp.cos(turned))


def silu_slope(pre):
    sigmoid_pre = jax.nn.sigmoid(pre)
    return sigmoid_pre * (1.0 + pre * (1.0 - sigmoid_pre))


def attention_scores(query_low, key_nope, key_rope, scale):
    nope_part = jnp.einsum(
        "qhd,khd->hqk", query_low[..., :NOPE], key_nope, preferred_element_type=jnp.float32
    )
    rope_part = jnp.einsum(
        "qhd,kd->hqk", query_low[..., NOPE:], key_rope, preferred_element_type=jnp.float32
    )
    return scale * (nope_part + rope_part)


def regroup(received, groups):
    total_rows, capacity, width = received.shape
    local_count = total_rows // groups
    sectioned = received.reshape(groups, local_count, capacity, width)
    return jnp.swapaxes(sectioned, 0, 1).reshape(local_count, groups * capacity, width)


def ungroup(owned, groups):
    local_count, total_slots, width = owned.shape
    capacity = total_slots // groups
    sectioned = owned.reshape(local_count, groups, capacity, width)
    return jnp.swapaxes(sectioned, 0, 1).reshape(groups * local_count, capacity, width)


def on_device(
    inputs,
    segments,
    routes,
    gate_share,
    cotangent,
    attn_gain,
    kv_gain,
    ffn_gain,
    w_query,
    w_latent,
    w_expand,
    w_output,
    w_shared_gate,
    w_shared_up,
    w_shared_down,
    expert_gate,
    expert_up,
    expert_down,
):
    tokens_here, width = inputs.shape
    (
        attn_full,
        kv_full,
        ffn_full,
        query_full,
        latent_full,
        expand_full,
        output_full,
        sgate_full,
        sup_full,
        sdown_full,
    ) = (
        lax.all_gather(attn_gain, ("shard", "ctx"), axis=0, tiled=True),
        lax.all_gather(kv_gain, ("shard", "ctx"), axis=0, tiled=True),
        lax.all_gather(ffn_gain, ("shard", "ctx"), axis=0, tiled=True),
        lax.all_gather(w_query, ("shard", "ctx"), axis=0, tiled=True),
        lax.all_gather(w_latent, ("shard", "ctx"), axis=0, tiled=True),
        lax.all_gather(w_expand, ("shard", "ctx"), axis=0, tiled=True),
        lax.all_gather(w_output, ("shard", "ctx"), axis=1, tiled=True),
        lax.all_gather(w_shared_gate, ("shard", "ctx"), axis=0, tiled=True),
        lax.all_gather(w_shared_up, ("shard", "ctx"), axis=0, tiled=True),
        lax.all_gather(w_shared_down, ("shard", "ctx"), axis=1, tiled=True),
    )
    attn_scale = attn_full.astype(jnp.float32)
    kv_scale = kv_full.astype(jnp.float32)
    ffn_scale = ffn_full.astype(jnp.float32)
    residual = inputs.astype(jnp.float32)
    normed_one, inverse_one = norm_forward(residual, attn_scale)
    attn_low = normed_one.astype(jnp.bfloat16)
    heads_here = query_full.shape[1] // (NOPE + ROPE)
    query_raw = jnp.dot(attn_low, query_full, preferred_element_type=jnp.float32).reshape(
        tokens_here, heads_here, NOPE + ROPE
    )
    positions = lax.axis_index("ctx") * tokens_here + jnp.arange(tokens_here, dtype=jnp.int32)
    sines, cosines = angles(positions)
    query_rot = jnp.concatenate(
        [
            query_raw[..., :NOPE],
            rotate(query_raw[..., NOPE:], sines[:, None, :], cosines[:, None, :]),
        ],
        -1,
    )
    query_low = query_rot.astype(jnp.bfloat16)
    latent_raw = jnp.dot(attn_low, latent_full, preferred_element_type=jnp.float32)
    compressed = latent_raw[:, :R]
    compressed_normed, inverse_kv = norm_forward(compressed, kv_scale)
    compressed_low = compressed_normed.astype(jnp.bfloat16)
    key_rope_low = rotate(latent_raw[:, R:], sines, cosines).astype(jnp.bfloat16)
    all_latent, all_rope, all_segments = (
        lax.all_gather(compressed_low, "ctx", axis=0, tiled=True),
        lax.all_gather(key_rope_low, "ctx", axis=0, tiled=True),
        lax.all_gather(segments, "ctx", axis=0, tiled=True),
    )
    key_count = all_latent.shape[0]
    expanded = (
        jnp.dot(all_latent, expand_full, preferred_element_type=jnp.float32)
        .astype(jnp.bfloat16)
        .reshape(key_count, heads_here, NOPE + V)
    )
    key_nope = expanded[..., :NOPE]
    values_low = expanded[..., NOPE:]
    scale = (NOPE + ROPE) ** (-0.5)
    visible = (all_segments[None, :] == segments[:, None]) & (
        jnp.arange(key_count, dtype=jnp.int32)[None, :] <= positions[:, None]
    )
    scores = attention_scores(query_low, key_nope, all_rope, scale)
    masked = jnp.where(visible[None], scores, -1e30)
    row_peak = jnp.max(masked, -1, keepdims=True)
    exponent = jnp.exp(masked - row_peak)
    row_total = jnp.sum(exponent, -1, keepdims=True)
    log_total = row_peak + jnp.log(row_total)
    probs_low = (exponent / row_total).astype(jnp.bfloat16)
    attended = (
        jnp.einsum("hqk,khd->qhd", probs_low, values_low, preferred_element_type=jnp.float32)
        .astype(jnp.bfloat16)
        .reshape(tokens_here, heads_here * V)
    )
    attn_part = jnp.dot(attended, output_full, preferred_element_type=jnp.float32)
    attn_total = lax.psum(attn_part, "tp")
    middle = residual + attn_total
    normed_two, inverse_two = norm_forward(middle, ffn_scale)
    ffn_low = normed_two.astype(jnp.bfloat16)
    shared_gate = jnp.dot(ffn_low, sgate_full, preferred_element_type=jnp.float32)
    shared_up = jnp.dot(ffn_low, sup_full, preferred_element_type=jnp.float32)
    shared_hidden = (jax.nn.silu(shared_gate) * shared_up).astype(jnp.bfloat16)
    shared_part = jnp.dot(shared_hidden, sdown_full, preferred_element_type=jnp.float32)
    top_count = routes.shape[1]
    local_count = expert_gate.shape[0]
    group_size = lax.axis_size(("shard", "ctx"))
    expert_count = local_count * group_size
    capacity = 3 * tokens_here * top_count // (2 * expert_count)
    flat_routes = routes.reshape(-1)
    row_count = flat_routes.shape[0]
    onehot_rows = (
        flat_routes[:, None] == jnp.arange(expert_count, dtype=jnp.int32)[None, :]
    ).astype(jnp.int32)
    ranks = jnp.sum(jnp.cumsum(onehot_rows, 0) * onehot_rows, 1) - 1
    slot_index = flat_routes * capacity + ranks
    source_rows = (
        jnp.full((expert_count * capacity,), row_count, jnp.int32)
        .at[slot_index]
        .set(jnp.arange(row_count, dtype=jnp.int32))
    )
    token_rows = jnp.where(source_rows < row_count, source_rows // top_count, tokens_here)
    padded_in = jnp.concatenate([ffn_low, jnp.zeros((1, width), jnp.bfloat16)], 0)
    dispatch = padded_in[token_rows].reshape(expert_count, capacity, width)
    gate_all, up_all, down_all = (expert_gate, expert_up, expert_down)
    rows_in = regroup(
        lax.all_to_all(dispatch, ("shard", "ctx"), split_axis=0, concat_axis=0, tiled=True),
        group_size,
    )
    gate_pre = jnp.einsum("erd,edf->erf", rows_in, gate_all, preferred_element_type=jnp.float32)
    up_pre = jnp.einsum("erd,edf->erf", rows_in, up_all, preferred_element_type=jnp.float32)
    gate_act = jax.nn.silu(gate_pre)
    hidden_low = (gate_act * up_pre).astype(jnp.bfloat16)
    expert_out = jnp.einsum(
        "erf,efd->erd", hidden_low, down_all, preferred_element_type=jnp.float32
    ).astype(jnp.bfloat16)
    returned = lax.all_to_all(
        ungroup(expert_out, group_size), ("shard", "ctx"), split_axis=0, concat_axis=0, tiled=True
    )
    picked = returned.reshape(expert_count * capacity, width)[slot_index].reshape(
        tokens_here, top_count, width
    )
    combined = jnp.sum(gate_share[:, :, None] * picked, 1)
    moe_total = lax.psum(shared_part + combined, "tp")
    result = (middle + moe_total).astype(jnp.bfloat16)
    grad_out = cotangent.astype(jnp.float32)
    weighted = (
        (gate_share[:, :, None] * grad_out[:, None, :])
        .astype(jnp.bfloat16)
        .reshape(row_count, width)
    )
    grad_dispatch = jnp.concatenate([weighted, jnp.zeros((1, width), jnp.bfloat16)], 0)[
        source_rows
    ].reshape(expert_count, capacity, width)
    grad_rows = regroup(
        lax.all_to_all(grad_dispatch, ("shard", "ctx"), split_axis=0, concat_axis=0, tiled=True),
        group_size,
    )
    grad_hidden = jnp.einsum(
        "erd,efd->erf", grad_rows, down_all, preferred_element_type=jnp.float32
    )
    grad_gate = (grad_hidden * up_pre * silu_slope(gate_pre)).astype(jnp.bfloat16)
    grad_up = (grad_hidden * gate_act).astype(jnp.bfloat16)
    down_grad = jnp.einsum(
        "erf,erd->efd", hidden_low, grad_rows, preferred_element_type=jnp.float32
    )
    gate_grad = jnp.einsum("erd,erf->edf", rows_in, grad_gate, preferred_element_type=jnp.float32)
    up_grad = jnp.einsum("erd,erf->edf", rows_in, grad_up, preferred_element_type=jnp.float32)
    grad_in_rows = jnp.einsum(
        "erf,edf->erd", grad_gate, gate_all, preferred_element_type=jnp.float32
    )
    grad_in_rows = (
        grad_in_rows
        + jnp.einsum("erf,edf->erd", grad_up, up_all, preferred_element_type=jnp.float32)
    ).astype(jnp.bfloat16)
    back_rows = lax.all_to_all(
        ungroup(grad_in_rows, group_size), ("shard", "ctx"), split_axis=0, concat_axis=0, tiled=True
    )
    routed_grad = jnp.sum(
        back_rows.reshape(expert_count * capacity, width)[slot_index].reshape(
            tokens_here, top_count, width
        ),
        1,
        dtype=jnp.float32,
    )
    grad_shared_hidden = jnp.einsum(
        "td,fd->tf", cotangent, sdown_full, preferred_element_type=jnp.float32
    )
    grad_sgate = (grad_shared_hidden * shared_up * silu_slope(shared_gate)).astype(jnp.bfloat16)
    grad_sup = (grad_shared_hidden * jax.nn.silu(shared_gate)).astype(jnp.bfloat16)
    sdown_grad = jnp.einsum(
        "tf,td->fd", shared_hidden, cotangent, preferred_element_type=jnp.float32
    )
    sgate_grad = jnp.einsum("td,tf->df", ffn_low, grad_sgate, preferred_element_type=jnp.float32)
    sup_grad = jnp.einsum("td,tf->df", ffn_low, grad_sup, preferred_element_type=jnp.float32)
    grad_normed_two = routed_grad + jnp.einsum(
        "tf,df->td", grad_sgate, sgate_full, preferred_element_type=jnp.float32
    )
    grad_normed_two = grad_normed_two + jnp.einsum(
        "tf,df->td", grad_sup, sup_full, preferred_element_type=jnp.float32
    )
    grad_normed_two = lax.psum(grad_normed_two, "tp")
    grad_mid_norm, ffn_gain_grad = norm_backward(middle, inverse_two, ffn_scale, grad_normed_two)
    grad_middle = grad_out + grad_mid_norm
    grad_middle_low = grad_middle.astype(jnp.bfloat16)
    output_grad = jnp.einsum(
        "tc,td->cd", attended, grad_middle_low, preferred_element_type=jnp.float32
    )
    grad_attended = (
        jnp.einsum("td,cd->tc", grad_middle_low, output_full, preferred_element_type=jnp.float32)
        .astype(jnp.bfloat16)
        .reshape(tokens_here, heads_here, V)
    )
    scores_again = attention_scores(query_low, key_nope, all_rope, scale)
    probs_again = jnp.exp(jnp.where(visible[None], scores_again, -1e30) - log_total)
    probs_again_low = probs_again.astype(jnp.bfloat16)
    grad_values = jnp.einsum(
        "hqk,qhd->khd", probs_again_low, grad_attended, preferred_element_type=jnp.float32
    )
    grad_probs = jnp.einsum(
        "qhd,khd->hqk", grad_attended, values_low, preferred_element_type=jnp.float32
    )
    grad_scores = (
        probs_again * (grad_probs - jnp.sum(probs_again * grad_probs, -1, keepdims=True))
    ).astype(jnp.bfloat16)
    grad_query_nope = scale * jnp.einsum(
        "hqk,khd->qhd", grad_scores, key_nope, preferred_element_type=jnp.float32
    )
    grad_query_rope = scale * jnp.einsum(
        "hqk,kd->qhd", grad_scores, all_rope, preferred_element_type=jnp.float32
    )
    grad_key_nope = scale * jnp.einsum(
        "hqk,qhd->khd", grad_scores, query_low[..., :NOPE], preferred_element_type=jnp.float32
    )
    grad_key_rope = scale * jnp.einsum(
        "hqk,qhd->kd", grad_scores, query_low[..., NOPE:], preferred_element_type=jnp.float32
    )
    grad_query = jnp.concatenate(
        [grad_query_nope, rotate(grad_query_rope, -sines[:, None, :], cosines[:, None, :])], -1
    )
    grad_query = grad_query.astype(jnp.bfloat16).reshape(tokens_here, heads_here * (NOPE + ROPE))
    query_grad = jnp.einsum("td,tc->dc", attn_low, grad_query, preferred_element_type=jnp.float32)
    grad_norm_query = jnp.einsum(
        "tc,dc->td", grad_query, query_full, preferred_element_type=jnp.float32
    )
    grad_kv = jnp.concatenate([grad_key_nope, grad_values], -1).reshape(
        key_count, heads_here * (NOPE + V)
    )
    own_kv, own_rope = (
        lax.psum_scatter(grad_kv, "ctx", scatter_dimension=0, tiled=True),
        lax.psum_scatter(grad_key_rope, "ctx", scatter_dimension=0, tiled=True),
    )
    own_kv_low = own_kv.astype(jnp.bfloat16)
    expand_grad = jnp.einsum(
        "tr,tc->rc", compressed_low, own_kv_low, preferred_element_type=jnp.float32
    )
    grad_comp_norm = jnp.einsum(
        "tc,rc->tr", own_kv_low, expand_full, preferred_element_type=jnp.float32
    )
    grad_norm_query, grad_comp_norm, own_rope = lax.psum(
        (grad_norm_query, grad_comp_norm, own_rope), "tp"
    )
    grad_compressed, kv_gain_grad = norm_backward(compressed, inverse_kv, kv_scale, grad_comp_norm)
    grad_latent = jnp.concatenate([grad_compressed, rotate(own_rope, -sines, cosines)], -1).astype(
        jnp.bfloat16
    )
    latent_grad = jnp.einsum("td,tc->dc", attn_low, grad_latent, preferred_element_type=jnp.float32)
    grad_normed_one = grad_norm_query + jnp.einsum(
        "tc,dc->td", grad_latent, latent_full, preferred_element_type=jnp.float32
    )
    grad_in_norm, attn_gain_grad = norm_backward(residual, inverse_one, attn_scale, grad_normed_one)
    grad_inputs = grad_middle + grad_in_norm
    owned = (
        lax.psum_scatter(attn_gain_grad, ("shard", "ctx"), scatter_dimension=0, tiled=True),
        lax.psum_scatter(kv_gain_grad, ("shard", "ctx"), scatter_dimension=0, tiled=True),
        lax.psum_scatter(ffn_gain_grad, ("shard", "ctx"), scatter_dimension=0, tiled=True),
        lax.psum_scatter(query_grad, ("shard", "ctx"), scatter_dimension=0, tiled=True),
        lax.psum_scatter(latent_grad, ("shard", "ctx"), scatter_dimension=0, tiled=True),
        lax.psum_scatter(expand_grad, ("shard", "ctx"), scatter_dimension=0, tiled=True),
        lax.psum_scatter(output_grad, ("shard", "ctx"), scatter_dimension=1, tiled=True),
        lax.psum_scatter(sgate_grad, ("shard", "ctx"), scatter_dimension=0, tiled=True),
        lax.psum_scatter(sup_grad, ("shard", "ctx"), scatter_dimension=0, tiled=True),
        lax.psum_scatter(sdown_grad, ("shard", "ctx"), scatter_dimension=1, tiled=True),
    )
    return (
        result,
        grad_inputs,
        owned[0],
        owned[1],
        owned[2],
        owned[3],
        owned[4],
        owned[5],
        owned[6],
        owned[7],
        owned[8],
        owned[9],
        gate_grad,
        up_grad,
        down_grad,
    )


def solution(mesh):
    placed = (
        P(("shard", "ctx"), None),
        P(("shard", "ctx")),
        P(("shard", "ctx"), None),
        P(("shard", "ctx"), None),
        P(("shard", "ctx"), None),
        P(("shard", "ctx")),
        P(("shard", "ctx")),
        P(("shard", "ctx")),
        P(("shard", "ctx"), "tp"),
        P(("shard", "ctx"), None),
        P(("shard", "ctx"), "tp"),
        P("tp", ("shard", "ctx")),
        P(("shard", "ctx"), "tp"),
        P(("shard", "ctx"), "tp"),
        P("tp", ("shard", "ctx")),
        P(("shard", "ctx"), None, "tp"),
        P(("shard", "ctx"), None, "tp"),
        P(("shard", "ctx"), "tp", None),
    )
    return jax.shard_map(
        on_device,
        mesh=mesh,
        in_specs=placed,
        out_specs=(
            P(("shard", "ctx"), None),
            P(("shard", "ctx"), None),
            P(("shard", "ctx")),
            P(("shard", "ctx")),
            P(("shard", "ctx")),
            P(("shard", "ctx"), "tp"),
            P(("shard", "ctx"), None),
            P(("shard", "ctx"), "tp"),
            P("tp", ("shard", "ctx")),
            P(("shard", "ctx"), "tp"),
            P(("shard", "ctx"), "tp"),
            P("tp", ("shard", "ctx")),
            P(("shard", "ctx"), None, "tp"),
            P(("shard", "ctx"), None, "tp"),
            P(("shard", "ctx"), "tp", None),
        ),
        check_vma=False,
    )
```

profile of v0, /device:TPU:0, one launch (start us, length us, event | category | flops | bytes accessed | tf_op | source)
XLA Modules:
  0.0 3532.7 jit_solution(16127793434254810038)
XLA Ops:
  11.6 35.4 %all-reduce.2 = bf16[512]{0:T(512)(128)(2,1)S(1)} all-reduce(bf16[512]{0:T(512)(128)(2,1)S(1)} %dynamic-update-slice), channel_id=1, replica_groups=mesh['shard'=4,'ctx'=4,'tp'=2] {'shard','ctx'}, use_global_device_ids=true, to_apply=%add.2 | all-reduce | flops 512 | bytes 2048
  47.0 17.3 all-gather
  99.5 23.0 all-gather.14.cloned.1.call-done
  122.5 10.1 convolution_convert_fusion.1
  132.6 54.0 %all-gather.18.cloned.1.call-done = bf16[2048,1536]{1,0:T(8,128)(2,1)} async-done(((bf16[128,1536]{1,0:T(8,128)(2,1)}), bf16[2048,1536]{1,0:T(8,128)(2,1)}) %all-gather.18.cloned.1.call-update) | async-done | bytes 6291472 | tf_op jit(solution)/shard_map/all_gather | solution.py:108
  193.4 13.2 fusion.56
  206.6 24.6 fusion.95
  231.2 13.8 fusion.2
  245.0 16.3 fusion.40
  269.5 19.0 all-gather.2
  294.4 11.8 scatter_custom_fusion
  306.3 68.7 %all-reduce.12.cloned.1.call-done = f32[512,2048]{1,0:T(8,128)} async-done(((f32[512,2048]{1,0:T(8,128)}), f32[512,2048]{1,0:T(8,128)}) %all-reduce.12.cloned.1.call-update) | async-done | bytes 4194320 | tf_op jit(solution)/shard_map/psum | solution.py:171
  382.7 36.9 %gather_fusion = bf16[4608,2048]{1,0:T(8,128)(2,1)} fusion(bf16[513,2048]{1,0:T(8,128)(2,1)} %concatenate.28, s32[5120]{0:T(1024)S(1)} %get-tuple-element.65), kind=kCustom, calls=%fused_computation | custom fusion | bytes 37767168 | tf_op jit(solution)/shard_map/gather | solution.py:198
  426.0 12.3 mul.463
  438.4 29.6 mul.464
  468.0 9.6 multiply_convert_fusion.1
  483.4 41.3 %gather_fusion.2 = bf16[4608,2048]{1,0:T(8,128)(2,1)} fusion(bf16[3073,2048]{1,0:T(8,128)(2,1)} %concatenate.29, s32[5120]{0:T(1024)S(1)} %get-tuple-element.64), kind=kCustom, calls=%fused_computation.2 | custom fusion | bytes 37767168 | tf_op jit(solution)/shard_map/gather | solution.py:226
  524.7 234.3 %all-to-all-done = bf16[16,288,2048]{2,1,0:T(8,128)(2,1)} async-done(((bf16[16,288,2048]{2,1,0:T(8,128)(2,1)}), bf16[16,288,2048]{2,1,0:T(8,128)(2,1)}, u32[]{:S(2)}, u32[]{:S(2)}) %all-to-all-start) | async-done | bytes 18874400 | tf_op jit(solution)/shard_map/all_to_all | solution.py:201
  759.0 79.1 %all-to-all-start.2 = ((bf16[16,288,2048]{2,1,0:T(8,128)(2,1)}), bf16[16,288,2048]{2,1,0:T(8,128)(2,1)}, u32[]{:S(2)}, u32[]{:S(2)}) async-start(bf16[16,288,2048]{2,1,0:T(8,128)(2,1)} %bitcast.140), calls=%async_computation.2 | async-start | bytes 37748736 | tf_op jit(solution)/shard_map/all_to_all | solution.py:230
  838.1 19.8 fusion.32
  858.0 19.1 fusion.36
  877.1 294.3 %all-to-all-done.2 = bf16[16,288,2048]{2,1,0:T(8,128)(2,1)} async-done(((bf16[16,288,2048]{2,1,0:T(8,128)(2,1)}), bf16[16,288,2048]{2,1,0:T(8,128)(2,1)}, u32[]{:S(2)}, u32[]{:S(2)}) %all-to-all-start.2) | async-done | bytes 18874400 | tf_op jit(solution)/shard_map/all_to_all | solution.py:230
  1171.4 39.0 %multiply_convert_fusion.2 = (bf16[4608,704]{0,1:T(8,128)(2,1)}, bf16[4608,704]{0,1:T(8,128)(2,1)}, bf16[4608,704]{0,1:T(8,128)(2,1)}) fusion(f32[4608,704]{0,1:T(8,128)} %fusion.36, f32[4608,704]{0,1:T(8,128)} %fusion.32, bf16[4608,2048]{1,0:T(8,128)(2,1)} %bitcast.24, bf16[1,704,2048]{2,1,0:T(8,128)(2,1)S(1)} %copy-done), kind=kOutput, calls=%fused_computation.23 | convolution fusion | flops 13336215552 | bytes 67174400 | tf_op jit(solution)/shard_map/erd,efd->erf/dot_general | solution.py:233
  1210.4 22.4 fusion.34
  1232.8 28.9 add_convert_fusion
  1261.7 78.8 %all-to-all-start.3 = ((bf16[16,288,2048]{2,1,0:T(8,128)(2,1)}), bf16[16,288,2048]{2,1,0:T(8,128)(2,1)}, u32[]{:S(2)}, u32[]{:S(2)}) async-start(bf16[16,288,2048]{2,1,0:T(8,128)(2,1)} %bitcast.142), calls=%async_computation.3 | async-start | bytes 37748736 | tf_op jit(solution)/shard_map/all_to_all | solution.py:250
  1343.1 291.6 %all-gather.24.cloned.1.call-done = bf16[2048,1408]{1,0:T(8,128)(2,1)} async-done(((bf16[128,1408]{1,0:T(8,128)(2,1)}), bf16[2048,1408]{1,0:T(8,128)(2,1)}) %all-gather.24.cloned.1.call-update) | async-done | bytes 5767184 | tf_op jit(solution)/shard_map/all_gather | solution.py:113
  1642.9 99.9 %all-gather.22.cloned.1.call-done = bf16[2048,1408]{1,0:T(8,128)(2,1)} async-done(((bf16[128,1408]{1,0:T(8,128)(2,1)}), bf16[2048,1408]{1,0:T(8,128)(2,1)}) %all-gather.22.cloned.1.call-update) | async-done | bytes 5767184 | tf_op jit(solution)/shard_map/all_gather | solution.py:112
  1751.1 69.9 %all-gather.26.cloned.1.call-done = bf16[1408,2048]{1,0:T(8,128)(2,1)} async-done(((bf16[1408,128]{1,0:T(8,128)(2,1)}), bf16[1408,2048]{1,0:T(8,128)(2,1)}) %all-gather.26.cloned.1.call-update) | async-done | bytes 5767184 | tf_op jit(solution)/shard_map/all_gather | solution.py:114
  1821.0 11.1 multiply_convert_fusion.6
  1838.6 32.6 gather_fusion.3
  1871.2 22.1 reshape.407
  1893.3 17.9 reduce_sum.132
  1911.2 10.9 add_add_fusion
  1922.9 20.8 convolution_convert_fusion
  1943.7 18.4 all-to-all-start.1
  1962.1 80.7 %all-reduce.14.cloned.1.call-done = f32[512,2048]{1,0:T(8,128)} async-done(((f32[512,2048]{1,0:T(8,128)}), f32[512,2048]{1,0:T(8,128)}) %all-reduce.14.cloned.1.call-update) | async-done | bytes 4194320 | tf_op jit(solution)/shard_map/psum | solution.py:276
  2059.4 24.0 multiply_reduce_fusion
  2083.4 27.9 multiply_convert_fusion
  2111.3 12.2 multiply_bitcast_fusion
  2123.4 17.4 fusion.9
  2140.8 11.8 pad_maximum_fusion
  2152.6 142.8 %all-to-all-done.1 = bf16[16,288,2048]{2,1,0:T(8,128)(2,1)} async-done(((bf16[16,288,2048]{2,1,0:T(8,128)(2,1)}), bf16[16,288,2048]{2,1,0:T(8,128)(2,1)}, u32[]{:S(2)}, u32[]{:S(2)}) %all-to-all-start.1) | async-done | bytes 18874400 | tf_op jit(solution)/shard_map/all_to_all | solution.py:211
  2295.5 33.3 gather_fusion.1
  2328.8 22.2 reshape.406
  2351.0 18.4 multiply_reduce_fusion.1
  2381.3 11.9 fusion.48
  2393.3 11.5 fusion.45
  2421.7 77.5 %reduce-scatter.12.cloned.1.call-done = f32[512,64]{0,1:T(8,128)} async-done(((f32[2048,64]{0,1:T(8,128)}), f32[512,64]{0,1:T(8,128)}) %reduce-scatter.12.cloned.1.call-update) | async-done | bytes 131088 | tf_op jit(solution)/shard_map/reduce_scatter | solution.py:325
  2499.3 10.3 fusion.102
  2509.7 9.7 fusion.101
  2519.7 9.7 fusion.103
  2538.4 10.3 fusion.88
  2556.9 19.5 convolution_bitcast_fusion.2
  2576.4 151.1 %all-reduce.16.cloned.1.call-done = (f32[512,2048]{1,0:T(8,128)}, f32[512,2048]{1,0:T(8,128)}, f32[512,64]{0,1:T(8,128)}, f32[512,512]{0,1:T(8,128)}) async-done(((f32[512,2048]{1,0:T(8,128)}, f32[512,2048]{1,0:T(8,128)}, f32[512,64]{0,1:T(8,128)}, f32[512,512]{0,1:T(8,128)}), (f32[512,2048]{1,0:T(8,128)}, f32[512,2048]{1,0:T(8,128)}, f32[512,64]{0,1:T(8,128)}, ...) | async-done | bytes 9568272 | tf_op jit(solution)/shard_map/psum | solution.py:218
  2736.3 20.6 convolution_bitcast_fusion
  2756.8 19.7 convolution_bitcast_fusion.1
  2781.3 64.2 %all-reduce.6 = (f32[2048]{0:T(1024)S(1)}, f32[512]{0:T(512)S(1)}, f32[2048]{0:T(1024)S(1)}) all-reduce(f32[2048]{0:T(1024)S(1)} %get-tuple-element.17, f32[512]{0:T(512)S(1)} %get-tuple-element.19, f32[2048]{0:T(1024)S(1)} %copy-done.45), channel_id=4, replica_groups=mesh['shard'=4,'ctx'=4,'tp'=2] {'shard','ctx'}, use_global_device_ids=true, to_apply=%region_24.25.clone | all-reduce | flops 4608 | bytes 36864
  2859.1 131.2 %reduce-scatter.22.cloned.1.call-done = f32[128,1408]{1,0:T(8,128)} async-done(((f32[2048,1408]{1,0:T(8,128)}), f32[128,1408]{1,0:T(8,128)}) %reduce-scatter.22.cloned.1.call-update) | async-done | bytes 720912 | tf_op jit(solution)/shard_map/reduce_scatter | solution.py:355
  2990.3 130.6 %reduce-scatter.26.cloned.1.call-done = f32[1408,128]{1,0:T(8,128)} async-done(((f32[1408,2048]{1,0:T(8,128)}), f32[1408,128]{1,0:T(8,128)}) %reduce-scatter.26.cloned.1.call-update) | async-done | bytes 720912 | tf_op jit(solution)/shard_map/reduce_scatter | solution.py:357
  3121.0 109.7 %reduce-scatter.20.cloned.1.call-done = f32[1024,128]{1,0:T(8,128)} async-done(((f32[1024,2048]{1,0:T(8,128)}), f32[1024,128]{1,0:T(8,128)}) %reduce-scatter.20.cloned.1.call-update) | async-done | bytes 524304 | tf_op jit(solution)/shard_map/reduce_scatter | solution.py:354
  3230.6 139.4 %reduce-scatter.14.cloned.1.call-done = f32[128,1536]{1,0:T(8,128)} async-done(((f32[2048,1536]{1,0:T(8,128)}), f32[128,1536]{1,0:T(8,128)}) %reduce-scatter.14.cloned.1.call-update) | async-done | bytes 786448 | tf_op jit(solution)/shard_map/reduce_scatter | solution.py:351
  3370.1 76.5 %reduce-scatter.18.cloned.1.call-done = f32[32,2048]{1,0:T(8,128)} async-done(((f32[512,2048]{1,0:T(8,128)}), f32[32,2048]{1,0:T(8,128)}) %reduce-scatter.18.cloned.1.call-update) | async-done | bytes 262160 | tf_op jit(solution)/shard_map/reduce_scatter | solution.py:353
  3446.5 78.9 %reduce-scatter.16.cloned.1.call-done = f32[128,576]{0,1:T(8,128)} async-done(((f32[2048,576]{0,1:T(8,128)}), f32[128,576]{0,1:T(8,128)}) %reduce-scatter.16.cloned.1.call-update) | async-done | bytes 294928 | tf_op jit(solution)/shard_map/reduce_scatter | solution.py:352
  (265 shorter events, 194.2 us)
Async XLA Ops:
  7.2 1164.2 %copy-start = (bf16[1,704,2048]{2,1,0:T(8,128)(2,1)S(1)}, bf16[1,704,2048]{2,1,0:T(8,128)(2,1)}, u32[]{:S(2)}) copy-start(bf16[1,704,2048]{2,1,0:T(8,128)(2,1)} %param.35) | copy-start | bytes 8650756
  7.2 59.9 %all-gather.12.cloned.1.call-start = ((), (), s32[]{:S(2)}) async-start(), calls=%async_computation.13 | async-start | bytes 2506752 | tf_op jit(solution)/shard_map/all_gather | solution.py:109
  7.9 91.6 %all-gather.16.cloned.1.call-start = ((), (), s32[]{:S(2)}) async-start(), calls=%async_computation.15 | async-start | bytes 2228224 | tf_op jit(solution)/shard_map/all_gather | solution.py:110
  8.7 113.9 %all-gather.14.cloned.1.call-start = ((), (), s32[]{:S(2)}) async-start(), calls=%async_computation.14 | async-start | bytes 2621440 | tf_op jit(solution)/shard_map/all_gather | solution.py:142
  47.0 24.8 copy-start.43
  64.4 122.2 %copy-start.39 = (f32[16,1,128]{2,1,0:T(1,128)}, f32[16,1,128]{2,1,0:T(1,128)S(1)}, u32[]{:S(2)}) copy-start(f32[16,1,128]{2,1,0:T(1,128)S(1)} %convert_element_type.155) | copy-start | bytes 24580
  67.1 119.5 %copy-start.53 = (f32[512]{0:T(512)}, f32[512]{0:T(512)S(1)}, u32[]{:S(2)}) copy-start(f32[512]{0:T(512)S(1)} %get-tuple-element.52) | copy-start | bytes 6148
  73.4 113.2 %all-gather.18.cloned.1.call-start = ((), (), s32[]{:S(2)}) async-start(), calls=%async_computation.16 | async-start | bytes 6684672 | tf_op jit(solution)/shard_map/all_gather | solution.py:108
  74.0 187.4 %all-gather.20.cloned.1.call-start = ((), (), s32[]{:S(2)}) async-start(), calls=%async_computation.17 | async-start | bytes 4456448 | tf_op jit(solution)/shard_map/all_gather | solution.py:111
  74.5 300.5 %all-reduce.12.cloned.1.call-start = ((), (), s32[]{:S(2)}) async-start(), calls=%async_computation.18 | async-start | bytes 8388608 | tf_op jit(solution)/shard_map/psum | solution.py:171
  74.6 9.3 copy-start.57
  74.6 9.3 copy-start.48
  83.9 109.3 %copy-start.25 = (f32[512,32]{0,1:T(8,128)}, f32[512,32]{0,1:T(8,128)S(1)}, u32[]{:S(2)}) copy-start(f32[512,32]{0,1:T(8,128)S(1)} %get-tuple-element.50) | copy-start | bytes 196612
  91.5 101.9 %copy-start.16 = (bf16[2048,64]{0,1:T(8,128)(2,1)}, bf16[2048,64]{0,1:T(8,128)(2,1)S(1)}, u32[]{:S(2)}) copy-start(bf16[2048,64]{0,1:T(8,128)(2,1)S(1)} %all_gather.46) | copy-start | bytes 786436
  193.2 13.5 copy-start.12
  193.4 13.3 copy-start.18
  193.4 13.3 copy-start.20
  193.4 13.2 copy-start.10
  231.2 13.8 copy-start.28
  245.0 16.3 copy-start.34
  288.5 90.6 %copy-start.30 = (f32[16,1,128]{2,1,0:T(1,128)}, f32[16,1,128]{2,1,0:T(1,128)S(1)}, u32[]{:S(2)}) copy-start(f32[16,1,128]{2,1,0:T(1,128)S(1)} %convert_element_type.156) | copy-start | bytes 24580
  294.4 84.1 %copy-start.37 = (s32[3072,1]{0,1:T(1,128)}, s32[3072,1]{0,1:T(1,128)S(1)}, u32[]{:S(2)}) copy-start(s32[3072,1]{0,1:T(1,128)S(1)} %compare_select_fusion) | copy-start | bytes 36868
  419.6 339.3 %all-to-all-start = ((bf16[16,288,2048]{2,1,0:T(8,128)(2,1)}), bf16[16,288,2048]{2,1,0:T(8,128)(2,1)}, u32[]{:S(2)}, u32[]{:S(2)}) async-start(bf16[16,288,2048]{2,1,0:T(8,128)(2,1)} %bitcast.139), calls=%async_computation | async-start | bytes 37748736 | tf_op jit(solution)/shard_map/all_to_all | solution.py:201
  425.9 12.5 copy-start.22
  759.0 412.4 %all-to-all-start.2 = ((bf16[16,288,2048]{2,1,0:T(8,128)(2,1)}), bf16[16,288,2048]{2,1,0:T(8,128)(2,1)}, u32[]{:S(2)}, u32[]{:S(2)}) async-start(bf16[16,288,2048]{2,1,0:T(8,128)(2,1)} %bitcast.140), calls=%async_computation.2 | async-start | bytes 37748736 | tf_op jit(solution)/shard_map/all_to_all | solution.py:230
  838.1 19.9 copy-start.62
  1261.7 81.3 %copy-start.38 = (s32[3072,1]{0,1:T(1,128)S(1)}, s32[3072,1]{0,1:T(1,128)}, u32[]{:S(2)}) copy-start(s32[3072,1]{0,1:T(1,128)} %copy-done.37) | copy-start | bytes 36868
  1261.7 576.9 %all-to-all-start.3 = ((bf16[16,288,2048]{2,1,0:T(8,128)(2,1)}), bf16[16,288,2048]{2,1,0:T(8,128)(2,1)}, u32[]{:S(2)}, u32[]{:S(2)}) async-start(bf16[16,288,2048]{2,1,0:T(8,128)(2,1)} %bitcast.142), calls=%async_computation.3 | async-start | bytes 37748736 | tf_op jit(solution)/shard_map/all_to_all | solution.py:250
  1340.5 294.2 %all-gather.24.cloned.1.call-start = ((), (), s32[]{:S(2)}) async-start(), calls=%async_computation.20 | async-start | bytes 6127616 | tf_op jit(solution)/shard_map/all_gather | solution.py:113
  1341.3 401.6 %all-gather.22.cloned.1.call-start = ((), (), s32[]{:S(2)}) async-start(), calls=%async_computation.19 | async-start | bytes 6127616 | tf_op jit(solution)/shard_map/all_gather | solution.py:112
  1342.0 479.0 %all-gather.26.cloned.1.call-start = ((), (), s32[]{:S(2)}) async-start(), calls=%async_computation.21 | async-start | bytes 6127616 | tf_op jit(solution)/shard_map/all_gather | solution.py:114
  1342.7 700.1 %all-reduce.14.cloned.1.call-start = ((), (), s32[]{:S(2)}) async-start(), calls=%async_computation.22 | async-start | bytes 8388608 | tf_op jit(solution)/shard_map/psum | solution.py:276
  1343.1 495.6 %copy-start.32 = (s32[3072]{0:T(1024)}, s32[3072]{0:T(1024)S(1)}, u32[]{:S(2)}) copy-start(s32[3072]{0:T(1024)S(1)} %broadcast_clamp_fusion) | copy-start | bytes 36868
  1821.0 12.2 copy-start.60
  1943.7 99.1 %copy-start.31 = (f32[16,1,128]{2,1,0:T(1,128)S(1)}, f32[16,1,128]{2,1,0:T(1,128)}, u32[]{:S(2)}) copy-start(f32[16,1,128]{2,1,0:T(1,128)} %copy-done.30) | copy-start | bytes 24580
  1943.7 99.1 %copy-start.47 = (f32[512]{0:T(512)S(1)}, f32[512]{0:T(512)}, u32[]{:S(2)}) copy-start(f32[512]{0:T(512)} %copy-done.46) | copy-start | bytes 6148
  1943.7 351.8 %all-to-all-start.1 = ((bf16[16,288,2048]{2,1,0:T(8,128)(2,1)}), bf16[16,288,2048]{2,1,0:T(8,128)(2,1)}, u32[]{:S(2)}, u32[]{:S(2)}) async-start(bf16[16,288,2048]{2,1,0:T(8,128)(2,1)} %bitcast.143), calls=%async_computation.1 | async-start | bytes 37748736 | tf_op jit(solution)/shard_map/all_to_all | solution.py:211
  1962.1 86.0 %copy-start.56 = (f32[512]{0:T(512)S(1)}, f32[512]{0:T(512)}, u32[]{:S(2)}) copy-start(f32[512]{0:T(512)} %get-tuple-element.55) | copy-start | bytes 6148
  1962.1 454.5 %reduce-scatter.10.cloned.1.call-start = ((), (), s32[]{:S(2)}) async-start(), calls=%async_computation.23 | async-start | bytes 20971520 | tf_op jit(solution)/shard_map/reduce_scatter | solution.py:324
  2152.6 142.9 %copy-start.33 = (s32[3072]{0:T(1024)S(1)}, s32[3072]{0:T(1024)}, u32[]{:S(2)}) copy-start(s32[3072]{0:T(1024)} %copy-done.32) | copy-start | bytes 36868
  2152.6 346.7 %reduce-scatter.12.cloned.1.call-start = ((), (), s32[]{:S(2)}) async-start(), calls=%async_computation.24 | async-start | bytes 655360 | tf_op jit(solution)/shard_map/reduce_scatter | solution.py:325
  2328.8 22.2 copy-start.23
  2350.9 18.4 copy-start.64
  2350.9 26.5 slice-start
  2351.0 26.5 slice-start.1
  2351.0 26.5 slice-start.2
  2393.3 11.6 copy-start.26
  2393.3 11.6 copy-start.27
  2404.8 322.7 %all-reduce.16.cloned.1.call-start = ((), (), s32[]{:S(2)}) async-start(), calls=%async_computation.32 | async-start | bytes 19136512 | tf_op jit(solution)/shard_map/psum | solution.py:218
  2499.3 359.9 %reduce-scatter.24.cloned.1.call-start = ((), (), s32[]{:S(2)}) async-start(), calls=%async_computation.30 | async-start | bytes 12255232 | tf_op jit(solution)/shard_map/reduce_scatter | solution.py:356
  2509.7 480.6 %reduce-scatter.22.cloned.1.call-start = ((), (), s32[]{:S(2)}) async-start(), calls=%async_computation.29 | async-start | bytes 12255232 | tf_op jit(solution)/shard_map/reduce_scatter | solution.py:355
  2519.5 601.5 %reduce-scatter.26.cloned.1.call-start = ((), (), s32[]{:S(2)}) async-start(), calls=%async_computation.31 | async-start | bytes 12255232 | tf_op jit(solution)/shard_map/reduce_scatter | solution.py:357
  2529.5 701.2 %reduce-scatter.20.cloned.1.call-start = ((), (), s32[]{:S(2)}) async-start(), calls=%async_computation.28 | async-start | bytes 8912896 | tf_op jit(solution)/shard_map/reduce_scatter | solution.py:354
  2537.7 832.4 %reduce-scatter.14.cloned.1.call-start = ((), (), s32[]{:S(2)}) async-start(), calls=%async_computation.25 | async-start | bytes 13369344 | tf_op jit(solution)/shard_map/reduce_scatter | solution.py:351
  2548.7 897.8 %reduce-scatter.18.cloned.1.call-start = ((), (), s32[]{:S(2)}) async-start(), calls=%async_computation.27 | async-start | bytes 4456448 | tf_op jit(solution)/shard_map/reduce_scatter | solution.py:353
  2555.3 970.2 %reduce-scatter.16.cloned.1.call-start = ((), (), s32[]{:S(2)}) async-start(), calls=%async_computation.26 | async-start | bytes 5013504 | tf_op jit(solution)/shard_map/reduce_scatter | solution.py:352
  2556.9 170.6 %copy-start.42 = (f32[512]{0:T(512)S(1)}, f32[512]{0:T(512)}, u32[]{:S(2)}) copy-start(f32[512]{0:T(512)} %copy-done.41) | copy-start | bytes 6148
  2556.9 170.6 %copy-start.44 = (f32[512]{0:T(512)S(1)}, f32[512]{0:T(512)}, u32[]{:S(2)}) copy-start(f32[512]{0:T(512)} %copy-done.43) | copy-start | bytes 6148
  2556.9 172.6 %copy-start.49 = (f32[512]{0:T(512)S(1)}, f32[512]{0:T(512)}, u32[]{:S(2)}) copy-start(f32[512]{0:T(512)} %copy-done.48) | copy-start | bytes 6148
  2556.9 172.6 %copy-start.58 = (f32[32]{0:T(128)S(1)}, f32[32]{0:T(128)}, u32[]{:S(2)}) copy-start(f32[32]{0:T(128)} %copy-done.57) | copy-start | bytes 388
  2556.9 173.8 %copy-start.55 = (f32[512]{0:T(512)S(1)}, f32[512]{0:T(512)}, u32[]{:S(2)}) copy-start(f32[512]{0:T(512)} %get-tuple-element.53) | copy-start | bytes 6148
  2756.8 19.7 copy-start.6
  2756.8 19.7 copy-start.61
  2756.8 19.7 copy-start.63
  (30 other events, 114.9 us)
Sparse Core Ops, SparseCore 0:
  10.2 45.5 all-gather.11
  58.0 41.5 all-gather.15
  101.1 21.3 all-gather.13
  124.7 61.8 all-gather.17
  188.6 51.8 all-gather.19
  268.4 106.5 all-reduce.11
  1343.9 290.7 all-gather.23
  1637.2 105.5 all-gather.21
  1745.2 75.7 all-gather.25
  1922.3 120.4 all-reduce.13
  2152.7 189.1 reduce-scatter.9
  2404.9 94.2 reduce-scatter.11
  2502.5 225.0 all-reduce.15
  2732.0 127.0 reduce-scatter.23
  2864.2 126.0 reduce-scatter.21
  2994.9 126.0 reduce-scatter.25
  3126.0 104.6 reduce-scatter.19
  3235.7 134.3 reduce-scatter.13
  3375.0 71.4 reduce-scatter.17
  3450.8 74.6 reduce-scatter.15
where the time goes:
time: 3540 us; the launch traced here: 3530 us
  waiting for transfers between devices  2270 us (64%)
  matrix products  503 us (14%)
  local copies, waits for them, and re-layouts  269 us (8%)
  starting transfers between devices  184 us (5%)
  blocking collectives  149 us (4%)
  other arithmetic  142 us (4%)
    all_to_all x1, waiting for transfers between devices, on_device(): lax.all_to_all(grad_dispatch, ('shard', 'ctx'), split_axis=0, concat_axis...  294 us
    all_gather x1, waiting for transfers between devices, on_device(): lax.all_gather(w_shared_up, ('shard', 'ctx'), axis=0, tiled=True)  292 us
    all_to_all x1, waiting for transfers between devices, on_device(): lax.all_to_all(dispatch, ('shard', 'ctx'), split_axis=0, concat_axis=0, t...  234 us
    psum x1, waiting for transfers between devices, on_device(): moe_total = lax.psum(shared_part + combined, 'tp')  151 us
    all_to_all x1, waiting for transfers between devices, on_device(): lax.all_to_all(ungroup(expert_out, group_size), ('shard', 'ctx'), split_a...  143 us
    reduce_scatter x1, waiting for transfers between devices, on_device(): lax.psum_scatter(query_grad, ('shard', 'ctx'), scatter_dimension=0, tiled...  139 us
    reduce_scatter x1, waiting for transfers between devices, on_device(): lax.psum_scatter(sgate_grad, ('shard', 'ctx'), scatter_dimension=0, tiled...  131 us
    reduce_scatter x1, waiting for transfers between devices, on_device(): lax.psum_scatter(sdown_grad, ('shard', 'ctx'), scatter_dimension=1, tiled...  131 us
  transfers between devices with their start and end apart: 24, of which 20 were waited for; matrix products, arithmetic and copies ran while one was open for 19% of the time, Pallas kernels for 0%

commit v1 on v0

v1 whole, which is shorter than its diff:
```python
import functools

import jax
import jax.numpy as jnp
from jax import lax
from jax.experimental import pallas as pl
from jax.experimental.pallas import tpu as pltpu
from jax.sharding import PartitionSpec as P

NOPE = 128
ROPE = 64
V = 128
R = 512
HEAD = 256
EPS = 1e-06
GROUP = ("shard", "ctx")
MESH = pl.DeviceIdType.MESH
BF = jnp.bfloat16
F32 = jnp.float32
MIB = 1 << 20


def norm_forward(values, gain):
    inverse = lax.rsqrt(jnp.mean(values * values, -1, keepdims=True) + EPS)
    return (values * inverse * gain, inverse)


def norm_backward(values, inverse, gain, upstream):
    scaled = upstream * gain
    gain_grad = jnp.sum(upstream * values * inverse, 0)
    value_grad = inverse * scaled - values * inverse**3 * jnp.mean(
        scaled * values, -1, keepdims=True
    )
    return (value_grad, gain_grad)


def rotate(values, sines, cosines):
    half_width = values.shape[-1] // 2
    first = values[..., :half_width]
    second = values[..., half_width:]
    return jnp.concatenate([first * cosines - second * sines, second * cosines + first * sines], -1)


def angles(positions):
    half_width = ROPE // 2
    freq_table = 10000.0 ** (-jnp.arange(half_width, dtype=F32) / half_width)
    turned = positions.astype(F32)[:, None] * freq_table[None, :]
    return (jnp.sin(turned), jnp.cos(turned))


def mm(a, b):
    return jnp.dot(a, b, preferred_element_type=F32)


def mm_nt(a, b):
    return lax.dot_general(a, b, (((1,), (1,)), ((), ())), preferred_element_type=F32)


def mm_tn(a, b):
    return lax.dot_general(a, b, (((0,), (0,)), ((), ())), preferred_element_type=F32)


def ring_place(nz):
    z = lax.axis_index("shard")
    c = lax.axis_index("ctx")
    x, core = c // 2, c % 2
    return jnp.where(x == 0, z, 2 * nz - 1 - z), x, core


def ring_at(nz, p):
    p = lax.rem(p + 4 * nz, 2 * nz)
    return jnp.where(p < nz, p, 2 * nz - 1 - p), p // nz


def ring_lanes(shapes, pieces):
    lanes = []
    for index, (rows, _) in enumerate(shapes):
        first = -(-rows // 32) * 16
        ways = []
        for towards, start, size in ((1, 0, first), (-1, first, rows - first)):
            units = size // 16
            parts = min(pieces, units)
            way, at = [], start
            for part in range(parts):
                here = 16 * (units // parts + (1 if part < units % parts else 0))
                way.append((index, towards, at, here))
                at += here
            ways.append(way)
        for part in range(pieces):
            lanes += [way[part] for way in ways if part < len(way)]
    return lanes


def greet(devices):
    barrier = pltpu.get_barrier_semaphore()
    for device in devices:
        pl.semaphore_signal(barrier, inc=1, device_id=device, device_id_type=MESH)
    pl.semaphore_wait(barrier, len(devices))


def ring_neighbours(nz):
    me, x, core = ring_place(nz)
    zr, xr = ring_at(nz, me + 1)
    zl, xl = ring_at(nz, me - 1)
    right = {"shard": zr, "ctx": xr * 2 + core}
    left = {"shard": zl, "ctx": xl * 2 + core}
    sibling = {"ctx": x * 2 + 1 - core}
    return me, core, right, left, sibling


def link_cost(size, rate):
    return pl.CostEstimate(flops=int(size / rate * 9e14), bytes_accessed=2 * size, transcendentals=0)


def remote(src, dst, send, recv, device):
    return pltpu.make_async_remote_copy(
        src_ref=src, dst_ref=dst, send_sem=send, recv_sem=recv, device_id=device, device_id_type=MESH
    )


def ring_semaphores(nz, count, lanes):
    return (
        [pltpu.SemaphoreType.DMA((count,))]
        + [pltpu.SemaphoreType.DMA((len(lanes), 2 * nz - 1))] * 2
        + [pltpu.SemaphoreType.DMA((len(lanes), 2 * nz))] * 2
    )


def ring_steps(nz, lanes, ins, outs, me, core, right, left, sibling, own_sem, send, recv, sib_send, sib_recv):
    steps = 2 * nz

    def block(place, which):
        z, x = ring_at(nz, place)
        return z * 4 + x * 2 + which

    own = block(me, core)
    local = [pltpu.make_async_copy(a, b.at[own], own_sem.at[i]) for i, (a, b) in enumerate(zip(ins, outs))]
    flying = []
    last = {}
    for step in range(steps):
        for lane, (i, towards, row, rows) in enumerate(lanes):
            here = block(me - towards * step, core)
            piece = pl.ds(row, rows)
            if step > 0:
                last[lane].wait_recv()
            src = ins[i].at[piece] if step == 0 else outs[i].at[here, piece]
            dst = outs[i].at[here, piece]
            if step < steps - 1:
                copy = remote(
                    src, dst, send.at[lane, step], recv.at[lane, step], right if towards > 0 else left
                )
                copy.start()
                last[lane] = copy
                flying.append((copy, False))
            copy = remote(src, dst, sib_send.at[lane, step], sib_recv.at[lane, step], sibling)
            copy.start()
            flying.append((copy, True))
        if step == 0:
            for copy in local:
                copy.start()
        yield
    for copy in local:
        copy.wait()
    for copy, both in flying:
        copy.wait_send()
        if both:
            copy.wait_recv()


def trade_copies(nz, x_ref, o_ref, own_sem, send, recv):
    devices = 4 * nz
    me = lax.axis_index("shard") * 4 + lax.axis_index("ctx")
    local = pltpu.make_async_copy(x_ref.at[me], o_ref.at[me], own_sem)
    copies = []
    for shift in range(1, devices):
        there = lax.rem(me + shift, devices)
        device = {"shard": there // 4, "ctx": lax.rem(there, 4)}
        copies.append(remote(x_ref.at[there], o_ref.at[me], send.at[shift - 1], recv.at[shift - 1], device))
    return local, copies


def trade_partners(nz):
    devices = 4 * nz
    me = lax.axis_index("shard") * 4 + lax.axis_index("ctx")
    there = [lax.rem(me + shift, devices) for shift in range(1, devices)]
    return tuple({"shard": t // 4, "ctx": lax.rem(t, 4)} for t in there)


def trade_semaphores(nz):
    return [pltpu.SemaphoreType.DMA] + [pltpu.SemaphoreType.DMA((4 * nz - 1,))] * 2


def gather_kernel(nz, count, swaps, lanes, *refs):
    total = count + swaps
    ins, outs = refs[:total], refs[total : 2 * total]
    *ring, swap_send, swap_recv = refs[2 * total :]
    me, core, right, left, sibling = ring_neighbours(nz)
    across = {"tp": 1 - lax.axis_index("tp")}
    greet((right, left, sibling) + ((across,) if swaps else ()))
    swapped = [
        remote(ins[count + i], outs[count + i], swap_send.at[i], swap_recv.at[i], across) for i in range(swaps)
    ]
    for step, _ in enumerate(ring_steps(nz, lanes, ins[:count], outs[:count], me, core, right, left, sibling, *ring)):
        if step == 0:
            for copy in swapped:
                copy.start()
    for copy in swapped:
        copy.wait()


def ring_gather(arrays, collective_id, pieces=2, swaps=()):
    nz = lax.axis_size("shard")
    lanes = ring_lanes([a.shape for a in arrays], pieces)
    given = [*arrays, *swaps]
    count, total = len(arrays), len(given)
    return pl.pallas_call(
        functools.partial(gather_kernel, nz, count, len(swaps), lanes),
        out_shape=[jax.ShapeDtypeStruct((4 * nz,) + a.shape, a.dtype) for a in arrays]
        + [jax.ShapeDtypeStruct(a.shape, a.dtype) for a in swaps],
        in_specs=[pl.BlockSpec(memory_space=pl.ANY)] * total,
        out_specs=[pl.BlockSpec(memory_space=pl.ANY)] * total,
        scratch_shapes=ring_semaphores(nz, count, lanes)
        + [pltpu.SemaphoreType.DMA((max(len(swaps), 1),))] * 2,
        compiler_params=pltpu.CompilerParams(collective_id=collective_id, has_side_effects=True),
        cost_estimate=link_cost(4 * nz * sum(a.size * a.dtype.itemsize for a in arrays), 190e9),
        name="ring_gather",
    )(*given)


def gather_shared_kernel(
    nz, swaps, lanes, row_ref, cot_ref, gate_ref, up_ref, down_ref, *refs
):
    swap_in, refs = refs[:swaps], refs[swaps:]
    all_ref, out_ref, gin_ref, dg_ref, du_ref, dd_ref, *refs = refs
    swap_out, refs = refs[:swaps], refs[swaps:]
    xs, cs, outs, gins, own_sem, send, recv, sib_send, sib_recv, loads, stores, swap_sem = refs
    me, core, right, left, sibling = ring_neighbours(nz)
    across = {"tp": 1 - lax.axis_index("tp")}
    greet((right, left, sibling) + ((across,) if swaps else ()))
    steps = 2 * nz
    first = sum(rows for _, towards, _, rows in lanes if towards > 0)
    total = row_ref.shape[0]
    halves = ((1, 0, first), (-1, first, total - first))

    def block(place, which):
        z, x = ring_at(nz, place)
        return z * 4 + x * 2 + which

    def ring_copy(lane, step):
        _, towards, row, rows = lanes[lane]
        ref = all_ref.at[block(me - towards * step, core), pl.ds(row, rows)]
        return remote(ref, ref, send.at[lane, step], recv.at[lane, step], right if towards > 0 else left)

    def sibling_copy(lane, step, which):
        _, towards, row, rows = lanes[lane]
        ref = all_ref.at[block(me - towards * step, which), pl.ds(row, rows)]
        return remote(ref, ref, sib_send.at[lane, step], sib_recv.at[lane, step], sibling)

    def pieces_of(slot, step):
        which = core if slot == 0 else 1 - core
        return [(k, block(me - towards * step, which), pl.ds(row, rows)) for k, (towards, row, rows) in enumerate(halves)]

    def taken(slot, step):
        return [
            pltpu.make_async_copy(src.at[here, piece], dst.at[slot, piece], loads.at[slot, k, j])
            for k, here, piece in pieces_of(slot, step)
            for j, (src, dst) in enumerate(((all_ref, xs), (cot_ref, cs)))
        ]

    def given(slot, step):
        return [
            pltpu.make_async_copy(src.at[slot, piece], dst.at[here, piece], stores.at[slot, k, j])
            for k, here, piece in pieces_of(slot, step)
            for j, (src, dst) in enumerate(((outs, out_ref), (gins, gin_ref)))
        ]

    def work(slot, step, first_time):
        for copy in taken(slot, step):
            copy.wait()

        @pl.when(jnp.logical_not(first_time))
        def _():
            for copy in given(slot, jnp.maximum(step - 1, 0)):
                copy.wait()

        x, c = xs[slot], cs[slot]
        a = mm_nt(x, gate_ref[...])
        b = mm_nt(x, up_ref[...])
        sig = jax.nn.sigmoid(a)
        act = a * sig
        hidden = (act * b).astype(BF)
        grad_hidden = mm_nt(c, down_ref[...])
        grad_gate = (grad_hidden * b * (sig * (1.0 + a * (1.0 - sig)))).astype(BF)
        grad_up = (grad_hidden * act).astype(BF)
        outs[slot] = mm(hidden, down_ref[...]).astype(BF)
        gins[slot] = (mm(grad_gate, gate_ref[...]) + mm(grad_up, up_ref[...])).astype(BF)
        dg_ref[...] += mm_tn(grad_gate, x)
        du_ref[...] += mm_tn(grad_up, x)
        dd_ref[...] += mm_tn(hidden, c)
        for copy in given(slot, step):
            copy.start()

    local = pltpu.make_async_copy(row_ref, all_ref.at[block(me, core)], own_sem)
    local.start()
    swapped = [
        remote(swap_in[i], swap_out[i], swap_sem.at[0, i], swap_sem.at[1, i], across) for i in range(swaps)
    ]
    for copy in swapped:
        copy.start()
    dg_ref[...] = jnp.zeros_like(dg_ref)
    du_ref[...] = jnp.zeros_like(du_ref)
    dd_ref[...] = jnp.zeros_like(dd_ref)
    local.wait()

    def one_step(step, carry):
        for lane in range(len(lanes)):

            @pl.when(jnp.logical_and(step > 0, step < steps))
            def _(lane=lane):
                ring_copy(lane, jnp.maximum(step - 1, 0)).wait_recv()

            @pl.when(step < steps - 1)
            def _(lane=lane):
                ring_copy(lane, step).start()

            @pl.when(step < steps)
            def _(lane=lane):
                sibling_copy(lane, step, core).start()

        @pl.when(step < steps)
        def _():
            for copy in taken(0, step):
                copy.start()

        @pl.when(step > 0)
        def _():
            for lane in range(len(lanes)):
                sibling_copy(lane, step - 1, 1 - core).wait_recv()
            for copy in taken(1, step - 1):
                copy.start()

        @pl.when(step < steps)
        def _():
            work(0, step, step == 0)

        @pl.when(step > 0)
        def _():
            work(1, step - 1, step == 1)

        return carry

    lax.fori_loop(0, steps + 1, one_step, 0)
    for slot in range(2):
        for copy in given(slot, steps - 1):
            copy.wait()
    for lane in range(len(lanes)):
        for step in range(steps):
            if step < steps - 1:
                ring_copy(lane, step).wait_send()
            sibling_copy(lane, step, core).wait_send()
    for copy in swapped:
        copy.wait()


def gather_shared(rows, cot, shared, collective_id, swaps=(), pieces=2):
    nz = lax.axis_size("shard")
    lanes = ring_lanes([rows.shape], pieces)
    tokens, width = rows.shape
    hidden = shared[0].shape[0]
    blocks = jax.ShapeDtypeStruct((4 * nz, tokens, width), BF)
    anywhere, vmem = pl.BlockSpec(memory_space=pl.ANY), pl.BlockSpec(memory_space=pltpu.VMEM)
    return pl.pallas_call(
        functools.partial(gather_shared_kernel, nz, len(swaps), lanes),
        out_shape=[blocks] * 3
        + [jax.ShapeDtypeStruct((hidden, width), F32)] * 3
        + [jax.ShapeDtypeStruct(a.shape, a.dtype) for a in swaps],
        in_specs=[anywhere] * 2 + [vmem] * 3 + [anywhere] * len(swaps),
        out_specs=[anywhere] * 3 + [vmem] * 3 + [anywhere] * len(swaps),
        scratch_shapes=[pltpu.VMEM((2, tokens, width), BF)] * 4
        + [pltpu.SemaphoreType.DMA]
        + [pltpu.SemaphoreType.DMA((len(lanes), 2 * nz - 1))] * 2
        + [pltpu.SemaphoreType.DMA((len(lanes), 2 * nz))] * 2
        + [pltpu.SemaphoreType.DMA((2, 2, 2))] * 2
        + [pltpu.SemaphoreType.DMA((2, max(len(swaps), 1)))],
        compiler_params=pltpu.CompilerParams(
            collective_id=collective_id, has_side_effects=True, vmem_limit_bytes=56 * MIB
        ),
        cost_estimate=link_cost(4 * nz * rows.size * 2, 190e9),
        name="gather_shared",
    )(rows, cot, *shared, *swaps)


def ctx_neighbours():
    c = lax.axis_index("ctx")
    x, core = c // 2, c % 2
    return c, x, core, {"ctx": (1 - x) * 2 + core}, {"ctx": x * 2 + 1 - core}


def ctx_gather_kernel(nz, pieces, x_ref, t_ref, o_ref, u_ref, own_sem, send, recv, sib_send, sib_recv, *trade):
    c, x, core, across, sibling = ctx_neighbours()
    greet(trade_partners(nz))
    size = x_ref.shape[0] // pieces
    far = (1 - x) * 2 + core
    local = pltpu.make_async_copy(x_ref, o_ref.at[c], own_sem)
    first, beside = [], []
    for k in range(pieces):
        piece = pl.ds(k * size, size)
        copy = remote(x_ref.at[piece], o_ref.at[c, piece], send.at[k], recv.at[k], across)
        copy.start()
        first.append(copy)
    copy = remote(x_ref, o_ref.at[c], sib_send.at[pieces], sib_recv.at[pieces], sibling)
    copy.start()
    beside.append(copy)
    local.start()
    kept, traded = trade_copies(nz, t_ref, u_ref, *trade)
    for copy in [kept] + traded:
        copy.start()
    for k in range(pieces):
        piece = pl.ds(k * size, size)
        first[k].wait_recv()
        copy = remote(o_ref.at[far, piece], o_ref.at[far, piece], sib_send.at[k], sib_recv.at[k], sibling)
        copy.start()
        beside.append(copy)
    local.wait()
    for copy in first:
        copy.wait_send()
    for copy in beside + [kept] + traded:
        copy.wait()


def ctx_gather(array, trade, collective_id, pieces=4):
    nz = lax.axis_size("shard")
    return pl.pallas_call(
        functools.partial(ctx_gather_kernel, nz, pieces),
        out_shape=[
            jax.ShapeDtypeStruct((4,) + array.shape, array.dtype),
            jax.ShapeDtypeStruct(trade.shape, trade.dtype),
        ],
        in_specs=[pl.BlockSpec(memory_space=pl.ANY)] * 2,
        out_specs=[pl.BlockSpec(memory_space=pl.ANY)] * 2,
        scratch_shapes=[pltpu.SemaphoreType.DMA]
        + [pltpu.SemaphoreType.DMA((pieces,))] * 2
        + [pltpu.SemaphoreType.DMA((pieces + 1,))] * 2
        + trade_semaphores(nz),
        compiler_params=pltpu.CompilerParams(collective_id=collective_id, has_side_effects=True),
        cost_estimate=link_cost(array.size * array.dtype.itemsize, 30e9),
        name="ctx_gather",
    )(array, trade)


def ctx_scatter_kernel(
    nz, pieces, x_ref, t_ref, o_ref, u_ref, mine, theirs, came, own_sem, sib_send, sib_recv, send, recv, *trade
):
    c, x, core, across, sibling = ctx_neighbours()
    greet(trade_partners(nz))
    size = x_ref.shape[1] // pieces
    loads, shares, flying = {}, {}, []
    for turn in range(2):
        place = (1 - x if turn == 0 else x) * 2
        for k in range(pieces):
            piece = pl.ds(k * size, size)
            loads[turn, k] = pltpu.make_async_copy(
                x_ref.at[place + core, piece], mine.at[turn, piece], own_sem.at[turn, k]
            )
            shares[turn, k] = remote(
                x_ref.at[place + 1 - core, piece],
                theirs.at[turn, piece],
                sib_send.at[turn, k],
                sib_recv.at[turn, k],
                sibling,
            )
            loads[turn, k].start()
            shares[turn, k].start()
    kept, traded = trade_copies(nz, t_ref, u_ref, *trade)
    for copy in [kept] + traded:
        copy.start()
    for turn in range(2):
        for k in range(pieces):
            loads[turn, k].wait()
            shares[turn, k].wait_recv()
            if turn == 1:
                flying[k].wait_recv()

            @pl.loop(0, size // 16)
            def _(step, turn=turn, k=k):
                at = pl.ds(pl.multiple_of(k * size + step * 16, 16), 16)
                total = mine[turn, at, :].astype(F32) + theirs[turn, at, :].astype(F32)
                if turn == 0:
                    mine[turn, at, :] = total.astype(BF)
                else:
                    o_ref[at, :] = total + came[at, :].astype(F32)

            if turn == 0:
                piece = pl.ds(k * size, size)
                copy = remote(mine.at[0, piece], came.at[piece], send.at[k], recv.at[k], across)
                copy.start()
                flying.append(copy)
    for copy in flying:
        copy.wait_send()
    for copy in shares.values():
        copy.wait_send()
    for copy in [kept] + traded:
        copy.wait()


def ctx_scatter(array, trade, collective_id, pieces=4):
    nz = lax.axis_size("shard")
    rows, width = array.shape[1:]
    return pl.pallas_call(
        functools.partial(ctx_scatter_kernel, nz, pieces),
        out_shape=[jax.ShapeDtypeStruct((rows, width), F32), jax.ShapeDtypeStruct(trade.shape, trade.dtype)],
        in_specs=[pl.BlockSpec(memory_space=pl.ANY)] * 2,
        out_specs=[pl.BlockSpec(memory_space=pltpu.VMEM), pl.BlockSpec(memory_space=pl.ANY)],
        scratch_shapes=[
            pltpu.VMEM((2, rows, width), BF),
            pltpu.VMEM((2, rows, width), BF),
            pltpu.VMEM((rows, width), BF),
        ]
        + [pltpu.SemaphoreType.DMA((2, pieces))] * 3
        + [pltpu.SemaphoreType.DMA((pieces,))] * 2
        + trade_semaphores(nz),
        compiler_params=pltpu.CompilerParams(
            collective_id=collective_id, has_side_effects=True, vmem_limit_bytes=32 * MIB
        ),
        cost_estimate=link_cost(array.size * array.dtype.itemsize, 120e9),
        name="ctx_scatter",
    )(array, trade)


def scatter_kernel(nz, count, lanes, *refs):
    ins, outs = refs[:count], refs[count : 2 * count]
    mine, theirs, came = (refs[(2 + k) * count : (3 + k) * count] for k in range(3))
    own_sem, sib_send, sib_recv, send, recv = refs[5 * count :]
    me, core, right, left, sibling = ring_neighbours(nz)
    greet((right, left, sibling))
    steps = 2 * nz

    def block(place, which):
        z, x = ring_at(nz, place)
        return z * 4 + x * 2 + which

    loads, shares = {}, {}
    for step in range(steps):
        for lane, (i, towards, row, rows) in enumerate(lanes):
            place = me - towards * (1 + step)
            piece = pl.ds(row, rows)
            load = pltpu.make_async_copy(
                ins[i].at[block(place, core), piece], mine[i].at[step, piece], own_sem.at[lane, step]
            )
            load.start()
            loads[lane, step] = load
            share = remote(
                ins[i].at[block(place, 1 - core), piece],
                theirs[i].at[step, piece],
                sib_send.at[lane, step],
                sib_recv.at[lane, step],
                sibling,
            )
            share.start()
            shares[lane, step] = share
    flying = {}
    for step in range(steps):
        for lane, (i, towards, row, rows) in enumerate(lanes):
            loads[lane, step].wait()
            shares[lane, step].wait_recv()
            if step > 0:
                flying[lane, step - 1].wait_recv()

            @pl.loop(0, rows // 16)
            def _(turn, i=i, row=row, step=step):
                at = pl.ds(pl.multiple_of(row + turn * 16, 16), 16)
                total = mine[i][step, at, :].astype(F32) + theirs[i][step, at, :].astype(F32)
                if step > 0:
                    total = total + came[i][step - 1, at, :].astype(F32)
                if step < steps - 1:
                    mine[i][step, at, :] = total.astype(BF)
                else:
                    outs[i][at, :] = total

            if step < steps - 1:
                piece = pl.ds(row, rows)
                copy = remote(
                    mine[i].at[step, piece],
                    came[i].at[step, piece],
                    send.at[lane, step],
                    recv.at[lane, step],
                    right if towards > 0 else left,
                )
                copy.start()
                flying[lane, step] = copy
    for copy in flying.values():
        copy.wait_send()
    for copy in shares.values():
        copy.wait_send()


def ring_scatter(arrays, collective_id, pieces=2):
    nz = lax.axis_size("shard")
    shapes = [a.shape[1:] for a in arrays]
    lanes = ring_lanes(shapes, pieces)
    count, steps = len(arrays), 2 * nz
    buffers = [
        pltpu.VMEM((size,) + shape, BF) for size in (steps, steps, steps - 1) for shape in shapes
    ]
    return pl.pallas_call(
        functools.partial(scatter_kernel, nz, count, lanes),
        out_shape=[jax.ShapeDtypeStruct(shape, F32) for shape in shapes],
        in_specs=[pl.BlockSpec(memory_space=pl.ANY)] * count,
        out_specs=[pl.BlockSpec(memory_space=pltpu.VMEM)] * count,
        scratch_shapes=buffers
        + [pltpu.SemaphoreType.DMA((len(lanes), steps))] * 3
        + [pltpu.SemaphoreType.DMA((len(lanes), steps - 1))] * 2,
        compiler_params=pltpu.CompilerParams(
            collective_id=collective_id, has_side_effects=True, vmem_limit_bytes=56 * MIB
        ),
        cost_estimate=link_cost(sum(a.size * a.dtype.itemsize for a in arrays), 190e9),
        name="ring_scatter",
    )(*arrays)


def turn(values, tables):
    cosine, first, second = tables
    return values * cosine + pltpu.roll(values, 96, 1) * first + pltpu.roll(values, 32, 1) * second


def turn_tables(positions):
    sines, cosines = angles(positions)
    nothing = jnp.zeros_like(sines)
    return (
        jnp.concatenate([cosines] * 4, 1),
        jnp.concatenate([-sines, nothing] * 2, 1),
        jnp.concatenate([nothing, sines] * 2, 1),
    )


def turn_back(values, tables):
    cosines, sines = tables[0][:, : ROPE // 2], tables[2][:, ROPE // 2 : ROPE]
    return rotate(values, -sines, cosines)


def project_kernel(heads, x_ref, gain, kv_gain, w_ref, cosine, first, second, *outs):
    low_ref, q_ref, latent_ref, compressed_ref, one_ref, kv_ref = outs
    x = x_ref[...].astype(F32)
    inverse = lax.rsqrt(jnp.mean(x * x, -1, keepdims=True) + EPS)
    low = (x * inverse * gain[...]).astype(BF)
    low_ref[...] = low
    one_ref[...] = inverse
    tables = cosine[...], first[...], second[...]
    nope, rope = heads * NOPE, heads * ROPE
    q_ref[:, :nope] = mm(low, w_ref[:, :nope]).astype(BF)
    raw = mm(low, w_ref[:, nope : nope + rope])
    for k in range(rope // 128):
        q_ref[:, nope + k * 128 : nope + (k + 1) * 128] = turn(raw[:, k * 128 : (k + 1) * 128], tables).astype(BF)
    raw = mm(low, w_ref[:, nope + rope :])
    compressed = raw[:, :R]
    inverse = lax.rsqrt(jnp.mean(compressed * compressed, -1, keepdims=True) + EPS)
    compressed_ref[...] = compressed
    kv_ref[...] = inverse
    latent_ref[:, :R] = (compressed * inverse * kv_gain[...]).astype(BF)
    latent_ref[:, R:] = turn(raw[:, R:], tables).astype(BF)


def project(x, gain, kv_gain, weights, tables, heads):
    rows, width = x.shape
    tile = 128
    columns = heads * (NOPE + ROPE)
    by_row = lambda n: pl.BlockSpec((tile, n), lambda i: (i, 0))
    whole = lambda a: pl.BlockSpec(a.shape, lambda i: (0, 0))
    return pl.pallas_call(
        functools.partial(project_kernel, heads),
        out_shape=(
            jax.ShapeDtypeStruct((rows, width), BF),
            jax.ShapeDtypeStruct((rows, columns), BF),
            jax.ShapeDtypeStruct((rows, R + 128), BF),
            jax.ShapeDtypeStruct((rows, R), F32),
            jax.ShapeDtypeStruct((rows, 1), F32),
            jax.ShapeDtypeStruct((rows, 1), F32),
        ),
        grid=(rows // tile,),
        in_specs=[by_row(width), whole(gain), whole(kv_gain), whole(weights)] + [by_row(128)] * 3,
        out_specs=[by_row(width), by_row(columns), by_row(R + 128), by_row(R), by_row(1), by_row(1)],
        compiler_params=pltpu.CompilerParams(vmem_limit_bytes=48 * MIB),
        cost_estimate=pl.CostEstimate(
            flops=2 * rows * width * weights.shape[1], bytes_accessed=20 * MIB, transcendentals=0
        ),
        name="project",
    )(x, gain, kv_gain, weights, *tables)


def head_key(kv_ref, rope_ref, k):
    rope = rope_ref[...]
    if k:
        rope = pltpu.roll(rope.astype(F32), ROPE, 1).astype(BF)
    return jnp.concatenate([kv_ref[:, k * HEAD : k * HEAD + NOPE], rope], 1)


def attend_kernel(scale, start, qn_ref, qr_ref, kv_ref, rope_ref, seg_q, seg_k, o_ref, l_ref):
    rows, keys = qn_ref.shape[0], kv_ref.shape[0]
    at_q = start[0] + lax.broadcasted_iota(jnp.int32, (rows, keys), 0)
    at_k = lax.broadcasted_iota(jnp.int32, (rows, keys), 1)
    visible = (seg_q[...] == seg_k[...]) & (at_k <= at_q)
    for k in range(2):
        query = jnp.concatenate([qn_ref[:, k * NOPE : (k + 1) * NOPE], qr_ref[...]], 1)
        scores = jnp.where(visible, scale * mm_nt(query, head_key(kv_ref, rope_ref, k)), -1e30)
        peak = jnp.max(scores, -1, keepdims=True)
        weights = jnp.exp(scores - peak)
        total = jnp.sum(weights, -1, keepdims=True)
        values = kv_ref[:, k * HEAD + NOPE : (k + 1) * HEAD]
        o_ref[:, k * V : (k + 1) * V] = (mm(weights.astype(BF), values) * (1.0 / total)).astype(BF)
        l_ref[k] = peak + jnp.log(total)


def attend(query, expanded, rope, seg_q, seg_k, start, scale):
    rows, keys = query.shape[0], expanded.shape[0]
    heads = query.shape[1] // (NOPE + ROPE)
    return pl.pallas_call(
        functools.partial(attend_kernel, scale),
        out_shape=(
            jax.ShapeDtypeStruct((rows, heads * V), BF),
            jax.ShapeDtypeStruct((heads, rows, 1), F32),
        ),
        grid_spec=pltpu.PrefetchScalarGridSpec(
            num_scalar_prefetch=1,
            grid=(heads // 2,),
            in_specs=[
                pl.BlockSpec((rows, 2 * NOPE), lambda h, s: (0, h)),
                pl.BlockSpec((rows, 2 * ROPE), lambda h, s: (0, heads + h)),
                pl.BlockSpec((keys, 2 * HEAD), lambda h, s: (0, h)),
                pl.BlockSpec((keys, 128), lambda h, s: (0, R // 128)),
                pl.BlockSpec((rows, 1), lambda h, s: (0, 0)),
                pl.BlockSpec((1, keys), lambda h, s: (0, 0)),
            ],
            out_specs=[
                pl.BlockSpec((rows, 2 * V), lambda h, s: (0, h)),
                pl.BlockSpec((2, rows, 1), lambda h, s: (h, 0, 0)),
            ],
        ),
        compiler_params=pltpu.CompilerParams(vmem_limit_bytes=60 * MIB),
        cost_estimate=pl.CostEstimate(
            flops=2 * heads * rows * keys * 384, bytes_accessed=12 * MIB, transcendentals=heads * rows * keys
        ),
        name="attend",
    )(start, query, query, expanded, rope, seg_q, seg_k)


def attend_back_kernel(
    scale, start, qn_ref, qr_ref, kv_ref, rope_ref, g_ref, l_ref, seg_q, seg_k, cosine, first, second,
    dqn_ref, dqr_ref, dkv_ref, dr_ref, dr_acc,
):
    rows, keys = qn_ref.shape[0], kv_ref.shape[0]
    at_k = lax.broadcasted_iota(jnp.int32, (keys, rows), 0)
    at_q = start[0] + lax.broadcasted_iota(jnp.int32, (keys, rows), 1)
    visible = (seg_q[...] == seg_k[...]) & (at_k <= at_q)
    grad_ropes, grad_turned = [], None
    for k in range(2):
        key = head_key(kv_ref, rope_ref, k)
        query = jnp.concatenate([qn_ref[:, k * NOPE : (k + 1) * NOPE], qr_ref[...]], 1)
        grad = g_ref[:, k * V : (k + 1) * V]
        scores = scale * mm_nt(key, query)
        probs = jnp.exp(jnp.where(visible, scores, -1e30) - l_ref[k])
        grad_probs = mm_nt(kv_ref[:, k * HEAD + NOPE : (k + 1) * HEAD], grad)
        mean = jnp.sum(probs * grad_probs, 0, keepdims=True)
        grad_scores = (probs * (grad_probs - mean)).astype(BF)
        dkv_ref[:, k * HEAD + NOPE : (k + 1) * HEAD] = mm(probs.astype(BF), grad).astype(BF)
        grad_key = scale * mm(grad_scores, query)
        dkv_ref[:, k * HEAD : k * HEAD + NOPE] = grad_key[:, :NOPE].astype(BF)
        grad_ropes.append(grad_key[:, NOPE:])
        grad_query = scale * mm_tn(grad_scores, key)
        dqn_ref[:, k * NOPE : (k + 1) * NOPE] = grad_query[:, :NOPE].astype(BF)
        grad_turned = grad_query[:, NOPE:] if k == 0 else grad_turned + grad_query[:, NOPE:]
    dqr_ref[...] = turn(grad_turned, (cosine[...], -first[...], -second[...])).astype(BF)
    lane = lax.broadcasted_iota(jnp.int32, (keys, 128), 1)
    grad_rope = jnp.where(lane < ROPE, grad_ropes[0] + pltpu.roll(grad_ropes[1], ROPE, 1), 0.0)

    @pl.when(pl.program_id(0) == 0)
    def _():
        dr_acc[...] = grad_rope

    @pl.when(pl.program_id(0) > 0)
    def _():
        dr_acc[...] += grad_rope

    @pl.when(pl.program_id(0) == pl.num_programs(0) - 1)
    def _():
        dr_ref[...] = dr_acc[...].astype(BF)


def attend_back(query, expanded, rope, grad, logs, seg_q, seg_k, start, tables, scale):
    rows, keys = query.shape[0], expanded.shape[0]
    heads = query.shape[1] // (NOPE + ROPE)
    one = lambda shape: pl.BlockSpec(shape, lambda h, s: (0, 0))
    return pl.pallas_call(
        functools.partial(attend_back_kernel, scale),
        out_shape=(
            jax.ShapeDtypeStruct((rows, heads * NOPE), BF),
            jax.ShapeDtypeStruct((rows, heads * ROPE), BF),
            jax.ShapeDtypeStruct((keys, heads * (NOPE + V)), BF),
            jax.ShapeDtypeStruct((keys, 128), BF),
        ),
        grid_spec=pltpu.PrefetchScalarGridSpec(
            num_scalar_prefetch=1,
            grid=(heads // 2,),
            in_specs=[
                pl.BlockSpec((rows, 2 * NOPE), lambda h, s: (0, h)),
                pl.BlockSpec((rows, 2 * ROPE), lambda h, s: (0, heads + h)),
                pl.BlockSpec((keys, 2 * HEAD), lambda h, s: (0, h)),
                pl.BlockSpec((keys, 128), lambda h, s: (0, R // 128)),
                pl.BlockSpec((rows, 2 * V), lambda h, s: (0, h)),
                pl.BlockSpec((2, 1, rows), lambda h, s: (h, 0, 0)),
                one((1, rows)),
                one((keys, 1)),
            ]
            + [one((rows, 128))] * 3,
            out_specs=[
                pl.BlockSpec((rows, 2 * NOPE), lambda h, s: (0, h)),
                pl.BlockSpec((rows, 2 * ROPE), lambda h, s: (0, h)),
                pl.BlockSpec((keys, 2 * HEAD), lambda h, s: (0, h)),
                one((keys, 128)),
            ],
            scratch_shapes=[pltpu.VMEM((keys, 128), F32)],
        ),
        compiler_params=pltpu.CompilerParams(vmem_limit_bytes=60 * MIB),
        cost_estimate=pl.CostEstimate(
            flops=2 * heads * rows * keys * 1024, bytes_accessed=24 * MIB, transcendentals=heads * rows * keys
        ),
        name="attend_back",
    )(start, query, query, expanded, rope, grad, logs, seg_q, seg_k, *tables)


TILE = 256


def pack_kernel(pair_tile, pair_block, pair_first, pair_on, rank, share, x_ref, o_ref, w_ref, *, weighted):
    i = pl.program_id(0)
    tokens = x_ref.shape[1]

    @pl.when(pair_on[i] == 1)
    def _():
        slot = pair_tile[i] * TILE + lax.broadcasted_iota(jnp.int32, (TILE, tokens), 0)
        chosen = rank[0] == slot
        rows = mm(chosen.astype(F32).astype(BF), x_ref[0])
        weight = jnp.sum(jnp.where(chosen, share[0], 0.0), 1, keepdims=True)
        if weighted:
            rows = rows * weight
        rows = rows.astype(BF)

        @pl.when(pair_first[i] == 1)
        def _():
            o_ref[...] = rows
            w_ref[...] = weight

        @pl.when(pair_first[i] == 0)
        def _():
            o_ref[...] += rows
            w_ref[...] += weight


def pack(pairs, rank, share, x, weighted):
    blocks, tokens, width = x.shape
    slots = blocks * tokens
    return pl.pallas_call(
        functools.partial(pack_kernel, weighted=weighted),
        out_shape=(
            jax.ShapeDtypeStruct((slots, width), BF),
            jax.ShapeDtypeStruct((slots, 1), F32),
        ),
        grid_spec=pltpu.PrefetchScalarGridSpec(
            num_scalar_prefetch=4,
            grid=(pairs["tile"].shape[0],),
            in_specs=[
                pl.BlockSpec((1, 1, tokens), lambda i, t, b, f, a: (b[i], 0, 0)),
                pl.BlockSpec((1, 1, tokens), lambda i, t, b, f, a: (b[i], 0, 0)),
                pl.BlockSpec((1, tokens, width), lambda i, t, b, f, a: (b[i], 0, 0)),
            ],
            out_specs=[
                pl.BlockSpec((TILE, width), lambda i, t, b, f, a: (t[i], 0)),
                pl.BlockSpec((TILE, 1), lambda i, t, b, f, a: (t[i], 0)),
            ],
        ),
        compiler_params=pltpu.CompilerParams(vmem_limit_bytes=40 * MIB),
        cost_estimate=pl.CostEstimate(
            flops=2 * 24 * TILE * tokens * width, bytes_accessed=28 * MIB, transcendentals=0
        ),
        name="pack",
    )(pairs["tile"], pairs["block"], pairs["first_tile"], pairs["on"], rank, share, x)


def expert_kernel(parts, tiles, x_ref, g_ref, w_ref, *refs):
    gates, ups, downs = (refs[k * parts : (k + 1) * parts] for k in range(3))
    out_ref, gin_ref = refs[3 * parts : 3 * parts + 2]
    hids, ggs, gus = (refs[3 * parts + 2 + k * parts : 3 * parts + 2 + (k + 1) * parts] for k in range(3))

    @pl.when(pl.program_id(0) < tiles[0])
    def _():
        x, g = x_ref[...], g_ref[...]
        out = gin = None
        for part in range(parts):
            gate, up, down = gates[part][...], ups[part][...], downs[part][...]
            a = mm_nt(x, gate)
            b = mm_nt(x, up)
            sig = jax.nn.sigmoid(a)
            act = a * sig
            hidden = (act * b).astype(BF)
            hids[part][...] = hidden
            grad_hidden = mm_nt(g, down)
            grad_gate = (grad_hidden * b * (sig * (1.0 + a * (1.0 - sig)))).astype(BF)
            grad_up = (grad_hidden * act).astype(BF)
            ggs[part][...] = grad_gate
            gus[part][...] = grad_up
            o = mm(hidden, down)
            gi = mm(grad_gate, gate) + mm(grad_up, up)
            out = o if out is None else out + o
            gin = gi if gin is None else gin + gi
        out_ref[...] = (out * w_ref[...]).astype(BF)
        gin_ref[...] = gin.astype(BF)


def experts(tiles, x, g, w, gates, ups, downs):
    slots, width = x.shape
    parts, hidden = len(gates), gates[0].shape[0]
    row = lambda i, t: (jnp.minimum(i, t[0] - 1), 0)
    whole = lambda i, t: (0, 0)
    once = pl.Buffered(1)
    results = pl.pallas_call(
        functools.partial(expert_kernel, parts),
        out_shape=(jax.ShapeDtypeStruct((slots, width), BF),) * 2
        + (jax.ShapeDtypeStruct((slots, hidden), BF),) * (3 * parts),
        grid_spec=pltpu.PrefetchScalarGridSpec(
            num_scalar_prefetch=1,
            grid=(slots // TILE,),
            in_specs=[
                pl.BlockSpec((TILE, width), row),
                pl.BlockSpec((TILE, width), row),
                pl.BlockSpec((TILE, 1), row),
            ]
            + [pl.BlockSpec((hidden, width), whole, pipeline_mode=once)] * (3 * parts),
            out_specs=[pl.BlockSpec((TILE, width), row)] * 2
            + [pl.BlockSpec((TILE, hidden), row)] * (3 * parts),
        ),
        compiler_params=pltpu.CompilerParams(vmem_limit_bytes=60 * MIB),
        cost_estimate=pl.CostEstimate(
            flops=12 * 2560 * width * parts * hidden, bytes_accessed=100 * MIB, transcendentals=0
        ),
        name="experts",
    )(tiles, x, g, w, *gates, *ups, *downs)
    kept = [results[2 + k * parts : 2 + (k + 1) * parts] for k in range(3)]
    return results[0], results[1], kept


def expert_sums(tiles, x_ref, g_ref, hid_ref, gg_ref, gu_ref, sums):
    @pl.when(pl.program_id(0) < tiles[0])
    def _():
        x, g = x_ref[...], g_ref[...]
        sums[0][...] += mm_tn(gg_ref[...], x)
        sums[1][...] += mm_tn(gu_ref[...], x)
        sums[2][...] += mm_tn(hid_ref[...], g)


def expert_sums_kernel(tiles, x_ref, g_ref, hid_ref, gg_ref, gu_ref, *refs):
    outs, sums = refs[:3], refs[3:]

    @pl.when(pl.program_id(0) == 0)
    def _():
        for total in sums:
            total[...] = jnp.zeros_like(total)

    expert_sums(tiles, x_ref, g_ref, hid_ref, gg_ref, gu_ref, sums)

    @pl.when(pl.program_id(0) == pl.num_programs(0) - 1)
    def _():
        for out, total in zip(outs, sums):
            out[...] = total[...].astype(out.dtype)


def expert_totals_kernel(tiles, x_ref, g_ref, hid_ref, gg_ref, gu_ref, *refs):
    starts, outs = refs[:3], refs[3:]

    @pl.when(pl.program_id(0) == 0)
    def _():
        for out, start in zip(outs, starts):
            out[...] = start[...].astype(F32)

    expert_sums(tiles, x_ref, g_ref, hid_ref, gg_ref, gu_ref, outs)


def expert_grads(tiles, x, g, hid, gg, gu, starts=None):
    slots, width = x.shape
    hidden = hid.shape[1]
    row = lambda i, t: (jnp.minimum(i, t[0] - 1), 0)
    whole = lambda i, t: (0, 0)
    once = pl.Buffered(1)
    kernel = expert_sums_kernel if starts is None else expert_totals_kernel
    held = [pl.BlockSpec((hidden, width), whole, pipeline_mode=once)] * 3
    return pl.pallas_call(
        kernel,
        out_shape=(jax.ShapeDtypeStruct((hidden, width), BF if starts is None else F32),) * 3,
        grid_spec=pltpu.PrefetchScalarGridSpec(
            num_scalar_prefetch=1,
            grid=(slots // TILE,),
            in_specs=[pl.BlockSpec((TILE, width), row)] * 2
            + [pl.BlockSpec((TILE, hidden), row)] * 3
            + (held if starts is not None else []),
            out_specs=held,
            scratch_shapes=[pltpu.VMEM((hidden, width), F32)] * 3 if starts is None else [],
        ),
        compiler_params=pltpu.CompilerParams(vmem_limit_bytes=60 * MIB),
        cost_estimate=pl.CostEstimate(
            flops=6 * 2560 * width * hidden, bytes_accessed=40 * MIB, transcendentals=0
        ),
        name="expert_grads",
    )(tiles, x, g, hid, gg, gu, *(starts or ()))


def dense_kernel(
    pair_tile, pair_block, pair_first, pair_last, pair_real, rank, x_ref, c_ref, out_ref, gin_ref, total_ref, grad_ref, acc, gacc
):
    i = pl.program_id(0)

    @pl.when(pair_first[i] == 1)
    def _():
        acc[...] = x_ref[0].astype(F32)
        gacc[...] = c_ref[0].astype(F32)

    @pl.when(pair_real[i] == 1)
    def _():
        tokens = rank.shape[1]
        slot = pair_tile[i] * TILE + lax.broadcasted_iota(jnp.int32, (tokens, TILE), 1)
        chosen = (rank[0] == slot).astype(F32).astype(BF)
        acc[...] += mm(chosen, out_ref[...])
        gacc[...] += mm(chosen, gin_ref[...])

    @pl.when(pair_last[i] == 1)
    def _():
        total_ref[0] = acc[...].astype(BF)
        grad_ref[0] = gacc[...].astype(BF)


def dense(pairs, rank_column, shared_out, shared_gin, out, gin):
    blocks, tokens, width = shared_out.shape
    by_block = lambda i, t, b, f, l, r: (b[i], 0, 0)
    by_tile = lambda i, t, b, f, l, r: (t[i], 0)
    return pl.pallas_call(
        dense_kernel,
        out_shape=(jax.ShapeDtypeStruct((blocks, tokens, width), BF),) * 2,
        grid_spec=pltpu.PrefetchScalarGridSpec(
            num_scalar_prefetch=5,
            grid=(pairs["tile"].shape[0],),
            in_specs=[
                pl.BlockSpec((1, tokens, 1), by_block),
                pl.BlockSpec((1, tokens, width), by_block),
                pl.BlockSpec((1, tokens, width), by_block),
                pl.BlockSpec((TILE, width), by_tile),
                pl.BlockSpec((TILE, width), by_tile),
            ],
            out_specs=[pl.BlockSpec((1, tokens, width), by_block)] * 2,
            scratch_shapes=[pltpu.VMEM((tokens, width), F32)] * 2,
        ),
        compiler_params=pltpu.CompilerParams(vmem_limit_bytes=60 * MIB),
        cost_estimate=pl.CostEstimate(
            flops=4 * 26 * TILE * tokens * width, bytes_accessed=90 * MIB, transcendentals=0
        ),
        name="dense",
    )(
        pairs["tile"], pairs["block"], pairs["first_block"], pairs["last_block"], pairs["real"],
        rank_column, shared_out, shared_gin, out, gin,
    )


def routing(share):
    blocks, tokens = share.shape
    used = (share > 0).astype(F32)
    upper = (jnp.arange(tokens)[:, None] <= jnp.arange(tokens)[None, :]).astype(BF)
    inside = mm(used.astype(BF), upper).astype(jnp.int32)
    counts = inside[:, -1]
    lower = jnp.arange(blocks)[:, None] > jnp.arange(blocks)[None, :]
    start = jnp.sum(jnp.where(lower, counts[None, :], 0), 1)
    end = start + counts
    rank = jnp.where(share > 0, start[:, None] + inside - 1, -1)
    last_tile = blocks * tokens // TILE - 1
    first = jnp.minimum(start // TILE, last_tile)
    last = jnp.where(counts > 0, (end - 1) // TILE, first)
    spans = last - first + 1
    after = jnp.sum(jnp.where(lower | jnp.eye(blocks, dtype=bool), spans[None, :], 0), 1)
    size = 2 * blocks
    turn = jnp.arange(size)
    all_pairs = after[-1]
    on = turn < all_pairs
    place = jnp.minimum(turn, all_pairs - 1)
    block = jnp.sum((after[None, :] <= place[:, None]).astype(jnp.int32), 1)
    pick = block[:, None] == jnp.arange(blocks)[None, :]
    take = lambda v: jnp.sum(jnp.where(pick, v[None, :], 0), 1)
    tile = take(first) + place - take(after - spans)
    shifted = lambda v: jnp.concatenate([jnp.full((1,), -1, v.dtype), v[:-1]])
    as_int = lambda v: v.astype(jnp.int32)
    pairs = {
        "tile": as_int(tile),
        "block": as_int(block),
        "on": as_int(on),
        "real": as_int(on & (take(counts) > 0)),
        "first_tile": as_int(on & (shifted(tile) != tile)),
        "first_block": as_int(on & (shifted(block) != block)),
        "last_block": as_int(on & (place == take(after) - 1)),
    }
    tiles = as_int(jnp.maximum((end[-1] + TILE - 1) // TILE, 1))[None]
    return rank.astype(jnp.int32), pairs, tiles


def other_half_sum(rows, product):
    parts, me = lax.axis_size("tp"), lax.axis_index("tp")
    size = rows.shape[0] // parts
    if parts != 2:
        return lax.psum_scatter(product(rows).astype(BF), "tp", scatter_dimension=0, tiled=True).astype(F32)
    sent = product(lax.dynamic_slice_in_dim(rows, (1 - me) * size, size)).astype(BF)
    came = lax.ppermute(sent, "tp", [(0, 1), (1, 0)])
    return product(lax.dynamic_slice_in_dim(rows, me * size, size)) + came.astype(F32)


def swap_tp(v):
    return lax.ppermute(v, "tp", [(0, 1), (1, 0)])


def join_tp(v):
    if lax.axis_size("tp") != 2:
        return lax.all_gather(v, "tp", axis=0, tiled=True)
    came = swap_tp(v)
    return jnp.where(lax.axis_index("tp") == 0, jnp.stack([v, came]), jnp.stack([came, v])).reshape(
        (2 * v.shape[0],) + v.shape[1:]
    )


def on_device(
    inputs,
    segments,
    routes,
    gate_share,
    cotangent,
    attn_gain,
    kv_gain,
    ffn_gain,
    w_query,
    w_latent,
    w_expand,
    w_output,
    w_shared_gate,
    w_shared_up,
    w_shared_down,
    expert_gate,
    expert_up,
    expert_down,
):
    tokens, width = inputs.shape
    parts, part = lax.axis_size("tp"), lax.axis_index("tp")
    half = tokens // parts
    group = lax.axis_size(GROUP)
    me = lax.axis_index(GROUP)
    ctx = lax.axis_size("ctx")
    query_width = w_query.shape[1]
    heads = query_width // (NOPE + ROPE)
    scale = (NOPE + ROPE) ** (-0.5)
    own_half = lambda v: lax.dynamic_slice_in_dim(v, part * half, half)

    gain_row = jnp.concatenate([attn_gain, kv_gain, ffn_gain])
    n_attn, n_kv = attn_gain.shape[0], kv_gain.shape[0]
    gain_rows = jnp.zeros((16, 384), BF).at[0, : gain_row.shape[0]].set(gain_row)
    by_head = w_query.reshape(-1, heads, NOPE + ROPE)
    first_weights = jnp.concatenate(
        [
            by_head[..., :NOPE].reshape(-1, heads * NOPE),
            by_head[..., NOPE:].reshape(-1, heads * ROPE),
            w_latent,
            jnp.zeros((w_latent.shape[0], 128 - ROPE), BF),
        ],
        1,
    )
    expert_ids = jnp.arange(group, dtype=jnp.int32)
    shares = jnp.sum(
        jnp.where(own_half(routes).T[None] == expert_ids[:, None, None], own_half(gate_share).T[None], 0.0), 1
    )
    gate, up, down = (jnp.swapaxes(expert_gate[0], 0, 1), jnp.swapaxes(expert_up[0], 0, 1), expert_down[0])
    together = lax.optimization_barrier
    piece = w_shared_gate.shape[1] // group
    depth = w_shared_gate.shape[0]
    cut = lambda v: v.reshape(group, piece, depth)
    shared_sent = jnp.concatenate(
        [cut(jnp.swapaxes(w_shared_gate, 0, 1)), cut(jnp.swapaxes(w_shared_up, 0, 1)), cut(w_shared_down)], 1
    )
    first = ring_gather(
        [
            first_weights,
            jnp.swapaxes(w_output, 0, 1),
            w_expand,
            gain_rows,
            shares,
            jnp.broadcast_to(segments[None], (16, tokens)),
        ],
        1,
        swaps=[gate] if parts == 2 else [],
    )
    first_full, output_full, expand_full, gains, share, all_segments = first[:6]
    expand_full = expand_full.reshape(R, -1)
    output_full = output_full.reshape(width, -1)
    attn_scale = gains[:, 0, :n_attn].reshape(-1).astype(F32)
    kv_scale = gains[:, 0, n_attn : n_attn + n_kv].reshape(-1).astype(F32)
    ffn_scale = gains[:, 0, n_attn + n_kv : gain_row.shape[0]].reshape(-1).astype(F32)
    first_full = first_full.reshape(width, -1)
    all_segments = lax.dynamic_slice_in_dim(
        all_segments[:, 0], lax.axis_index("shard") * ctx, ctx
    ).reshape(-1)
    share = lax.dynamic_index_in_dim(share, me, 1, keepdims=False)
    rank, pairs, tiles = routing(share)

    cot_all = lax.all_gather(together((own_half(cotangent), gains))[0], GROUP, axis=0, tiled=False)
    if parts == 2:
        up_other = swap_tp(together((up, gains))[0])

    residual = inputs.astype(F32)
    start = lax.axis_index("ctx") * tokens
    tables = turn_tables(start + jnp.arange(tokens, dtype=jnp.int32))
    attn_low, query_low, latent_low, compressed, inverse_one, inverse_kv = project(
        inputs, attn_scale[None], kv_scale[None], first_full, tables, heads
    )
    all_latent, shared_own = ctx_gather(latent_low, shared_sent, 5)
    all_latent = all_latent.reshape(ctx * tokens, -1)
    shared_own = jnp.swapaxes(shared_own, 0, 1).reshape(3 * piece, width)
    expanded = mm(all_latent[:, :R], expand_full).astype(BF)
    begin = start.astype(jnp.int32)[None]
    if parts == 2:
        expanded, shared_own, up_other = together((expanded, shared_own, up_other))
        shared_parts = [shared_own, swap_tp(shared_own)]
    else:
        shared_parts = list(lax.all_gather(shared_own, "tp", axis=0, tiled=False))
    attended, logs = attend(
        query_low, expanded, all_latent, segments[:, None], all_segments[None, :], begin, scale
    )
    attended, shared_parts = together((attended, shared_parts))
    shared = [
        jnp.concatenate([v[k * piece : (k + 1) * piece] for v in shared_parts], 0) for k in range(3)
    ]
    middle = own_half(residual) + other_half_sum(attended, lambda rows: mm_nt(rows, output_full))
    normed_two, inverse_two = norm_forward(middle, ffn_scale)
    ffn_low = normed_two.astype(BF)

    rank_row, share_row = rank[:, None, :], share[:, None, :]
    grad_rows, weights = pack(pairs, rank_row, share_row, cot_all, True)
    if parts == 2:
        ffn_low, grad_rows = together((ffn_low, grad_rows))
        rows_all, shared_out, shared_gin, *shared_grads, down_other = gather_shared(
            ffn_low, cot_all, shared, 2, swaps=[down]
        )
        gates, ups, downs = [gate, first[6]], [up, up_other], [down, down_other]
    else:
        rows_all, shared_out, shared_gin, *shared_grads = gather_shared(ffn_low, cot_all, shared, 2)
        gates, ups, downs = (list(lax.all_gather(v, "tp", axis=0, tiled=False)) for v in (gate, up, down))
    rows_in, _ = pack(pairs, rank_row, share_row, rows_all, False)
    expert_out, expert_gin, kept = experts(tiles, rows_in, grad_rows, weights, gates, ups, downs)

    grads_of = lambda which, *starts: expert_grads(
        tiles, rows_in, grad_rows, *(k[which] for k in kept), *starts
    )
    if parts == 2:
        expert_out, sent = together((expert_out, grads_of(1)))
        came = [swap_tp(v) for v in sent]
    moe_part, grad_part = dense(pairs, rank[:, :, None], shared_out, shared_gin, expert_out, expert_gin)
    (grad_normed_two,) = ring_scatter([grad_part], 3)
    if parts == 2:
        grad_normed_two, came = together((grad_normed_two, came))
        own_grads = grads_of(0, tuple(came))
    else:
        sent = [grads_of(k) for k in range(parts)]
        own_grads = [
            lax.psum_scatter(jnp.stack(v), "tp", scatter_dimension=0, tiled=False).astype(F32) for v in zip(*sent)
        ]

    grad_out = own_half(cotangent).astype(F32)
    grad_mid_norm, ffn_gain_grad = norm_backward(middle, inverse_two, ffn_scale, grad_normed_two)
    grad_middle = grad_out + grad_mid_norm
    grad_middle_low = join_tp(grad_middle.astype(BF))
    grad_middle_low, own_grads = together((grad_middle_low, own_grads))
    gate_grad, up_grad, down_grad = (
        jnp.swapaxes(own_grads[0], 0, 1)[None], jnp.swapaxes(own_grads[1], 0, 1)[None], own_grads[2][None]
    )
    shared_back = [
        jnp.concatenate([v[k * piece : (k + 1) * piece] for v in shared_grads], 0) for k in range(parts)
    ]
    shared_back, grad_middle_low = together((shared_back, grad_middle_low))
    if parts == 2:
        shared_back = (shared_back[0], swap_tp(shared_back[1].astype(BF)))
    else:
        shared_back = lax.psum_scatter(jnp.stack(shared_back).astype(BF), "tp", scatter_dimension=0, tiled=False)

    moe_part = lax.optimization_barrier((moe_part, grad_normed_two))[0]
    moe_total = lax.psum_scatter(
        moe_part.reshape(group * half, width), GROUP, scatter_dimension=0, tiled=True
    )

    grad_attended = mm(grad_middle_low, output_full).astype(BF)
    grad_nope, grad_turned, grad_kv, grad_rope = attend_back(
        query_low, expanded, all_latent, grad_attended, jnp.swapaxes(logs, 1, 2),
        segments[None, :], all_segments[:, None], begin, tables, scale,
    )
    shared_back, grad_kv = together((shared_back, grad_kv))
    if parts == 2:
        shared_back = shared_back[0] + shared_back[1].astype(F32)
    shared_back = jnp.swapaxes(shared_back.astype(BF).reshape(3 * piece, group, depth), 0, 1)
    output_grad = mm_tn(grad_middle_low, attended).astype(BF)
    grad_query = jnp.concatenate([grad_nope, grad_turned], 1)
    grad_comp = mm_nt(grad_kv, expand_full)
    grad_comp = jnp.concatenate([grad_comp.astype(BF), grad_rope], 1)
    grad_comp, shared_back = ctx_scatter(grad_comp.reshape(ctx, tokens, -1), shared_back, 6)
    expand_grad = mm_tn(all_latent[:, :R], grad_kv).astype(BF)
    query_grad = mm_tn(attn_low, grad_query).astype(BF)
    grad_compressed, kv_gain_grad = norm_backward(compressed, inverse_kv, kv_scale, grad_comp[:, :R])
    grad_latent = jnp.concatenate(
        [grad_compressed, turn_back(grad_comp[:, R : R + ROPE], tables)], -1
    ).astype(BF)
    latent_grad = mm_tn(attn_low, grad_latent).astype(BF)
    grad_first = jnp.concatenate([grad_query, grad_latent, jnp.zeros((tokens, 128 - ROPE), BF)], 1)
    grad_normed_one = other_half_sum(grad_first, lambda rows: mm_nt(rows, first_full))
    grad_in_norm, attn_gain_grad = norm_backward(
        own_half(residual), own_half(inverse_one), attn_scale, grad_normed_one
    )
    grad_inputs = join_tp((grad_middle + grad_in_norm).astype(BF))

    moe_total, attn_gain_grad = together((moe_total, attn_gain_grad))
    result = join_tp((middle + moe_total.astype(F32)).astype(BF))

    gain_grads = jnp.concatenate(
        [v.reshape(group, -1) for v in (attn_gain_grad, kv_gain_grad, ffn_gain_grad)], 1
    ).astype(BF)
    tail = jnp.zeros((group, 16, 384), BF).at[:, 0, : gain_grads.shape[1]].set(gain_grads)
    output_own, expand_own, query_own, latent_own, gains_own = ring_scatter(
        [
            output_grad.reshape(group, -1, output_grad.shape[1]),
            expand_grad.reshape(group, -1, expand_grad.shape[1]),
            query_grad.reshape(group, -1, query_width),
            latent_grad.reshape(group, -1, latent_grad.shape[1]),
            tail,
        ],
        4,
        pieces=1,
    )
    output_own = jnp.swapaxes(output_own, 0, 1)
    back = [shared_back[:, k * piece : (k + 1) * piece].reshape(-1, depth).astype(F32) for k in range(3)]
    sgate_grad, sup_grad, sdown_grad = jnp.swapaxes(back[0], 0, 1), jnp.swapaxes(back[1], 0, 1), back[2]
    nopes = query_own[:, : heads * NOPE].reshape(-1, heads, NOPE)
    query_own = jnp.concatenate([nopes, query_own[:, heads * NOPE :].reshape(-1, heads, ROPE)], -1)
    query_own = query_own.reshape(-1, query_width)
    if parts == 2:
        small = jnp.concatenate([latent_own.reshape(-1, 128), gains_own[:8].reshape(-1, 128)], 0)
        small = small + swap_tp(small)
        latent_own = small[: -gains_own[:8].size // 128].reshape(latent_own.shape)
        gains_own = small[-gains_own[:8].size // 128 :].reshape(8, -1)[0]
    else:
        latent_own, gains_own = lax.psum((latent_own, gains_own[0]), "tp")
    return (
        result,
        grad_inputs.astype(F32),
        gains_own[:n_attn],
        gains_own[n_attn : n_attn + n_kv],
        gains_own[n_attn + n_kv : gain_row.shape[0]],
        query_own,
        latent_own,
        expand_own,
        output_own,
        sgate_grad,
        sup_grad,
        sdown_grad,
        gate_grad,
        up_grad,
        down_grad,
    )


def solution(mesh):
    group = P(GROUP)
    rows = P(GROUP, None)
    both = P(GROUP, "tp")
    turned = P("tp", GROUP)
    return jax.shard_map(
        on_device,
        mesh=mesh,
        in_specs=(
            rows, group, rows, rows, rows, group, group, group,
            both, rows, both, turned, both, both, turned,
            P(GROUP, None, "tp"), P(GROUP, None, "tp"), P(GROUP, "tp", None),
        ),
        out_specs=(
            rows, rows, group, group, group,
            both, rows, both, turned, both, both, turned,
            P(GROUP, None, "tp"), P(GROUP, None, "tp"), P(GROUP, "tp", None),
        ),
        check_vma=False,
    )
```

time: 3540 us -> 1120 us (0.32)
  waiting for transfers between devices: 2270 us -> 70.6 us
  Pallas kernels: 0 us -> 850 us
  matrix products: 503 us -> 61.7 us
  local copies, waits for them, and re-layouts: 269 us -> 58.4 us
  starting transfers between devices: 184 us -> 12.1 us
  blocking collectives: 149 us -> 0 us
  other arithmetic: 142 us -> 46.4 us
    pallas_call x0 -> x15, Pallas kernels: none -> 850 us  [the longest x2 192 us: ring_scatter(): pl.pallas_call(functools.partial(scatter_kernel, nz, count, lanes), out_s...]
    reduce_scatter x9 -> x1, waiting for transfers between devices: 745 us -> 0.01 us  [on_device(): lax.psum_scatter(moe_part.reshape(group * half, width), GROUP, scatter_di...]
    all_to_all x4 -> x0, waiting for transfers between devices: 671 us -> none  [the longest x1 294 us: on_device(): lax.all_to_all(grad_dispatch, ('shard', 'ctx'), split_axis=0, concat_axis...]
    all_gather x8 -> x1, waiting for transfers between devices: 546 us -> 9.78 us  [on_device(): lax.all_gather(together((own_half(cotangent), gains))[0], GROUP, axis=0,...]
    dot_general x39 -> x12, matrix products: 503 us -> 61.7 us  [the longest x5 25.1 us: mm_nt(): lax.dot_general(a, b, (((1,), (1,)), ((), ())), preferred_element_type=F32)]
    psum x3 -> x0, waiting for transfers between devices: 301 us -> none  [the longest x1 151 us: on_device(): moe_total = lax.psum(shared_part + combined, 'tp')]
    all_to_all x4 -> x0, starting transfers between devices: 182 us -> none  [the longest x1 79.1 us: on_device(): lax.all_to_all(grad_dispatch, ('shard', 'ctx'), split_axis=0, concat_axis...]
    gather x4 -> x0, local copies, waits for them, and re-layouts: 144 us -> none  [the longest x1 41.3 us: on_device(): jnp.concatenate([weighted, jnp.zeros((1, width), jnp.bfloat16)], 0)]
  transfers between devices with their start and end apart: 24 -> 14, of which waited for: 20 -> 7; matrix products, arithmetic and copies ran while one was open for 19% -> 13% of each run, Pallas kernels for 0% -> 38%
where the time goes in v1:
time: 1120 us
  Pallas kernels  850 us (76%)
  waiting for transfers between devices  70.6 us (6%)
  matrix products  61.7 us (6%)
  local copies, waits for them, and re-layouts  58.4 us (5%)
  other arithmetic  46.4 us (4%)
  between operations  16.5 us (1%)
  starting transfers between devices  12.1 us (1%)
    pallas_call x2, Pallas kernels, ring_scatter(): pl.pallas_call(functools.partial(scatter_kernel, nz, count, lanes), out_s...  192 us
    pallas_call x1, Pallas kernels, gather_shared(): pl.pallas_call(functools.partial(gather_shared_kernel, nz, len(swaps), la...  129 us
    pallas_call x1, Pallas kernels, experts(): pl.pallas_call(functools.partial(expert_kernel, parts), out_shape=(jax.Sh...  119 us
    pallas_call x1, Pallas kernels, ring_gather(): pl.pallas_call(functools.partial(gather_kernel, nz, count, len(swaps), la...  90.5 us
    pallas_call x2, Pallas kernels, expert_grads(): pl.pallas_call(kernel, out_shape=(jax.ShapeDtypeStruct((hidden, width), B...  69 us
    pallas_call x2, Pallas kernels, pack(): pl.pallas_call(functools.partial(pack_kernel, weighted=weighted), out_sha...  52.3 us
    pallas_call x1, Pallas kernels, ctx_scatter(): pl.pallas_call(functools.partial(ctx_scatter_kernel, nz, pieces), out_sha...  48.3 us
    pallas_call x1, Pallas kernels, dense(): pl.pallas_call(dense_kernel, out_shape=(jax.ShapeDtypeStruct((blocks, tok...  44.4 us
  transfers between devices with their start and end apart: 14, of which 7 were waited for; matrix products, arithmetic and copies ran while one was open for 13% of the time, Pallas kernels for 38%

profile of v1, /device:TPU:0, one launch (start us, length us, event | category | flops | bytes accessed | tf_op | source)
XLA Modules:
  0.0 1115.7 jit_solution(4868581572772136520)
XLA Ops:
  7.3 1.4 copy.129
  16.2 90.5 %ring_gather.1 = (bf16[16,128,2176]{2,1,0:T(8,128)(2,1)}, bf16[16,128,1024]{2,1,0:T(8,128)(2,1)}, bf16[16,32,2048]{2,1,0:T(8,128)(2,1)}, bf16[16,16,384]{2,1,0:T...) custom-call(bf16[128,2176]{1,0:T(8,128)(2,1)} %concatenate.79.refs_0_, ...), custom_call_target="tpu_custom_call" | custom-call | flops 76677120000 | bytes 32374784 | tf_op jit(solution)/shard_map/ring_gather/pallas_call | solution.py:216
  106.8 1.6 collective-permute-start
  117.9 1.5 slice_convert_fusion.2
  119.4 11.4 %project.1 = (bf16[512,2048]{1,0:T(8,128)(2,1)}, bf16[512,1536]{1,0:T(8,128)(2,1)S(1)}, bf16[512,640]{1,0:T(8,128)(2,1)S(1)}, f32[512,512]{1,0:T(8,128)S(1)}, f3...) custom-call(bf16[512,2048]{1,0:T(8,128)(2,1)} %x_ref.1, f32[1,2048]{1,0:T(1,128)S(1)} %get-tuple-element.319.gain, ...), custom_call_target="tpu_custom_call" | custom-call | flops 4563402752 | bytes 20971520 | tf_op jit(solution)/shard_map/project/pallas_call | solution.py:669
  132.8 35.7 %ctx_gather.1 = (bf16[4,512,640]{2,1,0:T(8,128)(2,1)}, bf16[16,264,128]{2,1,0:T(8,128)(2,1)}) custom-call(bf16[512,640]{1,0:T(8,128)(2,1)} %copy-done.10, bf16[16,264,128]{2,1,0:T(8,128)(2,1)} %pad_maximum_fusion.3.t_ref), custom_call_target="tpu_custom_call" | custom-call | flops 19660800000 | bytes 1310720 | tf_op jit(solution)/shard_map/ctx_gather/pallas_call | solution.py:433
  168.5 1.5 copy_bitcast_fusion
  170.4 8.3 convolution_convert_fusion.1.kv_ref
  178.8 1.5 collective-permute-start.1
  183.0 2.0 copy.139.rank
  187.0 24.7 %attend.1 = (bf16[512,1024]{1,0:T(8,128)(2,1)}, f32[8,512,1]{2,1,0:T(8,128)}) custom-call(s32[1]{0:T(128)} %bitcast.start, bf16[512,1536]{1,0:T(8,128)(2,1)} %copy-done.8, bf16[512,1536]{1,0:T(8,128)(2,1)} %copy-done.8, bf16[2048,2048]{1,0:T(8,128)(2,1)} %convolution_convert_fusion.1.kv_ref, bf16[2048,640]{1,0:T(8,128)(2,1)} %bitcast.181, ...), custom_call_target="tpu_custom_call" | custom-call | flops 6442450944 | bytes 12582912 | tf_op jit(solution)/shard_map/attend/pallas_call | solution.py:716
  211.7 3.6 convolution_convert_fusion.6
  215.9 1.5 fusion.54
  220.2 20.0 %collective-permute-done.2 = bf16[256,2048]{1,0:T(8,128)(2,1)S(1)} collective-permute-done((bf16[256,2048]{1,0:T(8,128)(2,1)S(1)}, bf16[256,2048]{1,0:T(8,128)(2,1)S(1)}, u32[]{:S(2)}, u32[]{:S(2)}) %collective-permute-start.2) | collective-permute-done | bytes 1048608 | tf_op jit(solution)/shard_map/ppermute | solution.py:1114
  240.2 1.6 multiply_reduce_fusion.2
  244.4 9.8 all-gather.3.cloned.1.call-done
  254.2 26.0 %pack.2 = (bf16[4096,2048]{1,0:T(8,128)(2,1)}, f32[4096,1]{1,0:T(8,128)S(1)}) custom-call(s32[32]{0:T(128)S(1)} %add_subtract_fusion.pair_tile, s32[32]{0:T(128)S(1)} %convert_reduce_fusion.pair_block, s32[32]{0:T(128)S(1)} %get-tuple-element.334.pair_first, s32[32]{0:T(128)S(1)} %get-tuple-element.335.pair_on, s32[16,1,256]{2,1,0:T(1,128)S(1)} %broadcast_in_dim.148.rank, ...), custom_call_target="tpu_custom_call" | custom-call | flops 6442450944 | bytes 29360128 | tf_op jit(solution)/shard_map/pack/pallas_call | solution.py:861
  280.2 1.3 copy-done.9
  281.5 129.3 %gather_shared.1 = (bf16[16,256,2048]{2,1,0:T(8,128)(2,1)}, bf16[16,256,2048]{2,1,0:T(8,128)(2,1)}, bf16[16,256,2048]{2,1,0:T(8,128)(2,1)}, f32[176,2048]{1,0:T(...) custom-call(bf16[256,2048]{1,0:T(8,128)(2,1)} %multiply_convert_fusion.row_ref, ...), custom_call_target="tpu_custom_call" | custom-call | flops 79471026176 | bytes 33554432 | tf_op jit(solution)/shard_map/gather_shared/pallas_call | solution.py:372
  410.9 26.3 %pack.3 = (bf16[4096,2048]{1,0:T(8,128)(2,1)}, f32[4096,1]{1,0:T(8,128)}) custom-call(s32[32]{0:T(128)S(1)} %add_subtract_fusion.pair_tile, s32[32]{0:T(128)S(1)} %convert_reduce_fusion.pair_block, s32[32]{0:T(128)S(1)} %get-tuple-element.334.pair_first, s32[32]{0:T(128)S(1)} %get-tuple-element.335.pair_on, s32[16,1,256]{2,1,0:T(1,128)S(1)} %broadcast_in_dim.148.rank, ...), custom_call_target="tpu_custom_call" | custom-call | flops 6442450944 | bytes 29360128 | tf_op jit(solution)/shard_map/pack/pallas_call | solution.py:861
  437.1 119.2 %experts.1 = (bf16[4096,2048]{1,0:T(8,128)(2,1)}, bf16[4096,2048]{1,0:T(8,128)(2,1)}, bf16[4096,704]{1,0:T(8,128)(2,1)}, bf16[4096,704]{1,0:T(8,128)(2,1)}, bf16...) custom-call(s32[1]{0:T(128)} %bitcast.30.tiles, ...), custom_call_target="tpu_custom_call" | custom-call | flops 88583700480 | bytes 104857600 | tf_op jit(solution)/shard_map/experts/pallas_call | solution.py:924
  556.3 31.0 %expert_grads.2 = (bf16[704,2048]{1,0:T(8,128)(2,1)}, bf16[704,2048]{1,0:T(8,128)(2,1)}, bf16[704,2048]{1,0:T(8,128)(2,1)}) custom-call(s32[1]{0:T(128)} %bitcast.30.tiles, bf16[4096,2048]{1,0:T(8,128)(2,1)} %get-tuple-element.147.x_ref, bf16[4096,2048]{1,0:T(8,128)(2,1)} %get-tuple-element.148.g_ref, bf16[4096,704]{1,0:T(8,128)(2,1)} %get-tuple-element.154.hid_ref, ...), custom_call_target="tpu_custom_call" | custom-call | flops 22145925120 | bytes 41943040 | tf_op jit(solution)/shard_map/expert_grads/pallas_call | solution.py:994
  587.3 1.5 collective-permute-start.3
  589.4 1.5 collective-permute-start.5
  590.8 44.4 %dense.1 = (bf16[16,256,2048]{2,1,0:T(8,128)(2,1)}, bf16[16,256,2048]{2,1,0:T(8,128)(2,1)}) custom-call(s32[32]{0:T(128)} %copy-done.7, s32[32]{0:T(128)} %copy-done.6, s32[32]{0:T(128)} %get-tuple-element.330.pair_first, s32[32]{0:T(128)} %and_convert_fusion.2.pair_last, s32[32]{0:T(128)} %get-tuple-element.329.pair_real, s32[16,256,1]{2,1,0:T(8,128)} %copy.139.rank, ...), custom_call_target="tpu_custom_call" | custom-call | flops 13958643712 | bytes 94371840 | tf_op jit(solution)/shard_map/dense/pallas_call | solution.py:1042
  635.2 101.6 %ring_scatter.2 = f32[256,2048]{1,0:T(8,128)} custom-call(bf16[16,256,2048]{2,1,0:T(8,128)(2,1)} %get-tuple-element.163.refs_0_), custom_call_target="tpu_custom_call" | custom-call | flops 79471026176 | bytes 33554432 | tf_op jit(solution)/shard_map/ring_scatter/pallas_call | solution.py:605
  736.9 7.2 collective-permute-done.5.refs_2_
  744.9 1.4 copy.141.seg_k
  747.8 2.3 reduce.6
  750.7 1.3 slice.185
  754.9 1.7 copy-done.12
  758.2 1.4 copy-done.18
  759.6 2.3 fusion.51
  761.9 1.6 collective-permute-start.6
  763.5 38.0 %expert_grads.3 = (f32[704,2048]{1,0:T(8,128)}, f32[704,2048]{1,0:T(8,128)}, f32[704,2048]{1,0:T(8,128)}) custom-call(s32[1]{0:T(128)} %bitcast.30.tiles, bf16[4096,2048]{1,0:T(8,128)(2,1)} %get-tuple-element.147.x_ref, bf16[4096,2048]{1,0:T(8,128)(2,1)} %get-tuple-element.148.g_ref, bf16[4096,704]{1,0:T(8,128)(2,1)} %get-tuple-element.172.hid_ref, ...), custom_call_target="tpu_custom_call" | custom-call | flops 22145925120 | bytes 41943040 | tf_op jit(solution)/shard_map/expert_grads/pallas_call | solution.py:994
  801.6 2.9 maximum_select_fusion
  805.1 3.3 convolution_convert_fusion.8.g_ref
  808.4 33.5 %attend_back.1 = (bf16[512,1024]{1,0:T(8,128)(2,1)}, bf16[512,512]{1,0:T(8,128)(2,1)}, bf16[2048,2048]{1,0:T(8,128)(2,1)}, bf16[2048,128]{1,0:T(8,128)(2,1)}) custom-call(s32[1]{0:T(128)} %bitcast.start, bf16[512,1536]{1,0:T(8,128)(2,1)} %copy-done.8, bf16[512,1536]{1,0:T(8,128)(2,1)} %copy-done.8, bf16[2048,2048]{1,0:T(8,128)(2,1)} %convolution_convert_fusion.1.kv_ref, ...), custom_call_target="tpu_custom_call" | custom-call | flops 17179869184 | bytes 25165824 | tf_op jit(solution)/shard_map/attend_back/pallas_call | solution.py:792
  842.0 2.0 copy.142
  844.4 6.6 convolution_convert_fusion.2
  851.1 6.0 convolution_convert_fusion
  857.1 2.3 collective-permute-done.7
  859.4 4.8 convolution_convert_fusion.5
  864.2 1.7 pad_maximum_fusion
  865.9 4.4 copy.143
  870.3 1.6 bitcast_bitcast_fusion.t_ref
  872.4 48.3 %ctx_scatter.1 = (f32[512,640]{1,0:T(8,128)S(1)}, bf16[16,264,128]{2,1,0:T(8,128)(2,1)S(1)}) custom-call(bf16[4,512,640]{2,1,0:T(8,128)(2,1)S(1)} %bitcast.121, bf16[16,264,128]{2,1,0:T(8,128)(2,1)S(1)} %bitcast_bitcast_fusion.t_ref), custom_call_target="tpu_custom_call" | custom-call | flops 19660800000 | bytes 5242880 | tf_op jit(solution)/shard_map/ctx_scatter/pallas_call | solution.py:509
  921.3 1.8 add_convert_fusion.2
  924.2 4.3 concatenate.93
  928.5 7.6 convolution_convert_fusion.7
  939.1 3.1 convolution_convert_fusion.3
  942.2 2.7 copy.145
  945.9 15.7 %collective-permute-done.8 = bf16[256,2048]{1,0:T(8,128)(2,1)} collective-permute-done((bf16[256,2048]{1,0:T(8,128)(2,1)}, bf16[256,2048]{1,0:T(8,128)(2,1)}, u32[]{:S(2)}, u32[]{:S(2)}) %collective-permute-start.8) | collective-permute-done | bytes 1048608 | tf_op jit(solution)/shard_map/ppermute | solution.py:1114
  961.5 7.4 fusion
  970.8 9.1 convolution_convert_fusion.4
  979.9 14.1 %collective-permute-done.10 = bf16[256,2048]{1,0:T(8,128)(2,1)S(1)} collective-permute-done((bf16[256,2048]{1,0:T(8,128)(2,1)S(1)}, bf16[256,2048]{1,0:T(8,128)(2,1)S(1)}, u32[]{:S(2)}, u32[]{:S(2)}) %collective-permute-start.10) | collective-permute-done | bytes 1048608 | tf_op jit(solution)/shard_map/ppermute | solution.py:1119
  994.0 1.6 maximum_select_fusion.2
  996.3 1.5 add_convert_fusion.1
  999.0 90.0 %ring_scatter.3 = (f32[128,1024]{1,0:T(8,128)}, f32[32,2048]{1,0:T(8,128)}, f32[128,1536]{1,0:T(8,128)}, f32[128,576]{1,0:T(8,128)}, f32[16,384]{1,0:T(8,128)}) custom-call(bf16[16,128,1024]{2,1,0:T(8,128)(2,1)} %bitcast.179, bf16[16,32,2048]{2,1,0:T(8,128)(2,1)} %bitcast.186, bf16[16,128,1536]{2,1,0:T(8,128)(2,1)} %bitcast.172, ...), custom_call_target="tpu_custom_call" | custom-call | flops 71710179328 | bytes 30277632 | tf_op jit(solution)/shard_map/ring_scatter/pallas_call | solution.py:605
  1088.9 1.8 reshape.404
  1092.5 1.8 collective-permute-start.11
  1094.3 2.7 bitcast_convert_fusion
  1099.6 1.6 collective-permute-done.11
  1104.8 3.2 maximum_select_fusion.1
  (244 shorter events, 55.8 us)
Async XLA Ops:
  7.2 2.3 copy-start
  7.2 4.0 copy-start.35
  7.2 5.2 copy-start.17
  7.2 246.9 %all-gather.3.cloned.1.call-start = ((), (), s32[]{:S(2)}) async-start(), calls=%async_computation.2 | async-start | bytes 17825792 | tf_op jit(solution)/shard_map/all_gather | solution.py:1212
  12.1 3.5 copy-start.48
  16.2 94.3 %copy-start.32 = (bf16[128,1408]{1,0:T(8,128)(2,1)S(1)}, bf16[128,1408]{1,0:T(8,128)(2,1)}, u32[]{:S(2)}) copy-start(bf16[128,1408]{1,0:T(8,128)(2,1)} %param.34) | copy-start | bytes 1081348
  106.7 4.0 copy-start.33
  106.8 888.9 %reduce-scatter.2.cloned.1.call-start = ((), (), s32[]{:S(2)}) async-start(), calls=%async_computation.1 | async-start | bytes 17825792 | tf_op jit(solution)/shard_map/reduce_scatter | solution.py:1292
  106.8 72.0 %collective-permute-start = (bf16[704,2048]{1,0:T(8,128)(2,1)}, bf16[704,2048]{1,0:T(8,128)(2,1)}, u32[]{:S(2)}, u32[]{:S(2)}) collective-permute-start(bf16[704,2048]{1,0:T(8,128)(2,1)} %bitcast.167), channel_id=1, source_target_pairs={{0,1},{1,0},{2,3},{3,2},{4,5},{5,4},{6,7},{7,6},{8,9},{9,8},{10,11... | collective-permute-start | bytes 8650760 | tf_op jit(solution)/shard_map/ppermute | solution.py:1119
  110.5 5.0 copy-start.34
  113.5 3.2 copy-start.52
  113.5 3.1 copy-start.42
  113.6 297.2 %copy-start.6 = (s32[32]{0:T(128)}, s32[32]{0:T(128)S(1)}, u32[]{:S(2)}) copy-start(s32[32]{0:T(128)S(1)} %convert_reduce_fusion.pair_block) | copy-start | bytes 388
  115.0 15.8 %copy-start.5 = (f32[512,128]{1,0:T(8,128)}, f32[512,128]{1,0:T(8,128)S(1)}, u32[]{:S(2)}) copy-start(f32[512,128]{1,0:T(8,128)S(1)} %pad_maximum_fusion.8.cosine) | copy-start | bytes 786436
  115.5 15.3 %copy-start.3 = (f32[512,128]{1,0:T(8,128)}, f32[512,128]{1,0:T(8,128)S(1)}, u32[]{:S(2)}) copy-start(f32[512,128]{1,0:T(8,128)S(1)} %get-tuple-element.316.second) | copy-start | bytes 786436
  115.5 15.3 %copy-start.4 = (f32[512,128]{1,0:T(8,128)}, f32[512,128]{1,0:T(8,128)S(1)}, u32[]{:S(2)}) copy-start(f32[512,128]{1,0:T(8,128)S(1)} %get-tuple-element.317.first) | copy-start | bytes 786436
  117.8 293.0 %copy-start.7 = (s32[32]{0:T(128)}, s32[32]{0:T(128)S(1)}, u32[]{:S(2)}) copy-start(s32[32]{0:T(128)S(1)} %add_subtract_fusion.pair_tile) | copy-start | bytes 388
  119.4 123.0 %copy-start.37 = (f32[16,1,128]{2,1,0:T(1,128)}, f32[16,1,128]{2,1,0:T(1,128)S(1)}, u32[]{:S(2)}) copy-start(f32[16,1,128]{2,1,0:T(1,128)S(1)} %get-tuple-element.320) | copy-start | bytes 24580
  178.8 32.9 %collective-permute-start.1 = (bf16[264,2048]{1,0:T(8,128)(2,1)S(1)}, bf16[264,2048]{1,0:T(8,128)(2,1)}, u32[]{:S(2)}, u32[]{:S(2)}) collective-permute-start(bf16[264,2048]{1,0:T(8,128)(2,1)S(1)} %copy_bitcast_fusion), channel_id=1, source_target_pairs={{0,1},{1,0},{2,3},{3,2},{4,5},{5,4},{6,7},{7,6},{8,9},{9,8},{10,11... | collective-permute-start | bytes 3244040 | tf_op jit(solution)/shard_map/ppermute | solution.py:1119
  215.4 24.8 %collective-permute-start.2 = (bf16[256,2048]{1,0:T(8,128)(2,1)S(1)}, bf16[256,2048]{1,0:T(8,128)(2,1)S(1)}, u32[]{:S(2)}, u32[]{:S(2)}) collective-permute-start(bf16[256,2048]{1,0:T(8,128)(2,1)S(1)} %convolution_convert_fusion.6), channel_id=1, source_target_pairs={{0,1},{1,0},{2,3},{3,2},{4,5},{5,4},{6,7},{7,6},{8,9},{9,8},{10,11... | collective-permute-start | bytes 3145736 | tf_op jit(solution)/shard_map/ppermute | solution.py:1114
  215.9 24.2 %copy-start.54 = (bf16[16,128,1024]{2,1,0:T(8,128)(2,1)S(1)}, bf16[16,128,1024]{2,1,0:T(8,128)(2,1)}, u32[]{:S(2)}) copy-start(bf16[16,128,1024]{2,1,0:T(8,128)(2,1)} %get-tuple-element.137) | copy-start | bytes 12582916
  217.5 22.7 %copy-start.26 = (bf16[512,2048]{1,0:T(8,128)(2,1)S(1)}, bf16[512,2048]{1,0:T(8,128)(2,1)}, u32[]{:S(2)}) copy-start(bf16[512,2048]{1,0:T(8,128)(2,1)} %x_ref.1) | copy-start | bytes 6291460
  217.5 22.7 %copy-start.59 = (bf16[512,1024]{1,0:T(8,128)(2,1)S(1)}, bf16[512,1024]{1,0:T(8,128)(2,1)}, u32[]{:S(2)}) copy-start(bf16[512,1024]{1,0:T(8,128)(2,1)} %get-tuple-element.136) | copy-start | bytes 3145732
  242.4 37.7 %copy-start.45 = (f32[256]{0:T(256)}, f32[256]{0:T(256)S(1)}, u32[]{:S(2)}) copy-start(f32[256]{0:T(256)S(1)} %get-tuple-element.325) | copy-start | bytes 3076
  587.3 149.5 %collective-permute-start.3 = (bf16[704,2048]{1,0:T(8,128)(2,1)}, bf16[704,2048]{1,0:T(8,128)(2,1)}, u32[]{:S(2)}, u32[]{:S(2)}) collective-permute-start(bf16[704,2048]{1,0:T(8,128)(2,1)} %get-tuple-element.164), channel_id=1, source_target_pairs={{0,1},{1,0},{2,3},{3,2},{4,5},{5,4},{6,7},{7,6},{8,9},{9,8},{10,11... | collective-permute-start | bytes 8650760 | tf_op jit(solution)/shard_map/ppermute | solution.py:1119
  588.8 148.0 %collective-permute-start.4 = (bf16[704,2048]{1,0:T(8,128)(2,1)}, bf16[704,2048]{1,0:T(8,128)(2,1)}, u32[]{:S(2)}, u32[]{:S(2)}) collective-permute-start(bf16[704,2048]{1,0:T(8,128)(2,1)} %get-tuple-element.165), channel_id=1, source_target_pairs={{0,1},{1,0},{2,3},{3,2},{4,5},{5,4},{6,7},{7,6},{8,9},{9,8},{10,11... | collective-permute-start | bytes 8650760 | tf_op jit(solution)/shard_map/ppermute | solution.py:1119
  589.4 154.6 %collective-permute-start.5 = (bf16[704,2048]{1,0:T(8,128)(2,1)}, bf16[704,2048]{1,0:T(8,128)(2,1)}, u32[]{:S(2)}, u32[]{:S(2)}) collective-permute-start(bf16[704,2048]{1,0:T(8,128)(2,1)} %get-tuple-element.166), channel_id=1, source_target_pairs={{0,1},{1,0},{2,3},{3,2},{4,5},{5,4},{6,7},{7,6},{8,9},{9,8},{10,11... | collective-permute-start | bytes 8650760 | tf_op jit(solution)/shard_map/ppermute | solution.py:1119
  744.9 175.8 %copy-start.44 = (f32[512]{0:T(512)}, f32[512]{0:T(512)S(1)}, u32[]{:S(2)}) copy-start(f32[512]{0:T(512)S(1)} %reshape.413) | copy-start | bytes 6148
  747.8 172.9 %copy-start.41 = (f32[512]{0:T(512)}, f32[512]{0:T(512)S(1)}, u32[]{:S(2)}) copy-start(f32[512]{0:T(512)S(1)} %get-tuple-element.292) | copy-start | bytes 6148
  747.8 5.6 copy-start.24
  750.7 2.7 copy-start.23
  754.7 3.0 copy-start.16
  754.7 3.0 copy-start.38
  754.7 3.0 copy-start.46
  761.9 39.7 %collective-permute-start.6 = (bf16[256,2048]{1,0:T(8,128)(2,1)}, bf16[256,2048]{1,0:T(8,128)(2,1)}, u32[]{:S(2)}, u32[]{:S(2)}) collective-permute-start(bf16[256,2048]{1,0:T(8,128)(2,1)} %get-tuple-element.298), channel_id=1, source_target_pairs={{0,1},{1,0},{2,3},{3,2},{4,5},{5,4},{6,7},{7,6},{8,9},{9,8},{10,11... | collective-permute-start | bytes 3145736 | tf_op jit(solution)/shard_map/ppermute | solution.py:1119
  801.6 3.5 copy-start.55
  804.4 4.0 copy-start.20
  844.0 7.1 copy-start.22
  844.0 7.1 copy-start.28
  844.0 7.1 copy-start.60
  844.0 15.4 %collective-permute-start.7 = (bf16[264,2048]{1,0:T(8,128)(2,1)}, bf16[264,2048]{1,0:T(8,128)(2,1)S(1)}, u32[]{:S(2)}, u32[]{:S(2)}) collective-permute-start(bf16[264,2048]{1,0:T(8,128)(2,1)} %pad_maximum_fusion.2), channel_id=1, source_target_pairs={{0,1},{1,0},{2,3},{3,2},{4,5},{5,4},{6,7},{7,6},{8,9},{9,8},{10,11... | collective-permute-start | bytes 3244040 | tf_op jit(solution)/shard_map/ppermute | solution.py:1119
  844.4 14.9 %slice-start = ((s8[8388608]{0:T(1024)(128)(4,1)}), s8[4194304]{0:T(1024)(128)(4,1)S(1)}, s32[]{:S(2)}) async-start(s8[8388608]{0:T(1024)(128)(4,1)} %bitcast.187), calls=%async_computation.3 | async-start | bytes 8388608
  851.1 8.3 copy-start.58
  851.1 8.3 slice-start.1
  859.4 4.9 copy-start.21
  859.4 4.8 copy-start.19
  870.3 2.1 copy-start.2
  920.7 2.5 copy-start.47
  921.1 3.1 copy-start.29
  936.2 25.4 %collective-permute-start.8 = (bf16[256,2048]{1,0:T(8,128)(2,1)}, bf16[256,2048]{1,0:T(8,128)(2,1)}, u32[]{:S(2)}, u32[]{:S(2)}) collective-permute-start(bf16[256,2048]{1,0:T(8,128)(2,1)} %convolution_convert_fusion.7), channel_id=1, source_target_pairs={{0,1},{1,0},{2,3},{3,2},{4,5},{5,4},{6,7},{7,6},{8,9},{9,8},{10,11... | collective-permute-start | bytes 3145736 | tf_op jit(solution)/shard_map/ppermute | solution.py:1114
  936.7 2.4 copy-start.31
  942.2 19.4 %copy-start.39 = (f32[16,1,128]{2,1,0:T(1,128)S(1)}, f32[16,1,128]{2,1,0:T(1,128)}, u32[]{:S(2)}) copy-start(f32[16,1,128]{2,1,0:T(1,128)} %get-tuple-element.318) | copy-start | bytes 24580
  942.2 19.4 %copy-start.50 = (f32[256]{0:T(256)S(1)}, f32[256]{0:T(256)}, u32[]{:S(2)}) copy-start(f32[256]{0:T(256)} %get-tuple-element.291) | copy-start | bytes 3076
  961.5 7.5 copy-start.15
  961.5 7.5 copy-start.27
  961.5 7.5 copy-start.49
  969.7 24.3 %collective-permute-start.10 = (bf16[256,2048]{1,0:T(8,128)(2,1)S(1)}, bf16[256,2048]{1,0:T(8,128)(2,1)S(1)}, u32[]{:S(2)}, u32[]{:S(2)}) collective-permute-start(bf16[256,2048]{1,0:T(8,128)(2,1)S(1)} %fusion.6), channel_id=1, source_target_pairs={{0,1},{1,0},{2,3},{3,2},{4,5},{5,4},{6,7},{7,6},{8,9},{9,8},{10,11... | collective-permute-start | bytes 3145736 | tf_op jit(solution)/shard_map/ppermute | solution.py:1119
  994.0 2.3 copy-start.13
  997.8 106.9 %collective-permute-start.9 = (bf16[256,2048]{1,0:T(8,128)(2,1)S(1)}, bf16[256,2048]{1,0:T(8,128)(2,1)}, u32[]{:S(2)}, u32[]{:S(2)}) collective-permute-start(bf16[256,2048]{1,0:T(8,128)(2,1)S(1)} %add_convert_fusion.1), channel_id=1, source_target_pairs={{0,1},{1,0},{2,3},{3,2},{4,5},{5,4},{6,7},{7,6},{8,9},{9,8},{10,11... | collective-permute-start | bytes 3145736 | tf_op jit(solution)/shard_map/ppermute | solution.py:1119
  999.0 95.3 %copy-start.14 = (bf16[2,256,2048]{2,1,0:T(8,128)(2,1)S(1)}, bf16[2,256,2048]{2,1,0:T(8,128)(2,1)}, u32[]{:S(2)}) copy-start(bf16[2,256,2048]{2,1,0:T(8,128)(2,1)} %maximum_select_fusion.2) | copy-start | bytes 6291460
  1092.5 4.5 copy-start.25
  1092.5 8.7 collective-permute-start.11
  1104.8 3.9 copy-start.1
  1104.8 3.2 copy-start.36
  (13 other events, 17.8 us)
Sparse Core Ops, SparseCore 0:
  106.9 147.2 all-gather.2
  744.2 199.0 reduce-scatter.1

commit v2 on v1

--- a/solution.py
+++ b/solution.py
@@ -32,13 +32,6 @@
         scaled * values, -1, keepdims=True
     )
     return (value_grad, gain_grad)
-
-
-def rotate(values, sines, cosines):
-    half_width = values.shape[-1] // 2
-    first = values[..., :half_width]
-    second = values[..., half_width:]
-    return jnp.concatenate([first * cosines - second * sines, second * cosines + first * sines], -1)
 
 
 def angles(positions):
@@ -246,41 +239,46 @@
         z, x = ring_at(nz, place)
         return z * 4 + x * 2 + which
 
-    def ring_copy(lane, step):
+    def ring_copy(lane, step, src=None):
         _, towards, row, rows = lanes[lane]
         ref = all_ref.at[block(me - towards * step, core), pl.ds(row, rows)]
-        return remote(ref, ref, send.at[lane, step], recv.at[lane, step], right if towards > 0 else left)
-
-    def sibling_copy(lane, step, which):
+        src = ref if src is None else src.at[pl.ds(row, rows)]
+        return remote(src, ref, send.at[lane, step], recv.at[lane, step], right if towards > 0 else left)
+
+    def sibling_copy(lane, step, which, src=None):
         _, towards, row, rows = lanes[lane]
         ref = all_ref.at[block(me - towards * step, which), pl.ds(row, rows)]
-        return remote(ref, ref, sib_send.at[lane, step], sib_recv.at[lane, step], sibling)
-
-    def pieces_of(slot, step):
-        which = core if slot == 0 else 1 - core
+        src = ref if src is None else src.at[pl.ds(row, rows)]
+        return remote(src, ref, sib_send.at[lane, step], sib_recv.at[lane, step], sibling)
+
+    def pieces_of(beside, step):
+        which = 1 - core if beside else core
         return [(k, block(me - towards * step, which), pl.ds(row, rows)) for k, (towards, row, rows) in enumerate(halves)]
 
-    def taken(slot, step):
+    def taken(beside, step):
+        slot = 2 * beside + lax.rem(step, 2)
         return [
             pltpu.make_async_copy(src.at[here, piece], dst.at[slot, piece], loads.at[slot, k, j])
-            for k, here, piece in pieces_of(slot, step)
+            for k, here, piece in pieces_of(beside, step)
             for j, (src, dst) in enumerate(((all_ref, xs), (cot_ref, cs)))
         ]
 
-    def given(slot, step):
+    def given(beside, step):
+        slot = 2 * beside + lax.rem(step, 2)
         return [
             pltpu.make_async_copy(src.at[slot, piece], dst.at[here, piece], stores.at[slot, k, j])
-            for k, here, piece in pieces_of(slot, step)
+            for k, here, piece in pieces_of(beside, step)
             for j, (src, dst) in enumerate(((outs, out_ref), (gins, gin_ref)))
         ]
 
-    def work(slot, step, first_time):
-        for copy in taken(slot, step):
+    def work(beside, step):
+        slot = 2 * beside + lax.rem(step, 2)
+        for copy in taken(beside, step):
             copy.wait()
 
-        @pl.when(jnp.logical_not(first_time))
+        @pl.when(step > 1)
         def _():
-            for copy in given(slot, jnp.maximum(step - 1, 0)):
+            for copy in given(beside, step - 2):
                 copy.wait()
 
         x, c = xs[slot], cs[slot]
@@ -297,11 +295,15 @@
         dg_ref[...] += mm_tn(grad_gate, x)
         du_ref[...] += mm_tn(grad_up, x)
         dd_ref[...] += mm_tn(hidden, c)
-        for copy in given(slot, step):
+        for copy in given(beside, step):
             copy.start()
 
-    local = pltpu.make_async_copy(row_ref, all_ref.at[block(me, core)], own_sem)
+    local = pltpu.make_async_copy(row_ref, xs.at[3], own_sem)
     local.start()
+    for lane in range(len(lanes)):
+        ring_copy(lane, 0, row_ref).start()
+    for lane in range(len(lanes)):
+        sibling_copy(lane, 0, core, row_ref).start()
     swapped = [
         remote(swap_in[i], swap_out[i], swap_sem.at[0, i], swap_sem.at[1, i], across) for i in range(swaps)
     ]
@@ -311,48 +313,58 @@
     du_ref[...] = jnp.zeros_like(du_ref)
     dd_ref[...] = jnp.zeros_like(dd_ref)
     local.wait()
-
-    def one_step(step, carry):
-        for lane in range(len(lanes)):
+    local = pltpu.make_async_copy(xs.at[3], all_ref.at[block(me, core)], own_sem)
+    local.start()
+    local.wait()
+
+    def pass_on(step, some):
+        for lane in some:
 
             @pl.when(jnp.logical_and(step > 0, step < steps))
             def _(lane=lane):
-                ring_copy(lane, jnp.maximum(step - 1, 0)).wait_recv()
-
-            @pl.when(step < steps - 1)
+                ring_copy(lane, step - 1).wait_recv()
+
+            @pl.when(jnp.logical_and(step > 0, step < steps - 1))
             def _(lane=lane):
                 ring_copy(lane, step).start()
 
-            @pl.when(step < steps)
+            @pl.when(jnp.logical_and(step > 0, step < steps))
             def _(lane=lane):
                 sibling_copy(lane, step, core).start()
+
+    def one_step(step, carry):
+        middle = len(lanes) // 2
+        pass_on(step, range(middle))
+
+        @pl.when(jnp.logical_and(step > 0, step <= steps))
+        def _():
+            work(0, step - 1)
+
+        pass_on(step, range(middle, len(lanes)))
 
         @pl.when(step < steps)
         def _():
             for copy in taken(0, step):
                 copy.start()
 
-        @pl.when(step > 0)
+        @pl.when(jnp.logical_and(step > 0, step <= steps))
         def _():
             for lane in range(len(lanes)):
                 sibling_copy(lane, step - 1, 1 - core).wait_recv()
             for copy in taken(1, step - 1):
                 copy.start()
 
-        @pl.when(step < steps)
+        @pl.when(step > 1)
         def _():
-            work(0, step, step == 0)
-
-        @pl.when(step > 0)
-        def _():
-            work(1, step - 1, step == 1)
+            work(1, step - 2)
 
         return carry
 
-    lax.fori_loop(0, steps + 1, one_step, 0)
-    for slot in range(2):
-        for copy in given(slot, steps - 1):
-            copy.wait()
+    lax.fori_loop(0, steps + 2, one_step, 0)
+    for beside in range(2):
+        for step in (steps - 2, steps - 1):
+            for copy in given(beside, step):
+                copy.wait()
     for lane in range(len(lanes)):
         for step in range(steps):
             if step < steps - 1:
@@ -376,11 +388,11 @@
         + [jax.ShapeDtypeStruct(a.shape, a.dtype) for a in swaps],
         in_specs=[anywhere] * 2 + [vmem] * 3 + [anywhere] * len(swaps),
         out_specs=[anywhere] * 3 + [vmem] * 3 + [anywhere] * len(swaps),
-        scratch_shapes=[pltpu.VMEM((2, tokens, width), BF)] * 4
+        scratch_shapes=[pltpu.VMEM((4, tokens, width), BF)] * 4
         + [pltpu.SemaphoreType.DMA]
         + [pltpu.SemaphoreType.DMA((len(lanes), 2 * nz - 1))] * 2
         + [pltpu.SemaphoreType.DMA((len(lanes), 2 * nz))] * 2
-        + [pltpu.SemaphoreType.DMA((2, 2, 2))] * 2
+        + [pltpu.SemaphoreType.DMA((4, 2, 2))] * 2
         + [pltpu.SemaphoreType.DMA((2, max(len(swaps), 1)))],
         compiler_params=pltpu.CompilerParams(
             collective_id=collective_id, has_side_effects=True, vmem_limit_bytes=56 * MIB
@@ -396,12 +408,12 @@
     return c, x, core, {"ctx": (1 - x) * 2 + core}, {"ctx": x * 2 + 1 - core}
 
 
-def ctx_gather_kernel(nz, pieces, x_ref, t_ref, o_ref, u_ref, own_sem, send, recv, sib_send, sib_recv, *trade):
+def ctx_gather_kernel(nz, pieces, x_ref, t_ref, o_ref, u_ref, held, own_sem, send, recv, sib_send, sib_recv, *trade):
     c, x, core, across, sibling = ctx_neighbours()
     greet(trade_partners(nz))
     size = x_ref.shape[0] // pieces
     far = (1 - x) * 2 + core
-    local = pltpu.make_async_copy(x_ref, o_ref.at[c], own_sem)
+    local = pltpu.make_async_copy(x_ref, held, own_sem)
     first, beside = [], []
     for k in range(pieces):
         piece = pl.ds(k * size, size)
@@ -415,6 +427,9 @@
     kept, traded = trade_copies(nz, t_ref, u_ref, *trade)
     for copy in [kept] + traded:
         copy.start()
+    local.wait()
+    local = pltpu.make_async_copy(held, o_ref.at[c], own_sem)
+    local.start()
     for k in range(pieces):
         piece = pl.ds(k * size, size)
         first[k].wait_recv()
@@ -438,7 +453,7 @@
         ],
         in_specs=[pl.BlockSpec(memory_space=pl.ANY)] * 2,
         out_specs=[pl.BlockSpec(memory_space=pl.ANY)] * 2,
-        scratch_shapes=[pltpu.SemaphoreType.DMA]
+        scratch_shapes=[pltpu.VMEM(array.shape, array.dtype), pltpu.SemaphoreType.DMA]
         + [pltpu.SemaphoreType.DMA((pieces,))] * 2
         + [pltpu.SemaphoreType.DMA((pieces + 1,))] * 2
         + trade_semaphores(nz),
@@ -448,11 +463,9 @@
     )(array, trade)
 
 
-def ctx_scatter_kernel(
-    nz, pieces, x_ref, t_ref, o_ref, u_ref, mine, theirs, came, own_sem, sib_send, sib_recv, send, recv, *trade
-):
+def ctx_scatter_kernel(pieces, x_ref, o_ref, mine, theirs, came, own_sem, sib_send, sib_recv, send, recv):
     c, x, core, across, sibling = ctx_neighbours()
-    greet(trade_partners(nz))
+    greet((across, sibling))
     size = x_ref.shape[1] // pieces
     loads, shares, flying = {}, {}, []
     for turn in range(2):
@@ -471,9 +484,6 @@
             )
             loads[turn, k].start()
             shares[turn, k].start()
-    kept, traded = trade_copies(nz, t_ref, u_ref, *trade)
-    for copy in [kept] + traded:
-        copy.start()
     for turn in range(2):
         for k in range(pieces):
             loads[turn, k].wait()
@@ -499,40 +509,41 @@
         copy.wait_send()
     for copy in shares.values():
         copy.wait_send()
-    for copy in [kept] + traded:
-        copy.wait()
-
-
-def ctx_scatter(array, trade, collective_id, pieces=4):
-    nz = lax.axis_size("shard")
+
+
+def ctx_scatter(array, collective_id, pieces=4):
     rows, width = array.shape[1:]
     return pl.pallas_call(
-        functools.partial(ctx_scatter_kernel, nz, pieces),
-        out_shape=[jax.ShapeDtypeStruct((rows, width), F32), jax.ShapeDtypeStruct(trade.shape, trade.dtype)],
-        in_specs=[pl.BlockSpec(memory_space=pl.ANY)] * 2,
-        out_specs=[pl.BlockSpec(memory_space=pltpu.VMEM), pl.BlockSpec(memory_space=pl.ANY)],
+        functools.partial(ctx_scatter_kernel, pieces),
+        out_shape=jax.ShapeDtypeStruct((rows, width), F32),
+        in_specs=[pl.BlockSpec(memory_space=pl.ANY)],
+        out_specs=pl.BlockSpec(memory_space=pltpu.VMEM),
         scratch_shapes=[
             pltpu.VMEM((2, rows, width), BF),
             pltpu.VMEM((2, rows, width), BF),
             pltpu.VMEM((rows, width), BF),
         ]
         + [pltpu.SemaphoreType.DMA((2, pieces))] * 3
-        + [pltpu.SemaphoreType.DMA((pieces,))] * 2
-        + trade_semaphores(nz),
+        + [pltpu.SemaphoreType.DMA((pieces,))] * 2,
         compiler_params=pltpu.CompilerParams(
             collective_id=collective_id, has_side_effects=True, vmem_limit_bytes=32 * MIB
         ),
         cost_estimate=link_cost(array.size * array.dtype.itemsize, 120e9),
         name="ctx_scatter",
-    )(array, trade)
-
-
-def scatter_kernel(nz, count, lanes, *refs):
+    )(array)
+
+
+def scatter_kernel(nz, count, swaps, lanes, *refs):
+    swap_in, swap_out = refs[count : count + swaps], refs[2 * count + swaps : 2 * (count + swaps)]
+    swap_send, swap_recv = refs[-2:]
+    refs = refs[:count] + refs[count + swaps : 2 * count + swaps] + refs[2 * (count + swaps) : -2]
     ins, outs = refs[:count], refs[count : 2 * count]
     mine, theirs, came = (refs[(2 + k) * count : (3 + k) * count] for k in range(3))
     own_sem, sib_send, sib_recv, send, recv = refs[5 * count :]
     me, core, right, left, sibling = ring_neighbours(nz)
-    greet((right, left, sibling))
+    across = {"tp": 1 - lax.axis_index("tp")}
+    greet((right, left, sibling) + ((across,) if swaps else ()))
+    swapped = [remote(swap_in[i], swap_out[i], swap_send.at[i], swap_recv.at[i], across) for i in range(swaps)]
     steps = 2 * nz
 
     def block(place, which):
@@ -558,6 +569,8 @@
             )
             share.start()
             shares[lane, step] = share
+    for copy in swapped:
+        copy.start()
     flying = {}
     for step in range(steps):
         for lane, (i, towards, row, rows) in enumerate(lanes):
@@ -592,9 +605,11 @@
         copy.wait_send()
     for copy in shares.values():
         copy.wait_send()
-
-
-def ring_scatter(arrays, collective_id, pieces=2):
+    for copy in swapped:
+        copy.wait()
+
+
+def ring_scatter(arrays, collective_id, pieces=2, swaps=(), rate=190e9):
     nz = lax.axis_size("shard")
     shapes = [a.shape[1:] for a in arrays]
     lanes = ring_lanes(shapes, pieces)
@@ -603,19 +618,22 @@
         pltpu.VMEM((size,) + shape, BF) for size in (steps, steps, steps - 1) for shape in shapes
     ]
     return pl.pallas_call(
-        functools.partial(scatter_kernel, nz, count, lanes),
-        out_shape=[jax.ShapeDtypeStruct(shape, F32) for shape in shapes],
-        in_specs=[pl.BlockSpec(memory_space=pl.ANY)] * count,
-        out_specs=[pl.BlockSpec(memory_space=pltpu.VMEM)] * count,
+        functools.partial(scatter_kernel, nz, count, len(swaps), lanes),
+        out_shape=[jax.ShapeDtypeStruct(shape, F32) for shape in shapes]
+        + [jax.ShapeDtypeStruct(a.shape, a.dtype) for a in swaps],
+        in_specs=[pl.BlockSpec(memory_space=pl.ANY)] * (count + len(swaps)),
+        out_specs=[pl.BlockSpec(memory_space=pltpu.VMEM)] * count
+        + [pl.BlockSpec(memory_space=pl.ANY)] * len(swaps),
         scratch_shapes=buffers
         + [pltpu.SemaphoreType.DMA((len(lanes), steps))] * 3
-        + [pltpu.SemaphoreType.DMA((len(lanes), steps - 1))] * 2,
+        + [pltpu.SemaphoreType.DMA((len(lanes), steps - 1))] * 2
+        + [pltpu.SemaphoreType.DMA((max(len(swaps), 1),))] * 2,
         compiler_params=pltpu.CompilerParams(
             collective_id=collective_id, has_side_effects=True, vmem_limit_bytes=56 * MIB
         ),
-        cost_estimate=link_cost(sum(a.size * a.dtype.itemsize for a in arrays), 190e9),
+        cost_estimate=link_cost(sum(a.size * a.dtype.itemsize for a in arrays), rate),
         name="ring_scatter",
-    )(*arrays)
+    )(*arrays, *swaps)
 
 
 def turn(values, tables):
@@ -631,11 +649,6 @@
         jnp.concatenate([-sines, nothing] * 2, 1),
         jnp.concatenate([nothing, sines] * 2, 1),
     )
-
-
-def turn_back(values, tables):
-    cosines, sines = tables[0][:, : ROPE // 2], tables[2][:, ROPE // 2 : ROPE]
-    return rotate(values, -sines, cosines)
 
 
 def project_kernel(heads, x_ref, gain, kv_gain, w_ref, cosine, first, second, *outs):
@@ -694,9 +707,9 @@
     return jnp.concatenate([kv_ref[:, k * HEAD : k * HEAD + NOPE], rope], 1)
 
 
-def attend_kernel(scale, start, qn_ref, qr_ref, kv_ref, rope_ref, seg_q, seg_k, o_ref, l_ref):
+def attend_kernel(scale, qn_ref, qr_ref, kv_ref, rope_ref, seg_q, seg_k, o_ref, l_ref):
     rows, keys = qn_ref.shape[0], kv_ref.shape[0]
-    at_q = start[0] + lax.broadcasted_iota(jnp.int32, (rows, keys), 0)
+    at_q = lax.axis_index("ctx") * rows + lax.broadcasted_iota(jnp.int32, (rows, keys), 0)
     at_k = lax.broadcasted_iota(jnp.int32, (rows, keys), 1)
     visible = (seg_q[...] == seg_k[...]) & (at_k <= at_q)
     for k in range(2):
@@ -710,7 +723,7 @@
         l_ref[k] = peak + jnp.log(total)
 
 
-def attend(query, expanded, rope, seg_q, seg_k, start, scale):
+def attend(query, expanded, rope, seg_q, seg_k, scale):
     rows, keys = query.shape[0], expanded.shape[0]
     heads = query.shape[1] // (NOPE + ROPE)
     return pl.pallas_call(
@@ -719,37 +732,35 @@
             jax.ShapeDtypeStruct((rows, heads * V), BF),
             jax.ShapeDtypeStruct((heads, rows, 1), F32),
         ),
-        grid_spec=pltpu.PrefetchScalarGridSpec(
-            num_scalar_prefetch=1,
-            grid=(heads // 2,),
-            in_specs=[
-                pl.BlockSpec((rows, 2 * NOPE), lambda h, s: (0, h)),
-                pl.BlockSpec((rows, 2 * ROPE), lambda h, s: (0, heads + h)),
-                pl.BlockSpec((keys, 2 * HEAD), lambda h, s: (0, h)),
-                pl.BlockSpec((keys, 128), lambda h, s: (0, R // 128)),
-                pl.BlockSpec((rows, 1), lambda h, s: (0, 0)),
-                pl.BlockSpec((1, keys), lambda h, s: (0, 0)),
-            ],
-            out_specs=[
-                pl.BlockSpec((rows, 2 * V), lambda h, s: (0, h)),
-                pl.BlockSpec((2, rows, 1), lambda h, s: (h, 0, 0)),
-            ],
-        ),
+        grid=(heads // 2,),
+        in_specs=[
+            pl.BlockSpec((rows, 2 * NOPE), lambda h: (0, h)),
+            pl.BlockSpec((rows, 2 * ROPE), lambda h: (0, heads + h)),
+            pl.BlockSpec((keys, 2 * HEAD), lambda h: (0, h)),
+            pl.BlockSpec((keys, 128), lambda h: (0, R // 128)),
+            pl.BlockSpec((rows, 1), lambda h: (0, 0)),
+            pl.BlockSpec((1, keys), lambda h: (0, 0)),
+        ],
+        out_specs=[
+            pl.BlockSpec((rows, 2 * V), lambda h: (0, h)),
+            pl.BlockSpec((2, rows, 1), lambda h: (h, 0, 0)),
+        ],
         compiler_params=pltpu.CompilerParams(vmem_limit_bytes=60 * MIB),
         cost_estimate=pl.CostEstimate(
             flops=2 * heads * rows * keys * 384, bytes_accessed=12 * MIB, transcendentals=heads * rows * keys
         ),
         name="attend",
-    )(start, query, query, expanded, rope, seg_q, seg_k)
+    )(query, query, expanded, rope, seg_q, seg_k)
 
 
 def attend_back_kernel(
-    scale, start, qn_ref, qr_ref, kv_ref, rope_ref, g_ref, l_ref, seg_q, seg_k, cosine, first, second,
-    dqn_ref, dqr_ref, dkv_ref, dr_ref, dr_acc,
+    scale, qn_ref, qr_ref, kv_ref, rope_ref, g_ref, l_ref, seg_q, seg_k, expand_ref, cosine, first, second,
+    dqn_ref, dqr_ref, dkv_ref, dl_ref, comp_acc, rope_acc,
 ):
+    pair, last = pl.program_id(0), pl.num_programs(0) - 1
     rows, keys = qn_ref.shape[0], kv_ref.shape[0]
     at_k = lax.broadcasted_iota(jnp.int32, (keys, rows), 0)
-    at_q = start[0] + lax.broadcasted_iota(jnp.int32, (keys, rows), 1)
+    at_q = lax.axis_index("ctx") * rows + lax.broadcasted_iota(jnp.int32, (keys, rows), 1)
     visible = (seg_q[...] == seg_k[...]) & (at_k <= at_q)
     grad_ropes, grad_turned = [], None
     for k in range(2):
@@ -771,60 +782,120 @@
     dqr_ref[...] = turn(grad_turned, (cosine[...], -first[...], -second[...])).astype(BF)
     lane = lax.broadcasted_iota(jnp.int32, (keys, 128), 1)
     grad_rope = jnp.where(lane < ROPE, grad_ropes[0] + pltpu.roll(grad_ropes[1], ROPE, 1), 0.0)
-
-    @pl.when(pl.program_id(0) == 0)
+    grad_comp = mm_nt(dkv_ref[...], expand_ref[...])
+
+    @pl.when(pair == 0)
     def _():
-        dr_acc[...] = grad_rope
-
-    @pl.when(pl.program_id(0) > 0)
+        rope_acc[...] = grad_rope
+        comp_acc[...] = grad_comp
+
+    @pl.when(pair > 0)
     def _():
-        dr_acc[...] += grad_rope
-
-    @pl.when(pl.program_id(0) == pl.num_programs(0) - 1)
+        rope_acc[...] += grad_rope
+        comp_acc[...] += grad_comp
+
+    @pl.when(pair == last)
     def _():
-        dr_ref[...] = dr_acc[...].astype(BF)
-
-
-def attend_back(query, expanded, rope, grad, logs, seg_q, seg_k, start, tables, scale):
+        dl_ref[:, :R] = comp_acc[...].astype(BF)
+        dl_ref[:, R:] = rope_acc[...].astype(BF)
+
+
+def attend_back(query, expanded, rope, grad, logs, seg_q, seg_k, expand, tables, scale):
     rows, keys = query.shape[0], expanded.shape[0]
     heads = query.shape[1] // (NOPE + ROPE)
-    one = lambda shape: pl.BlockSpec(shape, lambda h, s: (0, 0))
+    one = lambda shape: pl.BlockSpec(shape, lambda h: (0, 0))
     return pl.pallas_call(
         functools.partial(attend_back_kernel, scale),
         out_shape=(
             jax.ShapeDtypeStruct((rows, heads * NOPE), BF),
             jax.ShapeDtypeStruct((rows, heads * ROPE), BF),
             jax.ShapeDtypeStruct((keys, heads * (NOPE + V)), BF),
-            jax.ShapeDtypeStruct((keys, 128), BF),
-        ),
-        grid_spec=pltpu.PrefetchScalarGridSpec(
-            num_scalar_prefetch=1,
-            grid=(heads // 2,),
-            in_specs=[
-                pl.BlockSpec((rows, 2 * NOPE), lambda h, s: (0, h)),
-                pl.BlockSpec((rows, 2 * ROPE), lambda h, s: (0, heads + h)),
-                pl.BlockSpec((keys, 2 * HEAD), lambda h, s: (0, h)),
-                pl.BlockSpec((keys, 128), lambda h, s: (0, R // 128)),
-                pl.BlockSpec((rows, 2 * V), lambda h, s: (0, h)),
-                pl.BlockSpec((2, 1, rows), lambda h, s: (h, 0, 0)),
-                one((1, rows)),
-                one((keys, 1)),
-            ]
-            + [one((rows, 128))] * 3,
-            out_specs=[
-                pl.BlockSpec((rows, 2 * NOPE), lambda h, s: (0, h)),
-                pl.BlockSpec((rows, 2 * ROPE), lambda h, s: (0, h)),
-                pl.BlockSpec((keys, 2 * HEAD), lambda h, s: (0, h)),
-                one((keys, 128)),
-            ],
-            scratch_shapes=[pltpu.VMEM((keys, 128), F32)],
-        ),
+            jax.ShapeDtypeStruct((keys, R + 128), BF),
+        ),
+        grid=(heads // 2,),
+        in_specs=[
+            pl.BlockSpec((rows, 2 * NOPE), lambda h: (0, h)),
+            pl.BlockSpec((rows, 2 * ROPE), lambda h: (0, heads + h)),
+            pl.BlockSpec((keys, 2 * HEAD), lambda h: (0, h)),
+            pl.BlockSpec((keys, 128), lambda h: (0, R // 128)),
+            pl.BlockSpec((rows, 2 * V), lambda h: (0, h)),
+            pl.BlockSpec((2, 1, rows), lambda h: (h, 0, 0)),
+            one((1, rows)),
+            one((keys, 1)),
+            pl.BlockSpec((R, 2 * HEAD), lambda h: (0, h)),
+        ]
+        + [one((rows, 128))] * 3,
+        out_specs=[
+            pl.BlockSpec((rows, 2 * NOPE), lambda h: (0, h)),
+            pl.BlockSpec((rows, 2 * ROPE), lambda h: (0, h)),
+            pl.BlockSpec((keys, 2 * HEAD), lambda h: (0, h)),
+            one((keys, R + 128)),
+        ],
+        scratch_shapes=[pltpu.VMEM((keys, R), F32), pltpu.VMEM((keys, 128), F32)],
         compiler_params=pltpu.CompilerParams(vmem_limit_bytes=60 * MIB),
         cost_estimate=pl.CostEstimate(
-            flops=2 * heads * rows * keys * 1024, bytes_accessed=24 * MIB, transcendentals=heads * rows * keys
+            flops=2 * heads * rows * keys * 1536, bytes_accessed=24 * MIB, transcendentals=heads * rows * keys
         ),
         name="attend_back",
-    )(start, query, query, expanded, rope, grad, logs, seg_q, seg_k, *tables)
+    )(query, query, expanded, rope, grad, logs, seg_q, seg_k, expand, *tables)
+
+
+def project_back_kernel(
+    gn_ref, gr_ref, gl_ref, compressed_ref, kv_ref, gain, cosine, first, second, w_ref, sum_ref, grad_ref, gain_ref
+):
+    upstream = gl_ref[:, :R]
+    compressed, inverse = compressed_ref[...], kv_ref[...]
+    scaled = upstream * gain[...]
+    mean = jnp.mean(scaled * compressed, -1, keepdims=True)
+    grad = inverse * scaled - compressed * (inverse * inverse * inverse * mean)
+    gains = jnp.sum(upstream * compressed * inverse, 0, keepdims=True)
+    nope, rope = gn_ref.shape[1], gr_ref.shape[1]
+    start = nope + rope
+    grad_ref[:, :nope] = gn_ref[...]
+    grad_ref[:, nope:start] = gr_ref[...]
+    grad_ref[:, start : start + R] = grad.astype(BF)
+    grad_ref[:, start + R :] = turn(gl_ref[:, R:], (cosine[...], -first[...], -second[...])).astype(BF)
+    sum_ref[...] = mm_nt(grad_ref[...], w_ref[...]).astype(BF)
+
+    @pl.when(pl.program_id(0) == 0)
+    def _():
+        gain_ref[...] = gains
+
+    @pl.when(pl.program_id(0) > 0)
+    def _():
+        gain_ref[...] += gains
+
+
+def project_back(grad_nope, grad_turned, grad_latent, compressed, inverse_kv, kv_gain, tables, weights):
+    rows, columns = grad_nope.shape[0], weights.shape[1]
+    width, tile = weights.shape[0], 128
+    by_row = lambda n: pl.BlockSpec((tile, n), lambda i: (i, 0))
+    whole = lambda a, **mode: pl.BlockSpec(a.shape, lambda i: (0, 0), **mode)
+    return pl.pallas_call(
+        project_back_kernel,
+        out_shape=(
+            jax.ShapeDtypeStruct((rows, width), BF),
+            jax.ShapeDtypeStruct((rows, columns), BF),
+            jax.ShapeDtypeStruct((1, R), F32),
+        ),
+        grid=(rows // tile,),
+        in_specs=[
+            by_row(grad_nope.shape[1]),
+            by_row(grad_turned.shape[1]),
+            by_row(R + 128),
+            by_row(R),
+            by_row(1),
+            whole(kv_gain),
+        ]
+        + [by_row(128)] * 3
+        + [whole(weights, pipeline_mode=pl.Buffered(1))],
+        out_specs=[by_row(width), by_row(columns), pl.BlockSpec((1, R), lambda i: (0, 0))],
+        compiler_params=pltpu.CompilerParams(vmem_limit_bytes=48 * MIB),
+        cost_estimate=pl.CostEstimate(
+            flops=2 * rows * width * columns, bytes_accessed=20 * MIB, transcendentals=0
+        ),
+        name="project_back",
+    )(grad_nope, grad_turned, grad_latent, compressed, inverse_kv, kv_gain, *tables, weights)
 
 
 TILE = 256
@@ -832,7 +903,7 @@
 
 def pack_kernel(pair_tile, pair_block, pair_first, pair_on, rank, share, x_ref, o_ref, w_ref, *, weighted):
     i = pl.program_id(0)
-    tokens = x_ref.shape[1]
+    tokens = rank.shape[2]
 
     @pl.when(pair_on[i] == 1)
     def _():
@@ -856,7 +927,7 @@
 
 
 def pack(pairs, rank, share, x, weighted):
-    blocks, tokens, width = x.shape
+    (blocks, _, tokens), width = rank.shape, x.shape[2]
     slots = blocks * tokens
     return pl.pallas_call(
         functools.partial(pack_kernel, weighted=weighted),
@@ -886,45 +957,53 @@
 
 
 def expert_kernel(parts, tiles, x_ref, g_ref, w_ref, *refs):
-    gates, ups, downs = (refs[k * parts : (k + 1) * parts] for k in range(3))
-    out_ref, gin_ref = refs[3 * parts : 3 * parts + 2]
-    hids, ggs, gus = (refs[3 * parts + 2 + k * parts : 3 * parts + 2 + (k + 1) * parts] for k in range(3))
+    given, (out_ref, gin_ref, hid, gg, gu, gate, up, down, sem) = refs[: 3 * parts], refs[3 * parts :]
+    size, room = given[0].shape[0], gate.shape[0] // parts
+
+    @pl.when(pl.program_id(0) == 0)
+    def _():
+        copies = [
+            pltpu.make_async_copy(given[k * parts + p], held.at[pl.ds(p * room, size)], sem.at[k, p])
+            for k, held in enumerate((gate, up, down))
+            for p in range(parts)
+        ]
+        for copy in copies:
+            copy.start()
+        if room > size:
+            for held in (gate, up, down):
+                for p in range(parts):
+                    held[pl.ds(p * room + size, room - size), :] = jnp.zeros((room - size, held.shape[1]), BF)
+        for copy in copies:
+            copy.wait()
 
     @pl.when(pl.program_id(0) < tiles[0])
     def _():
         x, g = x_ref[...], g_ref[...]
-        out = gin = None
-        for part in range(parts):
-            gate, up, down = gates[part][...], ups[part][...], downs[part][...]
-            a = mm_nt(x, gate)
-            b = mm_nt(x, up)
-            sig = jax.nn.sigmoid(a)
-            act = a * sig
-            hidden = (act * b).astype(BF)
-            hids[part][...] = hidden
-            grad_hidden = mm_nt(g, down)
-            grad_gate = (grad_hidden * b * (sig * (1.0 + a * (1.0 - sig)))).astype(BF)
-            grad_up = (grad_hidden * act).astype(BF)
-            ggs[part][...] = grad_gate
-            gus[part][...] = grad_up
-            o = mm(hidden, down)
-            gi = mm(grad_gate, gate) + mm(grad_up, up)
-            out = o if out is None else out + o
-            gin = gi if gin is None else gin + gi
-        out_ref[...] = (out * w_ref[...]).astype(BF)
-        gin_ref[...] = gin.astype(BF)
+        a = mm_nt(x, gate[...])
+        b = mm_nt(x, up[...])
+        grad_hidden = mm_nt(g, down[...])
+        sig = jax.nn.sigmoid(a)
+        act = a * sig
+        hidden = (act * b).astype(BF)
+        hid[...] = hidden
+        out_ref[...] = (mm(hidden, down[...]) * w_ref[...]).astype(BF)
+        grad_gate = (grad_hidden * b * (sig * (1.0 + a * (1.0 - sig)))).astype(BF)
+        grad_up = (grad_hidden * act).astype(BF)
+        gg[...] = grad_gate
+        gu[...] = grad_up
+        gin_ref[...] = (mm(grad_gate, gate[...]) + mm(grad_up, up[...])).astype(BF)
 
 
 def experts(tiles, x, g, w, gates, ups, downs):
     slots, width = x.shape
     parts, hidden = len(gates), gates[0].shape[0]
+    room = -(-hidden // 128) * 128
     row = lambda i, t: (jnp.minimum(i, t[0] - 1), 0)
-    whole = lambda i, t: (0, 0)
-    once = pl.Buffered(1)
-    results = pl.pallas_call(
+    anywhere = pl.BlockSpec(memory_space=pl.ANY)
+    return pl.pallas_call(
         functools.partial(expert_kernel, parts),
         out_shape=(jax.ShapeDtypeStruct((slots, width), BF),) * 2
-        + (jax.ShapeDtypeStruct((slots, hidden), BF),) * (3 * parts),
+        + (jax.ShapeDtypeStruct((slots, parts * room), BF),) * 3,
         grid_spec=pltpu.PrefetchScalarGridSpec(
             num_scalar_prefetch=1,
             grid=(slots // TILE,),
@@ -933,9 +1012,10 @@
                 pl.BlockSpec((TILE, width), row),
                 pl.BlockSpec((TILE, 1), row),
             ]
-            + [pl.BlockSpec((hidden, width), whole, pipeline_mode=once)] * (3 * parts),
+            + [anywhere] * (3 * parts),
             out_specs=[pl.BlockSpec((TILE, width), row)] * 2
-            + [pl.BlockSpec((TILE, hidden), row)] * (3 * parts),
+            + [pl.BlockSpec((TILE, parts * room), row)] * 3,
+            scratch_shapes=[pltpu.VMEM((parts * room, width), BF)] * 3 + [pltpu.SemaphoreType.DMA((3, parts))],
         ),
         compiler_params=pltpu.CompilerParams(vmem_limit_bytes=60 * MIB),
         cost_estimate=pl.CostEstimate(
@@ -943,17 +1023,16 @@
         ),
         name="experts",
     )(tiles, x, g, w, *gates, *ups, *downs)
-    kept = [results[2 + k * parts : 2 + (k + 1) * parts] for k in range(3)]
-    return results[0], results[1], kept
 
 
 def expert_sums(tiles, x_ref, g_ref, hid_ref, gg_ref, gu_ref, sums):
     @pl.when(pl.program_id(0) < tiles[0])
     def _():
         x, g = x_ref[...], g_ref[...]
-        sums[0][...] += mm_tn(gg_ref[...], x)
-        sums[1][...] += mm_tn(gu_ref[...], x)
-        sums[2][...] += mm_tn(hid_ref[...], g)
+        size = sums[0].shape[0]
+        sums[0][...] += mm_tn(gg_ref[:, :size], x)
+        sums[1][...] += mm_tn(gu_ref[:, :size], x)
+        sums[2][...] += mm_tn(hid_ref[:, :size], g)
 
 
 def expert_sums_kernel(tiles, x_ref, g_ref, hid_ref, gg_ref, gu_ref, *refs):
@@ -983,10 +1062,11 @@
     expert_sums(tiles, x_ref, g_ref, hid_ref, gg_ref, gu_ref, outs)
 
 
-def expert_grads(tiles, x, g, hid, gg, gu, starts=None):
+def expert_grads(tiles, x, g, hid, gg, gu, part, hidden, starts=None):
     slots, width = x.shape
-    hidden = hid.shape[1]
+    room = -(-hidden // 128) * 128
     row = lambda i, t: (jnp.minimum(i, t[0] - 1), 0)
+    column = lambda i, t: (jnp.minimum(i, t[0] - 1), part)
     whole = lambda i, t: (0, 0)
     once = pl.Buffered(1)
     kernel = expert_sums_kernel if starts is None else expert_totals_kernel
@@ -998,7 +1078,7 @@
             num_scalar_prefetch=1,
             grid=(slots // TILE,),
             in_specs=[pl.BlockSpec((TILE, width), row)] * 2
-            + [pl.BlockSpec((TILE, hidden), row)] * 3
+            + [pl.BlockSpec((TILE, room), column)] * 3
             + (held if starts is not None else []),
             out_specs=held,
             scratch_shapes=[pltpu.VMEM((hidden, width), F32)] * 3 if starts is None else [],
@@ -1081,7 +1161,7 @@
     last = jnp.where(counts > 0, (end - 1) // TILE, first)
     spans = last - first + 1
     after = jnp.sum(jnp.where(lower | jnp.eye(blocks, dtype=bool), spans[None, :], 0), 1)
-    size = 2 * blocks
+    size = blocks + blocks * tokens // TILE
     turn = jnp.arange(size)
     all_pairs = after[-1]
     on = turn < all_pairs
@@ -1105,24 +1185,25 @@
     return rank.astype(jnp.int32), pairs, tiles
 
 
-def other_half_sum(rows, product):
+def other_half_sum(rows, product, beside):
     parts, me = lax.axis_size("tp"), lax.axis_index("tp")
     size = rows.shape[0] // parts
     if parts != 2:
-        return lax.psum_scatter(product(rows).astype(BF), "tp", scatter_dimension=0, tiled=True).astype(F32)
+        summed = lax.psum_scatter(product(rows).astype(BF), "tp", scatter_dimension=0, tiled=True)
+        return summed.astype(F32), beside
     sent = product(lax.dynamic_slice_in_dim(rows, (1 - me) * size, size)).astype(BF)
-    came = lax.ppermute(sent, "tp", [(0, 1), (1, 0)])
-    return product(lax.dynamic_slice_in_dim(rows, me * size, size)) + came.astype(F32)
+    came, beside = lax.optimization_barrier((lax.ppermute(sent, "tp", [(0, 1), (1, 0)]), beside))
+    return product(lax.dynamic_slice_in_dim(rows, me * size, size)) + came.astype(F32), beside
 
 
 def swap_tp(v):
     return lax.ppermute(v, "tp", [(0, 1), (1, 0)])
 
 
-def join_tp(v):
+def join_tp(v, came=None):
     if lax.axis_size("tp") != 2:
         return lax.all_gather(v, "tp", axis=0, tiled=True)
-    came = swap_tp(v)
+    came = swap_tp(v) if came is None else came
     return jnp.where(lax.axis_index("tp") == 0, jnp.stack([v, came]), jnp.stack([came, v])).reshape(
         (2 * v.shape[0],) + v.shape[1:]
     )
@@ -1209,7 +1290,8 @@
     share = lax.dynamic_index_in_dim(share, me, 1, keepdims=False)
     rank, pairs, tiles = routing(share)
 
-    cot_all = lax.all_gather(together((own_half(cotangent), gains))[0], GROUP, axis=0, tiled=False)
+    cot_half = jnp.concatenate([own_half(cotangent), jnp.zeros((8, width), BF)], 0)
+    cot_all = lax.all_gather(together((cot_half, gains))[0], GROUP, axis=0, tiled=False)
     if parts == 2:
         up_other = swap_tp(together((up, gains))[0])
 
@@ -1223,27 +1305,26 @@
     all_latent = all_latent.reshape(ctx * tokens, -1)
     shared_own = jnp.swapaxes(shared_own, 0, 1).reshape(3 * piece, width)
     expanded = mm(all_latent[:, :R], expand_full).astype(BF)
-    begin = start.astype(jnp.int32)[None]
     if parts == 2:
         expanded, shared_own, up_other = together((expanded, shared_own, up_other))
         shared_parts = [shared_own, swap_tp(shared_own)]
     else:
         shared_parts = list(lax.all_gather(shared_own, "tp", axis=0, tiled=False))
-    attended, logs = attend(
-        query_low, expanded, all_latent, segments[:, None], all_segments[None, :], begin, scale
-    )
+    attended, logs = attend(query_low, expanded, all_latent, segments[:, None], all_segments[None, :], scale)
     attended, shared_parts = together((attended, shared_parts))
     shared = [
         jnp.concatenate([v[k * piece : (k + 1) * piece] for v in shared_parts], 0) for k in range(3)
     ]
-    middle = own_half(residual) + other_half_sum(attended, lambda rows: mm_nt(rows, output_full))
+    rank_row, share_row = rank[:, None, :], share[:, None, :]
+    packed_grads = pack(pairs, rank_row, share_row, cot_all, True)
+    attended_sum, (grad_rows, weights) = other_half_sum(
+        attended, lambda rows: mm_nt(rows, output_full), packed_grads
+    )
+    middle = own_half(residual) + attended_sum
     normed_two, inverse_two = norm_forward(middle, ffn_scale)
     ffn_low = normed_two.astype(BF)
 
-    rank_row, share_row = rank[:, None, :], share[:, None, :]
-    grad_rows, weights = pack(pairs, rank_row, share_row, cot_all, True)
     if parts == 2:
-        ffn_low, grad_rows = together((ffn_low, grad_rows))
         rows_all, shared_out, shared_gin, *shared_grads, down_other = gather_shared(
             ffn_low, cot_all, shared, 2, swaps=[down]
         )
@@ -1252,20 +1333,34 @@
         rows_all, shared_out, shared_gin, *shared_grads = gather_shared(ffn_low, cot_all, shared, 2)
         gates, ups, downs = (list(lax.all_gather(v, "tp", axis=0, tiled=False)) for v in (gate, up, down))
     rows_in, _ = pack(pairs, rank_row, share_row, rows_all, False)
-    expert_out, expert_gin, kept = experts(tiles, rows_in, grad_rows, weights, gates, ups, downs)
+
+    shared_back = [
+        jnp.concatenate([v[k * piece : (k + 1) * piece] for v in shared_grads], 0) for k in range(parts)
+    ]
+    if parts == 2:
+        shared_came = swap_tp(shared_back[1].astype(BF))
+        rows_in, shared_came = together((rows_in, shared_came))
+        shared_back = shared_back[0] + shared_came.astype(F32)
+    else:
+        shared_back = lax.psum_scatter(jnp.stack(shared_back).astype(BF), "tp", scatter_dimension=0, tiled=False)
+    shared_back = lax.all_gather(shared_back.astype(BF), GROUP, axis=0, tiled=False)
+    expert_out, expert_gin, *kept = experts(tiles, rows_in, grad_rows, weights, gates, ups, downs)
 
     grads_of = lambda which, *starts: expert_grads(
-        tiles, rows_in, grad_rows, *(k[which] for k in kept), *starts
+        tiles, rows_in, grad_rows, *kept, which, gate.shape[0], *starts
     )
     if parts == 2:
         expert_out, sent = together((expert_out, grads_of(1)))
         came = [swap_tp(v) for v in sent]
-    moe_part, grad_part = dense(pairs, rank[:, :, None], shared_out, shared_gin, expert_out, expert_gin)
+    moe_part, grad_part = dense(
+        pairs, rank[:, :, None], shared_out, shared_gin, expert_out, expert_gin
+    )
+    grad_part, shared_back = together((grad_part, shared_back))
+    shared_back = lax.dynamic_slice_in_dim(shared_back, me * depth, depth, 2)
     (grad_normed_two,) = ring_scatter([grad_part], 3)
     if parts == 2:
         grad_normed_two, came = together((grad_normed_two, came))
-        own_grads = grads_of(0, tuple(came))
-    else:
+    if parts != 2:
         sent = [grads_of(k) for k in range(parts)]
         own_grads = [
             lax.psum_scatter(jnp.stack(v), "tp", scatter_dimension=0, tiled=False).astype(F32) for v in zip(*sent)
@@ -1275,76 +1370,65 @@
     grad_mid_norm, ffn_gain_grad = norm_backward(middle, inverse_two, ffn_scale, grad_normed_two)
     grad_middle = grad_out + grad_mid_norm
     grad_middle_low = join_tp(grad_middle.astype(BF))
-    grad_middle_low, own_grads = together((grad_middle_low, own_grads))
+    moe_part = lax.optimization_barrier((moe_part, grad_normed_two))[0]
+    moe_total = lax.psum_scatter(
+        moe_part, GROUP, scatter_dimension=0, tiled=False
+    )
+
+    grad_attended = mm(grad_middle_low, output_full).astype(BF)
+    grad_nope, grad_turned, grad_kv, grad_latent = attend_back(
+        query_low, expanded, all_latent, grad_attended, jnp.swapaxes(logs, 1, 2),
+        segments[None, :], all_segments[:, None], expand_full, tables, scale,
+    )
+    grad_latent = ctx_scatter(grad_latent.reshape(ctx, tokens, -1), 6)
+    grad_normed_one, grad_first, kv_gain_grad = project_back(
+        grad_nope, grad_turned, grad_latent, compressed, inverse_kv, kv_scale[None], tables, first_full
+    )
+    if parts == 2:
+        grad_normed_came = swap_tp(lax.dynamic_slice_in_dim(grad_normed_one, (1 - part) * half, half))
+        (grad_middle_low, attended, all_latent, grad_kv, came), grad_normed_one = together(
+            ((grad_middle_low, attended, all_latent, grad_kv, came), grad_normed_one)
+        )
+        own_grads, grad_normed_came = together((grads_of(0, tuple(came)), grad_normed_came))
+        grad_normed_one = own_half(grad_normed_one).astype(F32) + grad_normed_came.astype(F32)
+    else:
+        grad_normed_one = lax.psum_scatter(grad_normed_one, "tp", scatter_dimension=0, tiled=True).astype(F32)
     gate_grad, up_grad, down_grad = (
         jnp.swapaxes(own_grads[0], 0, 1)[None], jnp.swapaxes(own_grads[1], 0, 1)[None], own_grads[2][None]
     )
-    shared_back = [
-        jnp.concatenate([v[k * piece : (k + 1) * piece] for v in shared_grads], 0) for k in range(parts)
-    ]
-    shared_back, grad_middle_low = together((shared_back, grad_middle_low))
-    if parts == 2:
-        shared_back = (shared_back[0], swap_tp(shared_back[1].astype(BF)))
-    else:
-        shared_back = lax.psum_scatter(jnp.stack(shared_back).astype(BF), "tp", scatter_dimension=0, tiled=False)
-
-    moe_part = lax.optimization_barrier((moe_part, grad_normed_two))[0]
-    moe_total = lax.psum_scatter(
-        moe_part.reshape(group * half, width), GROUP, scatter_dimension=0, tiled=True
-    )
-
-    grad_attended = mm(grad_middle_low, output_full).astype(BF)
-    grad_nope, grad_turned, grad_kv, grad_rope = attend_back(
-        query_low, expanded, all_latent, grad_attended, jnp.swapaxes(logs, 1, 2),
-        segments[None, :], all_segments[:, None], begin, tables, scale,
-    )
-    shared_back, grad_kv = together((shared_back, grad_kv))
-    if parts == 2:
-        shared_back = shared_back[0] + shared_back[1].astype(F32)
-    shared_back = jnp.swapaxes(shared_back.astype(BF).reshape(3 * piece, group, depth), 0, 1)
+    first_grad = mm_tn(attn_low, grad_first).astype(BF)
     output_grad = mm_tn(grad_middle_low, attended).astype(BF)
-    grad_query = jnp.concatenate([grad_nope, grad_turned], 1)
-    grad_comp = mm_nt(grad_kv, expand_full)
-    grad_comp = jnp.concatenate([grad_comp.astype(BF), grad_rope], 1)
-    grad_comp, shared_back = ctx_scatter(grad_comp.reshape(ctx, tokens, -1), shared_back, 6)
     expand_grad = mm_tn(all_latent[:, :R], grad_kv).astype(BF)
-    query_grad = mm_tn(attn_low, grad_query).astype(BF)
-    grad_compressed, kv_gain_grad = norm_backward(compressed, inverse_kv, kv_scale, grad_comp[:, :R])
-    grad_latent = jnp.concatenate(
-        [grad_compressed, turn_back(grad_comp[:, R : R + ROPE], tables)], -1
-    ).astype(BF)
-    latent_grad = mm_tn(attn_low, grad_latent).astype(BF)
-    grad_first = jnp.concatenate([grad_query, grad_latent, jnp.zeros((tokens, 128 - ROPE), BF)], 1)
-    grad_normed_one = other_half_sum(grad_first, lambda rows: mm_nt(rows, first_full))
     grad_in_norm, attn_gain_grad = norm_backward(
         own_half(residual), own_half(inverse_one), attn_scale, grad_normed_one
     )
-    grad_inputs = join_tp((grad_middle + grad_in_norm).astype(BF))
-
-    moe_total, attn_gain_grad = together((moe_total, attn_gain_grad))
-    result = join_tp((middle + moe_total.astype(F32)).astype(BF))
+    grad_inputs = (grad_middle + grad_in_norm).astype(BF)
 
     gain_grads = jnp.concatenate(
-        [v.reshape(group, -1) for v in (attn_gain_grad, kv_gain_grad, ffn_gain_grad)], 1
+        [v.reshape(group, -1) for v in (attn_gain_grad, kv_gain_grad[0], ffn_gain_grad)], 1
     ).astype(BF)
     tail = jnp.zeros((group, 16, 384), BF).at[:, 0, : gain_grads.shape[1]].set(gain_grads)
-    output_own, expand_own, query_own, latent_own, gains_own = ring_scatter(
+    moe_total, tail = together((moe_total, tail))
+    result = (middle + moe_total.astype(F32)).astype(BF)
+    first_own, output_own, expand_own, gains_own, *came = ring_scatter(
         [
+            first_grad.reshape(group, -1, first_grad.shape[1]),
             output_grad.reshape(group, -1, output_grad.shape[1]),
             expand_grad.reshape(group, -1, expand_grad.shape[1]),
-            query_grad.reshape(group, -1, query_width),
-            latent_grad.reshape(group, -1, latent_grad.shape[1]),
             tail,
         ],
         4,
         pieces=1,
-    )
+        swaps=[grad_inputs, result] if parts == 2 else [],
+    )
+    grad_inputs, result = join_tp(grad_inputs, *came[:1]), join_tp(result, *came[1:])
     output_own = jnp.swapaxes(output_own, 0, 1)
     back = [shared_back[:, k * piece : (k + 1) * piece].reshape(-1, depth).astype(F32) for k in range(3)]
     sgate_grad, sup_grad, sdown_grad = jnp.swapaxes(back[0], 0, 1), jnp.swapaxes(back[1], 0, 1), back[2]
-    nopes = query_own[:, : heads * NOPE].reshape(-1, heads, NOPE)
-    query_own = jnp.concatenate([nopes, query_own[:, heads * NOPE :].reshape(-1, heads, ROPE)], -1)
+    nopes = first_own[:, : heads * NOPE].reshape(-1, heads, NOPE)
+    query_own = jnp.concatenate([nopes, first_own[:, heads * NOPE : query_width].reshape(-1, heads, ROPE)], -1)
     query_own = query_own.reshape(-1, query_width)
+    latent_own = first_own[:, query_width : query_width + R + ROPE]
     if parts == 2:
         small = jnp.concatenate([latent_own.reshape(-1, 128), gains_own[:8].reshape(-1, 128)], 0)
         small = small + swap_tp(small)

time: 1120 us -> 993 us (0.89)
  Pallas kernels: 850 us -> 793 us
  waiting for transfers between devices: 70.6 us -> 29.1 us
  matrix products: 61.7 us -> 44.8 us
    pallas_call x1, Pallas kernels: 119 us -> 63.5 us  [experts(): pl.pallas_call(functools.partial(expert_kernel, parts), out_shape=(jax.Sh...]
    pallas_call x3 -> x4, Pallas kernels: 240 us -> 281 us  [the longest x2 242 us: ring_scatter(): pl.pallas_call(functools.partial(scatter_kernel, nz, count, len(swaps), l...]
    ppermute x2 -> x1, waiting for transfers between devices: 35.6 us -> 0.01 us  [other_half_sum(): lax.ppermute(sent, 'tp', [(0, 1), (1, 0)])]
    pallas_call x1, Pallas kernels: 129 us -> 100 us  [gather_shared(): pl.pallas_call(functools.partial(gather_shared_kernel, nz, len(swaps), la...]
    pallas_call x2, Pallas kernels: 69 us -> 47.1 us  [expert_grads(): pl.pallas_call(kernel, out_shape=(jax.ShapeDtypeStruct((hidden, width), B...]
    dot_general x5 -> x2, matrix products: 25.1 us -> 8.27 us  [mm_nt(): lax.dot_general(a, b, (((1,), (1,)), ((), ())), preferred_element_type=F32)]
    pallas_call x1, Pallas kernels: 35.7 us -> 47.7 us  [ctx_gather(): pl.pallas_call(functools.partial(ctx_gather_kernel, nz, pieces), out_shap...]
    ppermute x10 -> x9, waiting for transfers between devices: 25.2 us -> 19.1 us  [swap_tp(): return lax.ppermute(v, 'tp', [(0, 1), (1, 0)])]
  transfers between devices with their start and end apart: 14 -> 13, of which waited for: 7 -> 4; matrix products, arithmetic and copies ran while one was open for 13% -> 10% of each run, Pallas kernels for 38% -> 52%
where the time goes in v2:
time: 993 us; the launch traced here: 986 us
  Pallas kernels  793 us (80%)
  local copies, waits for them, and re-layouts  48 us (5%)
  other arithmetic  44.8 us (5%)
  matrix products  44.8 us (5%)
  waiting for transfers between devices  29.1 us (3%)
  between operations  16.3 us (2%)
    pallas_call x2, Pallas kernels, ring_scatter(): pl.pallas_call(functools.partial(scatter_kernel, nz, count, len(swaps), l...  242 us
    pallas_call x1, Pallas kernels, gather_shared(): pl.pallas_call(functools.partial(gather_shared_kernel, nz, len(swaps), la...  100 us
    pallas_call x1, Pallas kernels, ring_gather(): pl.pallas_call(functools.partial(gather_kernel, nz, count, len(swaps), la...  90.5 us
    pallas_call x1, Pallas kernels, experts(): pl.pallas_call(functools.partial(expert_kernel, parts), out_shape=(jax.Sh...  63.5 us
    pallas_call x1, Pallas kernels, ctx_gather(): pl.pallas_call(functools.partial(ctx_gather_kernel, nz, pieces), out_shap...  47.7 us
    pallas_call x2, Pallas kernels, expert_grads(): pl.pallas_call(kernel, out_shape=(jax.ShapeDtypeStruct((hidden, width), B...  47.1 us
    pallas_call x2, Pallas kernels, pack(): pl.pallas_call(functools.partial(pack_kernel, weighted=weighted), out_sha...  46.8 us
    pallas_call x1, Pallas kernels, attend_back(): pl.pallas_call(functools.partial(attend_back_kernel, scale), out_shape=(j...  40.4 us
  transfers between devices with their start and end apart: 13, of which 4 were waited for; matrix products, arithmetic and copies ran while one was open for 10% of the time, Pallas kernels for 52%

profile of v2, /device:TPU:0, one launch (start us, length us, event | category | flops | bytes accessed | tf_op | source)
XLA Modules:
  0.0 985.7 jit_solution(11200753771728520644)
XLA Ops:
  7.3 1.4 copy.92
  14.2 90.5 %ring_gather.1 = (bf16[16,128,2176]{2,1,0:T(8,128)(2,1)}, bf16[16,128,1024]{2,1,0:T(8,128)(2,1)}, bf16[16,32,2048]{2,1,0:T(8,128)(2,1)}, bf16[16,16,384]{2,1,0:T...) custom-call(bf16[128,2176]{1,0:T(8,128)(2,1)} %concatenate.68.refs_0_, ...), custom_call_target="tpu_custom_call" | custom-call | flops 76677120000 | bytes 32374784 | tf_op jit(solution)/shard_map/ring_gather/pallas_call | solution.py:209
  104.8 1.6 collective-permute-start
  114.8 1.5 slice_convert_fusion.4
  116.2 11.5 %project.1 = (bf16[512,2048]{1,0:T(8,128)(2,1)}, bf16[512,1536]{1,0:T(8,128)(2,1)S(1)}, bf16[512,640]{1,0:T(8,128)(2,1)S(1)}, f32[512,512]{1,0:T(8,128)S(1)}, f3...) custom-call(bf16[512,2048]{1,0:T(8,128)(2,1)} %x_ref.1, f32[1,2048]{1,0:T(1,128)S(1)} %get-tuple-element.310.gain, ...), custom_call_target="tpu_custom_call" | custom-call | flops 4563402752 | bytes 20971520 | tf_op jit(solution)/shard_map/project/pallas_call | solution.py:682
  127.7 1.2 copy-done.14
  129.7 47.7 %ctx_gather.1 = (bf16[4,512,640]{2,1,0:T(8,128)(2,1)}, bf16[16,264,128]{2,1,0:T(8,128)(2,1)}) custom-call(bf16[512,640]{1,0:T(8,128)(2,1)} %copy-done.17, bf16[16,264,128]{2,1,0:T(8,128)(2,1)} %pad_maximum_fusion.t_ref), custom_call_target="tpu_custom_call" | custom-call | flops 19660800000 | bytes 1310720 | tf_op jit(solution)/shard_map/ctx_gather/pallas_call | solution.py:448
  177.4 1.5 copy_bitcast_fusion
  179.4 8.4 convolution_convert_fusion.1.kv_ref
  190.6 24.5 %attend.1 = (bf16[512,1024]{1,0:T(8,128)(2,1)}, f32[8,512,1]{2,1,0:T(8,128)}) custom-call(bf16[512,1536]{1,0:T(8,128)(2,1)} %copy-done.14, bf16[512,1536]{1,0:T(8,128)(2,1)} %copy-done.14, bf16[2048,2048]{1,0:T(8,128)(2,1)} %convolution_convert_fusion.1.kv_ref, bf16[2048,640]{1,0:T(8,128)(2,1)} %bitcast.167, s32[512,1]{1,0:T(8,128)} %copy.100.seg_q, ...), custom_call_target="tpu_custom_call" | custom-call | flops 6442450944 | bytes 12582912 | tf_op jit(solution)/shard_map/attend/pallas_call | solution.py:729
  215.2 4.7 convolution_convert_fusion.4
  219.9 1.5 collective-permute-start.2
  221.4 1.4 fusion.34
  225.5 23.8 %pack.2 = (bf16[4096,2048]{1,0:T(8,128)(2,1)}, f32[4096,1]{1,0:T(8,128)S(1)}) custom-call(s32[32]{0:T(128)S(1)} %add_subtract_fusion.pair_tile, s32[32]{0:T(128)S(1)} %convert_reduce_fusion.1.pair_block, s32[32]{0:T(128)S(1)} %get-tuple-element.324.pair_first, s32[32]{0:T(128)S(1)} %get-tuple-element.325.pair_on, s32[16,1,256]{2,1,0:T(1,128)S(1)} %broadcast_in_dim.139.rank, ...), custom_call_target="tpu_custom_call" | custom-call | flops 6442450944 | bytes 29360128 | tf_op jit(solution)/shard_map/pack/pallas_call | solution.py:932
  249.3 3.6 multiply_reduce_fusion.2
  254.2 1.2 multiply_convert_fusion.row_ref
  255.4 100.1 %gather_shared.1 = (bf16[16,256,2048]{2,1,0:T(8,128)(2,1)}, bf16[16,256,2048]{2,1,0:T(8,128)(2,1)}, bf16[16,256,2048]{2,1,0:T(8,128)(2,1)}, f32[176,2048]{1,0:T(...) custom-call(bf16[256,2048]{1,0:T(8,128)(2,1)} %multiply_convert_fusion.row_ref, ...), custom_call_target="tpu_custom_call" | custom-call | flops 79471026176 | bytes 33554432 | tf_op jit(solution)/shard_map/gather_shared/pallas_call | solution.py:384
  355.5 1.3 slice.223
  356.8 1.1 slice.224
  358.0 1.3 slice.225
  359.3 1.2 collective-permute-start.3
  360.8 23.0 %pack.3 = (bf16[4096,2048]{1,0:T(8,128)(2,1)}, f32[4096,1]{1,0:T(8,128)}) custom-call(s32[32]{0:T(128)S(1)} %add_subtract_fusion.pair_tile, s32[32]{0:T(128)S(1)} %convert_reduce_fusion.1.pair_block, s32[32]{0:T(128)S(1)} %get-tuple-element.324.pair_first, s32[32]{0:T(128)S(1)} %get-tuple-element.325.pair_on, s32[16,1,256]{2,1,0:T(1,128)S(1)} %broadcast_in_dim.139.rank, ...), custom_call_target="tpu_custom_call" | custom-call | flops 6442450944 | bytes 29360128 | tf_op jit(solution)/shard_map/pack/pallas_call | solution.py:932
  383.8 1.5 collective-permute-done.3
  385.3 1.4 fusion
  387.9 2.0 copy.101.rank
  389.9 1.2 and_convert_fusion.1.pair_last
  391.1 1.2 and_convert_fusion
  392.3 63.5 %experts.1 = (bf16[4096,2048]{1,0:T(8,128)(2,1)}, bf16[4096,2048]{1,0:T(8,128)(2,1)}, bf16[4096,1536]{1,0:T(8,128)(2,1)}, bf16[4096,1536]{1,0:T(8,128)(2,1)}, bf16[4096,1536]{1,0:T(8,128)(2,1)}) custom-call(s32[1]{0:T(128)} %bitcast.29.tiles, bf16[4096,2048]{1,0:T(8,128)(2,1)} %get-tuple-element.158.x_ref, bf16[4096,2048]{1,0:T(8,128)(2,1)} %get-tuple-element.159.g_ref, ...), custom_call_target="tpu_custom_call" | custom-call | flops 88583700480 | bytes 104857600 | tf_op jit(solution)/shard_map/experts/pallas_call | solution.py:1003
  455.8 21.1 %expert_grads.2 = (bf16[704,2048]{1,0:T(8,128)(2,1)}, bf16[704,2048]{1,0:T(8,128)(2,1)}, bf16[704,2048]{1,0:T(8,128)(2,1)}) custom-call(s32[1]{0:T(128)} %bitcast.29.tiles, bf16[4096,2048]{1,0:T(8,128)(2,1)} %get-tuple-element.158.x_ref, bf16[4096,2048]{1,0:T(8,128)(2,1)} %get-tuple-element.159.g_ref, bf16[4096,1536]{1,0:T(8,128)(2,1)} %get-tuple-element.165.hid_ref, ...), custom_call_target="tpu_custom_call" | custom-call | flops 22145925120 | bytes 41943040 | tf_op jit(solution)/shard_map/expert_grads/pallas_call | solution.py:1074
  477.0 1.2 collective-permute-start.4
  479.0 1.2 collective-permute-start.6
  480.2 40.1 %dense.1 = (bf16[16,256,2048]{2,1,0:T(8,128)(2,1)}, bf16[16,256,2048]{2,1,0:T(8,128)(2,1)}) custom-call(s32[32]{0:T(128)} %copy-done.9, s32[32]{0:T(128)} %copy-done.8, s32[32]{0:T(128)} %get-tuple-element.320.pair_first, s32[32]{0:T(128)} %and_convert_fusion.1.pair_last, s32[32]{0:T(128)} %get-tuple-element.319.pair_real, s32[16,256,1]{2,1,0:T(8,128)} %copy.101.rank, ...), custom_call_target="tpu_custom_call" | custom-call | flops 13958643712 | bytes 94371840 | tf_op jit(solution)/shard_map/dense/pallas_call | solution.py:1122
  520.3 156.3 %ring_scatter.2 = f32[256,2048]{1,0:T(8,128)} custom-call(bf16[16,256,2048]{2,1,0:T(8,128)(2,1)} %get-tuple-element.176.refs_0_), custom_call_target="tpu_custom_call" | custom-call | flops 79471026176 | bytes 33554432 | tf_op jit(solution)/shard_map/ring_scatter/pallas_call | solution.py:620
  677.4 1.3 copy.103.seg_k
  678.9 2.3 reduce.6
  681.9 2.3 multiply_reduce_fusion
  684.7 2.3 fusion.32
  687.2 2.2 constant_dynamic-slice_fusion.2
  690.4 2.2 copy.112
  692.6 1.9 convert_bitcast_fusion
  694.5 2.2 copy.113
  696.7 1.9 bitcast_convert_fusion.1
  698.6 13.9 %collective-permute-done.7 = bf16[256,2048]{1,0:T(8,128)(2,1)} collective-permute-done((bf16[256,2048]{1,0:T(8,128)(2,1)}, bf16[256,2048]{1,0:T(8,128)(2,1)}, u32[]{:S(2)}, u32[]{:S(2)}) %collective-permute-start.7) | collective-permute-done | bytes 1048608 | tf_op jit(solution)/shard_map/ppermute | solution.py:1200
  712.5 3.5 maximum_select_fusion
  716.0 2.3 copy-done.56
  718.3 3.3 convolution_convert_fusion.5.g_ref
  721.6 40.4 %attend_back.1 = (bf16[512,1024]{1,0:T(8,128)(2,1)}, bf16[512,512]{1,0:T(8,128)(2,1)}, bf16[2048,2048]{1,0:T(8,128)(2,1)}, bf16[2048,640]{1,0:T(8,128)(2,1)}) custom-call(bf16[512,1536]{1,0:T(8,128)(2,1)} %copy-done.14, bf16[512,1536]{1,0:T(8,128)(2,1)} %copy-done.14, bf16[2048,2048]{1,0:T(8,128)(2,1)} %convolution_convert_fusion.1.kv_ref, ...), custom_call_target="tpu_custom_call" | custom-call | flops 25769803776 | bytes 25165824 | tf_op jit(solution)/shard_map/attend_back/pallas_call | solution.py:807
  762.1 1.7 copy-done.12
  763.8 21.7 %ctx_scatter.1.gl_ref = f32[512,640]{1,0:T(8,128)S(1)} custom-call(bf16[4,512,640]{2,1,0:T(8,128)(2,1)S(1)} %bitcast.112), custom_call_target="tpu_custom_call" | custom-call | flops 19660800000 | bytes 5242880 | tf_op jit(solution)/shard_map/ctx_scatter/pallas_call | solution.py:516
  785.6 16.8 %project_back.1 = (bf16[512,2048]{1,0:T(8,128)(2,1)}, bf16[512,2176]{1,0:T(8,128)(2,1)}, f32[1,512]{1,0:T(1,128)S(1)}) custom-call(bf16[512,1024]{1,0:T(8,128)(2,1)S(1)} %copy-done.13, bf16[512,512]{1,0:T(8,128)(2,1)S(1)} %copy-done.15, f32[512,640]{1,0:T(8,128)S(1)} %ctx_scatter.1.gl_ref, f32[512,512]{1,0:T(8,128)S(1)} %get-tuple-element.190.compressed_ref, ...), custom_call_target="tpu_custom_call" | custom-call | flops 4563402752 | bytes 20971520 | tf_op jit(solution)/shard_map/project_back/pallas_call | solution.py:874
  802.5 2.5 constant_dynamic-slice_fusion.3
  805.0 1.5 collective-permute-start.8
  806.4 5.7 convolution_convert_fusion.2
  812.1 9.2 convolution_convert_fusion.3
  821.3 25.9 %expert_grads.3 = (f32[704,2048]{1,0:T(8,128)}, f32[704,2048]{1,0:T(8,128)}, f32[704,2048]{1,0:T(8,128)}) custom-call(s32[1]{0:T(128)} %bitcast.29.tiles, bf16[4096,2048]{1,0:T(8,128)(2,1)} %get-tuple-element.158.x_ref, bf16[4096,2048]{1,0:T(8,128)(2,1)} %get-tuple-element.159.g_ref, bf16[4096,1536]{1,0:T(8,128)(2,1)} %get-tuple-element.165.hid_ref, ...), custom_call_target="tpu_custom_call" | custom-call | flops 22145925120 | bytes 41943040 | tf_op jit(solution)/shard_map/expert_grads/pallas_call | solution.py:1074
  847.2 9.8 convolution_convert_fusion
  858.6 1.8 fusion.7.refs_4_
  860.4 10.0 %reduce-scatter.2.cloned.1.call-done = bf16[1,256,2048]{2,1,0:T(8,128)(2,1)} async-done(((bf16[16,256,2048]{2,1,0:T(8,128)(2,1)}), bf16[1,256,2048]{2,1,0:T(8,128)(2,1)}) %reduce-scatter.2.cloned.1.call-update) | async-done | bytes 1048592 | tf_op jit(solution)/shard_map/reduce_scatter | solution.py:1374
  870.4 2.5 add_convert_fusion.refs_5_
  872.8 85.8 %ring_scatter.3 = (f32[128,2176]{1,0:T(8,128)}, f32[128,1024]{1,0:T(8,128)}, f32[32,2048]{1,0:T(8,128)}, f32[16,384]{1,0:T(8,128)}, bf16[256,2048]{1,0:T(8,128)(2,1)}, /*index=5*/bf16[256,2048]{1,0:T(8,128)(2,1)}) custom-call(bf16[16,128,2176]{2,1,0:T(8,128)(2,1)} %bitcast.158, bf16[16,128,1024]{2,1,0:T(8,128)(2,1)} %bitcast.165, ...), custom_call_target="tpu_custom_call" | custom-call | flops 72951914496 | bytes 30801920 | tf_op jit(solution)/shard_map/ring_scatter/pallas_call | solution.py:620
  962.2 2.7 bitcast_convert_fusion
  965.6 1.1 copy.109
  967.7 3.2 maximum_select_fusion.1
  970.9 3.7 collective-permute-done.9
  (224 shorter events, 37.3 us)
Async XLA Ops:
  7.2 3.0 copy-start
  7.2 2.0 copy-start.39
  7.2 2.9 copy-start.52
  7.2 2.9 copy-start.53
  7.2 2.9 copy-start.54
  7.2 3.0 copy-start.51
  7.3 3.0 copy-start.25
  7.3 218.2 %all-gather.5.cloned.1.call-start = ((), (), s32[]{:S(2)}) async-start(), calls=%async_computation.2 | async-start | bytes 18382848 | tf_op jit(solution)/shard_map/all_gather | solution.py:1294
  10.3 3.3 copy-start.48
  14.2 95.2 %copy-start.36 = (bf16[128,1408]{1,0:T(8,128)(2,1)S(1)}, bf16[128,1408]{1,0:T(8,128)(2,1)}, u32[]{:S(2)}) copy-start(bf16[128,1408]{1,0:T(8,128)(2,1)} %param.35) | copy-start | bytes 1081348
  104.7 4.9 copy-start.37
  104.8 415.5 %all-gather.7.cloned.1.call-start = ((), (), s32[]{:S(2)}) async-start(), calls=%async_computation.3 | async-start | bytes 18382848 | tf_op jit(solution)/shard_map/all_gather | solution.py:1346
  104.8 83.0 %collective-permute-start = (bf16[704,2048]{1,0:T(8,128)(2,1)}, bf16[704,2048]{1,0:T(8,128)(2,1)}, u32[]{:S(2)}, u32[]{:S(2)}) collective-permute-start(bf16[704,2048]{1,0:T(8,128)(2,1)} %bitcast.154), channel_id=1, source_target_pairs={{0,1},{1,0},{2,3},{3,2},{4,5},{5,4},{6,7},{7,6},{8,9},{9,8},{10,11... | collective-permute-start | bytes 8650760 | tf_op jit(solution)/shard_map/ppermute | solution.py:1200
  109.4 6.8 copy-start.10
  109.4 4.2 copy-start.38
  111.7 279.4 %copy-start.8 = (s32[32]{0:T(128)}, s32[32]{0:T(128)S(1)}, u32[]{:S(2)}) copy-start(s32[32]{0:T(128)S(1)} %convert_reduce_fusion.1.pair_block) | copy-start | bytes 388
  113.0 14.7 %copy-start.6 = (f32[512,128]{1,0:T(8,128)}, f32[512,128]{1,0:T(8,128)S(1)}, u32[]{:S(2)}) copy-start(f32[512,128]{1,0:T(8,128)S(1)} %pad_maximum_fusion.6.cosine) | copy-start | bytes 786436
  113.5 14.2 %copy-start.2 = (f32[512,128]{1,0:T(8,128)}, f32[512,128]{1,0:T(8,128)S(1)}, u32[]{:S(2)}) copy-start(f32[512,128]{1,0:T(8,128)S(1)} %get-tuple-element.307.second) | copy-start | bytes 786436
  113.6 14.2 %copy-start.4 = (f32[512,128]{1,0:T(8,128)}, f32[512,128]{1,0:T(8,128)S(1)}, u32[]{:S(2)}) copy-start(f32[512,128]{1,0:T(8,128)S(1)} %get-tuple-element.308.first) | copy-start | bytes 786436
  116.2 137.3 %copy-start.42 = (f32[16,1,128]{2,1,0:T(1,128)}, f32[16,1,128]{2,1,0:T(1,128)S(1)}, u32[]{:S(2)}) copy-start(f32[16,1,128]{2,1,0:T(1,128)S(1)} %get-tuple-element.311) | copy-start | bytes 24580
  177.4 2.0 copy-start.58
  187.9 27.3 %collective-permute-start.1 = (bf16[264,2048]{1,0:T(8,128)(2,1)S(1)}, bf16[264,2048]{1,0:T(8,128)(2,1)}, u32[]{:S(2)}, u32[]{:S(2)}) collective-permute-start(bf16[264,2048]{1,0:T(8,128)(2,1)S(1)} %copy_bitcast_fusion), channel_id=1, source_target_pairs={{0,1},{1,0},{2,3},{3,2},{4,5},{5,4},{6,7},{7,6},{8,9},{9,8},{10,11... | collective-permute-start | bytes 3244040 | tf_op jit(solution)/shard_map/ppermute | solution.py:1200
  189.9 170.9 %copy-start.9 = (s32[32]{0:T(128)}, s32[32]{0:T(128)S(1)}, u32[]{:S(2)}) copy-start(s32[32]{0:T(128)S(1)} %add_subtract_fusion.pair_tile) | copy-start | bytes 388
  219.9 29.4 %collective-permute-start.2 = (bf16[256,2048]{1,0:T(8,128)(2,1)}, bf16[256,2048]{1,0:T(8,128)(2,1)}, u32[]{:S(2)}, u32[]{:S(2)}) collective-permute-start(bf16[256,2048]{1,0:T(8,128)(2,1)} %convolution_convert_fusion.4), channel_id=1, source_target_pairs={{0,1},{1,0},{2,3},{3,2},{4,5},{5,4},{6,7},{7,6},{8,9},{9,8},{10,11... | collective-permute-start | bytes 3145736 | tf_op jit(solution)/shard_map/ppermute | solution.py:1195
  225.5 23.8 %copy-start.27 = (bf16[512,2048]{1,0:T(8,128)(2,1)S(1)}, bf16[512,2048]{1,0:T(8,128)(2,1)}, u32[]{:S(2)}) copy-start(bf16[512,2048]{1,0:T(8,128)(2,1)} %x_ref.1) | copy-start | bytes 6291460
  225.5 23.8 %copy-start.55 = (bf16[16,128,1024]{2,1,0:T(8,128)(2,1)S(1)}, bf16[16,128,1024]{2,1,0:T(8,128)(2,1)}, u32[]{:S(2)}) copy-start(bf16[16,128,1024]{2,1,0:T(8,128)(2,1)} %get-tuple-element.143) | copy-start | bytes 12582916
  225.5 23.8 %copy-start.59 = (bf16[512,1024]{1,0:T(8,128)(2,1)S(1)}, bf16[512,1024]{1,0:T(8,128)(2,1)}, u32[]{:S(2)}) copy-start(bf16[512,1024]{1,0:T(8,128)(2,1)} %get-tuple-element.207) | copy-start | bytes 3145732
  249.3 3.6 copy-start.16
  253.5 102.0 %copy-start.46 = (f32[256]{0:T(256)}, f32[256]{0:T(256)S(1)}, u32[]{:S(2)}) copy-start(f32[256]{0:T(256)S(1)} %get-tuple-element.316) | copy-start | bytes 3076
  355.5 5.0 copy-start.34
  358.0 2.7 copy-start.33
  359.3 25.9 %collective-permute-start.3 = (bf16[264,2048]{1,0:T(8,128)(2,1)S(1)}, bf16[264,2048]{1,0:T(8,128)(2,1)S(1)}, u32[]{:S(2)}, u32[]{:S(2)}) collective-permute-start(bf16[264,2048]{1,0:T(8,128)(2,1)S(1)} %pad_maximum_fusion.1), channel_id=1, source_target_pairs={{0,1},{1,0},{2,3},{3,2},{4,5},{5,4},{6,7},{7,6},{8,9},{9,8},{10,11... | collective-permute-start | bytes 3244040 | tf_op jit(solution)/shard_map/ppermute | solution.py:1200
  386.6 483.7 %reduce-scatter.2.cloned.1.call-start = ((), (), s32[]{:S(2)}) async-start(), calls=%async_computation.1 | async-start | bytes 17825792 | tf_op jit(solution)/shard_map/reduce_scatter | solution.py:1374
  477.0 199.7 %collective-permute-start.4 = (bf16[704,2048]{1,0:T(8,128)(2,1)}, bf16[704,2048]{1,0:T(8,128)(2,1)}, u32[]{:S(2)}, u32[]{:S(2)}) collective-permute-start(bf16[704,2048]{1,0:T(8,128)(2,1)} %get-tuple-element.177), channel_id=1, source_target_pairs={{0,1},{1,0},{2,3},{3,2},{4,5},{5,4},{6,7},{7,6},{8,9},{9,8},{10,11... | collective-permute-start | bytes 8650760 | tf_op jit(solution)/shard_map/ppermute | solution.py:1200
  478.2 198.5 %collective-permute-start.5 = (bf16[704,2048]{1,0:T(8,128)(2,1)}, bf16[704,2048]{1,0:T(8,128)(2,1)}, u32[]{:S(2)}, u32[]{:S(2)}) collective-permute-start(bf16[704,2048]{1,0:T(8,128)(2,1)} %get-tuple-element.178), channel_id=1, source_target_pairs={{0,1},{1,0},{2,3},{3,2},{4,5},{5,4},{6,7},{7,6},{8,9},{9,8},{10,11... | collective-permute-start | bytes 8650760 | tf_op jit(solution)/shard_map/ppermute | solution.py:1200
  479.0 197.7 %collective-permute-start.6 = (bf16[704,2048]{1,0:T(8,128)(2,1)}, bf16[704,2048]{1,0:T(8,128)(2,1)}, u32[]{:S(2)}, u32[]{:S(2)}) collective-permute-start(bf16[704,2048]{1,0:T(8,128)(2,1)} %get-tuple-element.179), channel_id=1, source_target_pairs={{0,1},{1,0},{2,3},{3,2},{4,5},{5,4},{6,7},{7,6},{8,9},{9,8},{10,11... | collective-permute-start | bytes 8650760 | tf_op jit(solution)/shard_map/ppermute | solution.py:1200
  676.7 5.2 copy-start.43
  676.7 5.1 copy-start.47
  678.9 3.0 copy-start.19
  681.9 2.3 copy-start.21
  681.9 2.9 copy-start.26
  681.9 2.8 copy-start.50
  687.0 25.5 %collective-permute-start.7 = (bf16[256,2048]{1,0:T(8,128)(2,1)}, bf16[256,2048]{1,0:T(8,128)(2,1)}, u32[]{:S(2)}, u32[]{:S(2)}) collective-permute-start(bf16[256,2048]{1,0:T(8,128)(2,1)} %get-tuple-element.291), channel_id=1, source_target_pairs={{0,1},{1,0},{2,3},{3,2},{4,5},{5,4},{6,7},{7,6},{8,9},{9,8},{10,11... | collective-permute-start | bytes 3145736 | tf_op jit(solution)/shard_map/ppermute | solution.py:1200
  712.5 5.8 copy-start.56
  716.0 5.6 copy-start.29
  763.8 21.8 %copy-start.3 = (f32[512,128]{1,0:T(8,128)S(1)}, f32[512,128]{1,0:T(8,128)}, u32[]{:S(2)}) copy-start(f32[512,128]{1,0:T(8,128)} %copy-done.2) | copy-start | bytes 786436
  763.8 21.8 %copy-start.5 = (f32[512,128]{1,0:T(8,128)S(1)}, f32[512,128]{1,0:T(8,128)}, u32[]{:S(2)}) copy-start(f32[512,128]{1,0:T(8,128)} %copy-done.4) | copy-start | bytes 786436
  763.8 21.8 %copy-start.7 = (f32[512,128]{1,0:T(8,128)S(1)}, f32[512,128]{1,0:T(8,128)}, u32[]{:S(2)}) copy-start(f32[512,128]{1,0:T(8,128)} %copy-done.6) | copy-start | bytes 786436
  763.8 21.8 %copy-start.11 = (f32[1,512]{1,0:T(1,128)S(1)}, f32[1,512]{1,0:T(1,128)}, u32[]{:S(2)}) copy-start(f32[1,512]{1,0:T(1,128)} %copy-done.10) | copy-start | bytes 6148
  763.8 21.8 %copy-start.13 = (bf16[512,1024]{1,0:T(8,128)(2,1)S(1)}, bf16[512,1024]{1,0:T(8,128)(2,1)}, u32[]{:S(2)}) copy-start(bf16[512,1024]{1,0:T(8,128)(2,1)} %get-tuple-element.187.gn_ref) | copy-start | bytes 3145732
  763.8 21.8 %copy-start.15 = (bf16[512,512]{1,0:T(8,128)(2,1)S(1)}, bf16[512,512]{1,0:T(8,128)(2,1)}, u32[]{:S(2)}) copy-start(bf16[512,512]{1,0:T(8,128)(2,1)} %get-tuple-element.188.gr_ref) | copy-start | bytes 1572868
  802.5 3.9 copy-start.30
  805.0 7.1 copy-start.57
  805.0 52.0 %collective-permute-start.8 = (bf16[256,2048]{1,0:T(8,128)(2,1)}, bf16[256,2048]{1,0:T(8,128)(2,1)S(1)}, u32[]{:S(2)}, u32[]{:S(2)}) collective-permute-start(bf16[256,2048]{1,0:T(8,128)(2,1)} %constant_dynamic-slice_fusion.3), channel_id=1, source_target_pairs={{0,1},{1,0},{2,3},{3,2},{4,5},{5,4},{6,7},{7,6},{8,9},{9,8},{10,11... | collective-permute-start | bytes 3145736 | tf_op jit(solution)/shard_map/ppermute | solution.py:1200
  847.2 9.8 copy-start.22
  847.2 9.8 copy-start.28
  847.2 9.8 copy-start.44
  958.6 3.2 copy-start.23
  958.6 3.2 copy-start.31
  962.2 2.9 copy-start.49
  965.1 9.5 collective-permute-start.9
  965.5 2.2 copy-start.24
  967.7 11.2 %copy-start.1 = (f32[512,6]{0,1:T(8,128)S(1)}, f32[512,6]{0,1:T(8,128)}, u32[]{:S(2)}) copy-start(f32[512,6]{0,1:T(8,128)} %param.25) | copy-start | bytes 36868
  970.9 7.3 copy-start.40
  (9 other events, 12.2 us)
Sparse Core Ops, SparseCore 0:
  104.9 117.2 all-gather.4
  386.8 91.2 all-gather.6
  676.8 193.4 reduce-scatter.1
